TPU v7x, 128 devices: a whole 4x4x4 slice. The times are simulated.
128 devices in a mesh: pre: 16 (over y, z), dec: 8 (over x, core).
Axes of the slice: x: 4, y: 4, z: 4, core: 2. Of those that a mesh axis runs over, the one named last changes fastest.
Arguments:
- hidden: bfloat16 [8, 6144, 7168], P('dec', None, 'pre'), may hold values from -6 to 6
- kv_down: bfloat16 [7168, 576], P('pre'), may hold values from -0.0625 to 0.0625
- kv_gain: float32 [512], replicated, may hold values from 0.1 to 1.9
- uk_weight: bfloat16 [128, 128, 512], P('pre'), may hold values from -0.5 to 0.5
- uv_weight: bfloat16 [128, 512, 128], P('pre'), may hold values from -0.25 to 0.25
- queries: bfloat16 [8, 16, 4, 128, 192], P('dec', None, None, 'pre'), may hold values from -100 to 100
- new_keys: bfloat16 [8, 16, 4, 576], P('dec'), may hold values from -6 to 6
- lengths: int32 [8, 16], replicated, may hold values from 1 to 384, 3840 in all within a row
- assign: int32 [128], replicated, may hold values from 0 to 127, each once
- block_table: int32 [8, 96], P('dec'), may hold values from 0 to 95, each once within a row
Outputs:
- cache: bfloat16 [8, 6144, 576], P('dec', 'pre')
- attended: bfloat16 [8, 16, 4, 128, 128], P('dec', None, None, 'pre')
Inputs may be any that keep to these rules, and one draw needn't show every extreme that they name: `lengths`: span d holds 16 request slots of 384 tokens; row d sums to 3840 and some request of each span fills its slot. Request r = d * 16 + j is the one in slot j of span d; decode slot b of instance e serves request assign[e * 16 + b]; every request is served once. `block_table`: each row is a permutation of the pages of one decode instance.
All inputs are finite; a program needn't handle non-finite values.
Results may differ from a plain program's by a relative error of at most 0.0082.
Values may be sent and summed in bfloat16 or wider, within the bound.
No kernel may reach another device: no remote copies, remote signals or barrier semaphores. Data moves between devices by JAX's collectives and lax.ppermute only.
A program may use at most 128 MiB of HBM per device.

v0:
```python
import math

import jax
import jax.numpy as jnp
from jax import lax
from jax.sharding import PartitionSpec as P

LAT = 512
ROPE = 64
HDIM = 128
BLK = 64


EPS = 1e-06


def rotate(values, positions):
    half_rope = ROPE // 2
    frequency = 10000.0 ** (-jnp.arange(half_rope, dtype=jnp.float32) * 2.0 / ROPE)
    angles = positions[:, None].astype(jnp.float32) * frequency[None, :]
    cosine, sine_part = (jnp.cos(angles), jnp.sin(angles))
    first_half, second_half = (values[..., :half_rope], values[..., half_rope:])
    return jnp.concatenate(
        [
            first_half * cosine - second_half * sine_part,
            second_half * cosine + first_half * sine_part,
        ],
        -1,
    )


def shards(
    hidden, kv_down, kv_gain, uk_weight, uv_weight, queries, new_keys, lengths, assign, block_table
):
    pre_count = lax.axis_size("pre")
    dec_count = lax.axis_size("dec")
    pre_rank = lax.axis_index("pre")
    dec_rank = lax.axis_index("dec")
    span_rows = hidden.shape[1]
    tok_rows = span_rows // pre_count
    row_width = kv_down.shape[1]
    local_rows = hidden[0]
    projected = lax.psum_scatter(
        jnp.dot(local_rows, kv_down, preferred_element_type=jnp.float32),
        "pre",
        scatter_dimension=0,
        tiled=True,
    )
    latent = projected[:, :LAT]
    scaling = lax.rsqrt(jnp.mean(latent * latent, -1, keepdims=True) + EPS)
    latent_part = (latent * scaling * kv_gain).astype(jnp.bfloat16)
    rope_part = rotate(projected[:, LAT:], jnp.arange(tok_rows, dtype=jnp.int32)).astype(
        jnp.bfloat16
    )
    own_block = jnp.concatenate([latent_part, rope_part], -1)
    flat_lengths = lengths.reshape(-1)
    request_ids = jnp.arange(flat_lengths.shape[0], dtype=jnp.int32)
    own_request = dec_rank * pre_count + pre_rank
    own_length = jnp.sum(jnp.where(request_ids == own_request, flat_lengths, 0))
    own_block = jnp.where(
        (jnp.arange(tok_rows, dtype=jnp.int32) < own_length)[:, None],
        own_block,
        jnp.zeros((), jnp.bfloat16),
    )
    matches = assign[None, :] == request_ids[:, None]
    slot_of = jnp.sum(jnp.where(matches, request_ids[None, :], 0), 1)
    own_slot = jnp.sum(jnp.where(request_ids == own_request, slot_of, 0))
    target_dec = own_slot // pre_count
    outgoing = jnp.where(
        (jnp.arange(dec_count) == target_dec)[:, None, None],
        own_block[None],
        jnp.zeros((), jnp.bfloat16),
    )
    incoming = lax.all_to_all(outgoing, "dec", split_axis=0, concat_axis=0, tiled=True)
    source_requests = jnp.arange(dec_count, dtype=jnp.int32) * pre_count + pre_rank
    source_slots = jnp.sum(
        jnp.where(source_requests[:, None] == request_ids[None, :], slot_of[None, :], 0), 1
    )
    is_mine = source_slots // pre_count == dec_rank
    local_slot = source_slots % pre_count
    pages_per = tok_rows // BLK
    table_row = block_table[0]
    page_count = table_row.shape[0]
    page_index = local_slot[:, None] * pages_per + jnp.arange(pages_per, dtype=jnp.int32)[None, :]
    page_dest = jnp.where(is_mine[:, None], table_row[page_index], page_count)
    page_blocks = incoming.reshape(dec_count * pages_per, BLK, row_width)
    placed = (
        jnp.zeros((page_count, BLK, row_width), jnp.bfloat16)
        .at[page_dest.reshape(-1)]
        .set(page_blocks, mode="drop")
    )
    placed = placed.reshape(page_count * BLK, row_width)
    cache_shard = (
        lax.psum_scatter(placed, "pre", scatter_dimension=0, tiled=True)
        .astype(jnp.float32)
        .astype(jnp.bfloat16)
    )
    full_cache = lax.all_gather(cache_shard, "pre", axis=0, tiled=True)
    page_table = table_row.reshape(pre_count, pages_per)
    keys = full_cache.reshape(page_count, BLK, row_width)[page_table].reshape(
        pre_count, tok_rows, row_width
    )
    slot_requests = lax.dynamic_slice_in_dim(assign, dec_rank * pre_count, pre_count)
    slot_lengths = jnp.sum(
        jnp.where(slot_requests[:, None] == request_ids[None, :], flat_lengths[None, :], 0), 1
    )
    local_queries = queries[0]
    absorbed = jnp.einsum(
        "bshk,hkl->bshl", local_queries[..., :HDIM], uk_weight, preferred_element_type=jnp.float32
    ).astype(jnp.bfloat16)
    query_full = jnp.concatenate([absorbed, local_queries[..., HDIM:]], -1)
    score_scale = 1.0 / math.sqrt(HDIM + ROPE)
    fresh = new_keys[0]
    steps_count = fresh.shape[1]
    cache_scores = (
        jnp.einsum("bshc,btc->bsht", query_full, keys, preferred_element_type=jnp.float32)
        * score_scale
    )
    fresh_scores = (
        jnp.einsum("bshc,btc->bsht", query_full, fresh, preferred_element_type=jnp.float32)
        * score_scale
    )
    cache_live = (jnp.arange(tok_rows, dtype=jnp.int32)[None, :] < slot_lengths[:, None])[
        :, None, None, :
    ]
    fresh_live = (jnp.arange(steps_count)[None, :] <= jnp.arange(steps_count)[:, None])[
        None, :, None, :
    ]
    cache_scores = jnp.where(cache_live, cache_scores, -1e30)
    fresh_scores = jnp.where(fresh_live, fresh_scores, -1e30)
    top_score = jnp.maximum(jnp.max(cache_scores, -1), jnp.max(fresh_scores, -1))[..., None]
    cache_exp = jnp.exp(cache_scores - top_score)
    fresh_exp = jnp.exp(fresh_scores - top_score)
    denominator = jnp.sum(cache_exp, -1, keepdims=True) + jnp.sum(fresh_exp, -1, keepdims=True)
    cache_prob = (cache_exp / denominator).astype(jnp.bfloat16)
    fresh_prob = (fresh_exp / denominator).astype(jnp.bfloat16)
    mixed = jnp.einsum(
        "bsht,btl->bshl", cache_prob, keys[..., :LAT], preferred_element_type=jnp.float32
    )
    mixed = mixed + jnp.einsum(
        "bsht,btl->bshl", fresh_prob, fresh[..., :LAT], preferred_element_type=jnp.float32
    )
    mixed = mixed.astype(jnp.bfloat16)
    attended = jnp.einsum(
        "bshl,hlv->bshv", mixed, uv_weight, preferred_element_type=jnp.float32
    ).astype(jnp.bfloat16)
    return (cache_shard[None], attended[None])


def solution(mesh):
    return jax.shard_map(
        shards,
        mesh=mesh,
        in_specs=(
            P("dec", None, "pre"),
            P("pre", None),
            P(),
            P("pre", None, None),
            P("pre", None, None),
            P("dec", None, None, "pre", None),
            P("dec", None, None, None),
            P(),
            P(),
            P("dec", None),
        ),
        out_specs=(P("dec", "pre", None), P("dec", None, None, "pre", None)),
        check_vma=False,
    )
```

profile of v0, /device:TPU:0, one launch (start us, length us, event | category | flops | bytes accessed | tf_op | source)
XLA Modules:
  0.0 372.7 jit_solution(15948953892797215932)
XLA Ops:
  7.2 11.7 %fusion.1 = f32[6144,576]{0,1:T(8,128)} fusion(bf16[448,576]{1,0:T(8,128)(2,1)} %param.11, bf16[1,6144,448]{1,2,0:T(8,128)(2,1)} %param.10), kind=kOutput, calls=%fused_computation.5 | convolution fusion | flops 3170893824 | bytes 20176896 | tf_op jit(solution)/shard_map/dot_general | solution.py:44
  19.0 0.6 copy-done.9
  19.7 0.6 fusion.30
  23.0 0.6 select_reduce_fusion.2
  23.6 0.6 iota_compare_fusion.5
  24.3 97.3 %reduce-scatter.3.cloned.1.call-done = f32[384,576]{0,1:T(8,128)} async-done(((f32[6144,576]{0,1:T(8,128)}), f32[384,576]{0,1:T(8,128)}) %reduce-scatter.3.cloned.1.call-update) | async-done | bytes 884752 | tf_op jit(solution)/shard_map/reduce_scatter | solution.py:43
  121.5 1.2 multiply_reduce_fusion
  122.8 1.3 multiply_convert_fusion
  124.1 1.1 fusion.26
  125.3 2.2 broadcast_select_fusion
  127.5 4.5 %all-to-all-start = ((bf16[8,384,576]{1,2,0:T(8,128)(2,1)}), bf16[8,384,576]{1,2,0:T(8,128)(2,1)}, u32[]{:S(2)}, u32[]{:S(2)}) async-start(bf16[8,384,576]{1,2,0:T(8,128)(2,1)} %broadcast_select_fusion), calls=%async_computation.1 | async-start | bytes 7077888 | tf_op jit(solution)/shard_map/all_to_all | solution.py:74
  132.1 0.2 select_reduce_fusion.3
  132.4 0.8 gather_fusion
  133.5 41.2 %all-to-all-done = bf16[8,384,576]{1,2,0:T(8,128)(2,1)} async-done(((bf16[8,384,576]{1,2,0:T(8,128)(2,1)}), bf16[8,384,576]{1,2,0:T(8,128)(2,1)}, u32[]{:S(2)}, u32[]{:S(2)}) %all-to-all-start) | async-done | bytes 3538976 | tf_op jit(solution)/shard_map/all_to_all | solution.py:74
  174.6 6.0 %copy.31 = bf16[8,384,576]{2,1,0:T(8,128)(2,1)} copy(bf16[8,384,576]{1,2,0:T(8,128)(2,1)} %all-to-all-done) | data formatting | bytes 7077888 | tf_op jit(solution)/shard_map/all_to_all | solution.py:74
  180.7 4.2 %broadcast_in_dim.150 = bf16[96,64,576]{2,1,0:T(8,128)(2,1)} broadcast(bf16[]{:T(256)} %constant.32.clone.1), dimensions={} | broadcast | bytes 7077890 | tf_op jit(solution)/shard_map/broadcast_in_dim | solution.py:88
  184.9 9.8 %scatter_fusion = bf16[96,64,576]{2,1,0:T(8,128)(2,1)} fusion(bf16[96,64,576]{2,1,0:T(8,128)(2,1)} %broadcast_in_dim.150, s32[48]{0:T(128)S(1)} %fusion.31, bf16[48,64,576]{2,1,0:T(8,128)(2,1)} %bitcast.62), kind=kCustom, calls=%fused_computation.2 | custom fusion | bytes 10617024 | tf_op jit(solution)/shard_map/scatter | solution.py:90
  194.8 0.2 all-gather.2.cloned.1.call-start
  195.0 81.3 %reduce-scatter.5.cloned.1.call-done = bf16[384,576]{1,0:T(8,128)(2,1)} async-done(((bf16[6144,576]{1,0:T(8,128)(2,1)}), bf16[384,576]{1,0:T(8,128)(2,1)}) %reduce-scatter.5.cloned.1.call-update) | async-done | bytes 442384 | tf_op jit(solution)/shard_map/reduce_scatter | solution.py:94
  276.4 0.5 broadcast.252
  276.9 0.7 reduce.4
  278.3 0.3 fusion.5
  278.7 1.9 fusion.34
  280.6 1.0 copy.37
  281.6 64.8 %all-gather.2.cloned.1.call-done = bf16[6144,576]{1,0:T(8,128)(2,1)} async-done(((bf16[384,576]{1,0:T(8,128)(2,1)}), bf16[6144,576]{1,0:T(8,128)(2,1)}) %all-gather.2.cloned.1.call-update) | async-done | bytes 7077904 | tf_op jit(solution)/shard_map/all_gather | solution.py:98
  346.4 10.3 %gather_fusion.1 = bf16[96,64,576]{2,1,0:T(8,128)(2,1)} fusion(bf16[96,64,576]{2,1,0:T(8,128)(2,1)} %bitcast.63, s32[1024]{0:T(1024)S(1)} %pad_clamp_fusion), kind=kCustom, calls=%fused_computation.1 | custom fusion | bytes 14156160 | tf_op jit(solution)/shard_map/gather | solution.py:100
  356.7 5.9 %fusion.33 = (f32[16,4,8]{2,1,0:T(4,128)S(1)}, f32[16,4,8,384]{3,2,1,0:T(8,128)S(1)}) fusion(bf16[16,384,576,1]{2,1,3,0:T(8,128)(2,1)} %bitcast.60, bf16[16,4,8,576]{3,0,1,2:T(8,128)(2,1)S(1)} %pad_maximum_fusion, pred[16,384]{1,0:T(8,128)(4,1)S(1)} %iota_compare_fusion.1), kind=kOutput, calls=%fused_computation.83 | convolution fusion | flops 227081728 | bytes 8462336 | tf_op jit(solution)/shard_map/bshc,btc->bsht/dot_general | solution.py:116
  362.7 0.3 fusion.10
  363.1 1.2 fusion
  364.3 0.4 fusion.3
  364.7 0.7 fusion.7
  365.4 0.8 copy.38
  (55 shorter events, 1.8 us)
Async XLA Ops:
  7.2 271.1 %copy-start = (bf16[8,128,512]{2,1,0:T(8,128)(2,1)S(1)}, bf16[8,128,512]{2,1,0:T(8,128)(2,1)}, u32[]{:S(2)}) copy-start(bf16[8,128,512]{2,1,0:T(8,128)(2,1)} %param.13) | copy-start | bytes 3145732
  7.2 114.3 %reduce-scatter.3.cloned.1.call-start = ((), (), s32[]{:S(2)}) async-start(), calls=%async_computation.3 | async-start | bytes 15040512 | tf_op jit(solution)/shard_map/reduce_scatter | solution.py:43
  18.9 0.7 copy-start.9
  18.9 4.0 %copy-start.7 = (s32[8,16]{1,0:T(8,128)S(1)}, s32[8,16]{1,0:T(8,128)}, u32[]{:S(2)}) copy-start(s32[8,16]{1,0:T(8,128)} %param.17) | copy-start | bytes 1540
  18.9 103.8 %copy-start.8 = (f32[512]{0:T(512)S(1)}, f32[512]{0:T(512)}, u32[]{:S(2)}) copy-start(f32[512]{0:T(512)} %param.12) | copy-start | bytes 6148
  124.1 8.4 %copy-start.1 = (s32[1,96]{1,0:T(1,128)S(1)}, s32[1,96]{1,0:T(1,128)}, u32[]{:S(2)}) copy-start(s32[1,96]{1,0:T(1,128)} %param.19) | copy-start | bytes 1156
  127.5 47.1 %all-to-all-start = ((bf16[8,384,576]{1,2,0:T(8,128)(2,1)}), bf16[8,384,576]{1,2,0:T(8,128)(2,1)}, u32[]{:S(2)}, u32[]{:S(2)}) async-start(bf16[8,384,576]{1,2,0:T(8,128)(2,1)} %broadcast_select_fusion), calls=%async_computation.1 | async-start | bytes 7077888 | tf_op jit(solution)/shard_map/all_to_all | solution.py:74
  132.0 144.3 %reduce-scatter.5.cloned.1.call-start = ((), (), s32[]{:S(2)}) async-start(), calls=%async_computation.4 | async-start | bytes 8355840 | tf_op jit(solution)/shard_map/reduce_scatter | solution.py:94
  194.7 83.1 %copy-start.5 = (bf16[1,16,4,8,192]{4,3,2,1,0:T(8,128)(2,1)S(1)}, bf16[1,16,4,8,192]{4,3,2,1,0:T(8,128)(2,1)}, u32[]{:S(2)}) copy-start(bf16[1,16,4,8,192]{4,3,2,1,0:T(8,128)(2,1)} %param.15) | copy-start | bytes 589828
  194.7 84.0 %copy-start.6 = (bf16[1,16,4,576]{3,2,1,0:T(4,128)(2,1)S(1)}, bf16[1,16,4,576]{3,2,1,0:T(4,128)(2,1)}, u32[]{:S(2)}) copy-start(bf16[1,16,4,576]{3,2,1,0:T(4,128)(2,1)} %param.16) | copy-start | bytes 221188
  194.8 151.6 %all-gather.2.cloned.1.call-start = ((), (), s32[]{:S(2)}) async-start(), calls=%async_computation.5 | async-start | bytes 8355840 | tf_op jit(solution)/shard_map/all_gather | solution.py:98
  276.3 4.3 %copy-start.3 = (bf16[384,576]{1,0:T(8,128)(2,1)S(1)}, bf16[384,576]{1,0:T(8,128)(2,1)}, u32[]{:S(2)}) copy-start(bf16[384,576]{1,0:T(8,128)(2,1)} %reduce-scatter.5.cloned.1.call-done) | copy-start | bytes 1327108
  356.7 6.5 %copy-start.2 = (bf16[96,64,576]{2,1,0:T(8,128)(2,1)S(1)}, bf16[96,64,576]{2,1,0:T(8,128)(2,1)}, u32[]{:S(2)}) copy-start(bf16[96,64,576]{2,1,0:T(8,128)(2,1)} %gather_fusion.1) | copy-start | bytes 21233668
  362.7 1.9 copy-start.4
Sparse Core Ops, SparseCore 0:
  19.1 102.4 reduce-scatter.2
  194.9 81.3 reduce-scatter.4
  278.5 67.8 all-gather.1
where the time goes:
time: 374 us; the launch traced here: 373 us
  waiting for transfers between devices  285 us (76%)
  local copies, waits for them, and re-layouts  34.8 us (9%)
  matrix products  22 us (6%)
  between operations  16.6 us (4%)
  other arithmetic  9.86 us (3%)
  starting transfers between devices  4.79 us (1%)
    reduce_scatter x1, waiting for transfers between devices, shards(): lax.psum_scatter(jnp.dot(local_rows, kv_down, preferred_element_type=jnp....  97.3 us
    reduce_scatter x1, waiting for transfers between devices, shards(): lax.psum_scatter(placed, 'pre', scatter_dimension=0, tiled=True)  81.3 us
    all_gather x1, waiting for transfers between devices, shards(): full_cache = lax.all_gather(cache_shard, 'pre', axis=0, tiled=True)  64.8 us
    all_to_all x1, waiting for transfers between devices, shards(): lax.all_to_all(outgoing, 'dec', split_axis=0, concat_axis=0, tiled=True)  41.2 us
    dot_general x1, matrix products, shards(): jnp.dot(local_rows, kv_down, preferred_element_type=jnp.float32)  11.7 us
    gather x1, local copies, waits for them, and re-layouts, shards(): full_cache.reshape(page_count, BLK, row_width)[page_table]  10.3 us
    scatter x1, local copies, waits for them, and re-layouts, shards(): placed = jnp.zeros((page_count, BLK, row_width), jnp.bfloat16).at[page_de...  9.84 us
  transfers between devices with their start and end apart: 4, of which 4 were waited for; matrix products, arithmetic and copies ran while one was open for 2% of the time, Pallas kernels for 0%

commit v1 on v0

v1 whole, which is shorter than its diff:
```python
import functools
import math

import jax
import jax.numpy as jnp
from jax import lax
from jax.experimental import pallas as pl
from jax.experimental.pallas import tpu as pltpu
from jax.sharding import PartitionSpec as P

LAT = 512
ROPE = 64
WIDTH = LAT + ROPE
HDIM = 128
BLK = 64
TOK = 384
REQS = 16
RUN = TOK // REQS
NPG = TOK // BLK
PACK = 256
HOLD = 288
WINDOW = 32
SIDE = 4
STEPS = 4

EPS = 1e-06
BF = jnp.bfloat16
F32 = jnp.float32


def project_kernel(len_ref, hid_ref, down_ref, out_ref, shift_ref, hold_ref, start_ref):
    step = pl.program_id(0)

    @pl.when(step == 0)
    def _():
        start_ref[0] = 0
        hold_ref[...] = jnp.zeros_like(hold_ref)
        shape = (REQS, WINDOW, TOK)
        offset = lax.broadcasted_iota(jnp.int32, shape, 2)
        offset = offset - lax.broadcasted_iota(jnp.int32, shape, 0)
        shift_ref[...] = offset - REQS * lax.broadcasted_iota(jnp.int32, shape, 1)

    start = start_ref[0]
    count = lax.div(len_ref[step] + (REQS - 1), REQS)
    lead = lax.rem(start, 8)
    base = pl.multiple_of(start - lead, 8)

    for tile in range(1, TOK // 128 + 1):
        tokens, window = 128 * tile, 8 * tile + 8

        @pl.when((count > 8 * tile - 8) & (count <= 8 * tile))
        def _():
            hid = hid_ref[:, :tokens]
            token = lax.broadcasted_iota(jnp.int32, hid.shape, 1)
            hid = jnp.where(token < count * REQS, hid, jnp.zeros((), BF))
            chosen = jnp.where(shift_ref[:, :window, :tokens] == -REQS * lead, 1.0, 0.0)
            chosen = chosen.reshape(REQS * window, tokens).astype(BF)
            rows = lax.dot_general(
                chosen, hid, (((1,), (1,)), ((), ())), preferred_element_type=F32
            ).astype(BF)
            part = jnp.dot(rows, down_ref[...], preferred_element_type=F32)
            hold_ref[:, pl.ds(base, window), :] += part.reshape(REQS, window, WIDTH)

    start_ref[0] = start + count

    @pl.when(step == pl.num_programs(0) - 1)
    def _():
        out_ref[...] = hold_ref[:, :PACK, :].astype(BF)


def project(lengths_row, hidden_t, kv_down):
    depth = hidden_t.shape[0]
    return pl.pallas_call(
        project_kernel,
        out_shape=jax.ShapeDtypeStruct((REQS, PACK, WIDTH), BF),
        grid_spec=pltpu.PrefetchScalarGridSpec(
            num_scalar_prefetch=1,
            grid=(REQS,),
            in_specs=[
                pl.BlockSpec((depth, TOK), lambda r, _: (0, r)),
                pl.BlockSpec((depth, WIDTH), lambda r, _: (0, 0)),
            ],
            out_specs=pl.BlockSpec((REQS, PACK, WIDTH), lambda r, _: (0, 0, 0)),
            scratch_shapes=[
                pltpu.VMEM((REQS, WINDOW, TOK), jnp.int32),
                pltpu.VMEM((REQS, HOLD, WIDTH), F32),
                pltpu.SMEM((1,), jnp.int32),
            ],
        ),
        compiler_params=pltpu.CompilerParams(vmem_limit_bytes=48 << 20),
        cost_estimate=pl.CostEstimate(
            flops=2 * REQS * TOK * depth * WIDTH, bytes_accessed=11 << 20, transcendentals=0
        ),
    )(lengths_row, hidden_t, kv_down)


def attend_kernel(query_ref, keys_ref, fresh_ref, live_ref, out_ref):
    rows = query_ref.shape[0]
    query = query_ref[...]
    keys = keys_ref[...]
    fresh = fresh_ref[...]
    scale = 1.0 / math.sqrt(HDIM + ROPE)
    across = (((1,), (1,)), ((), ()))
    score = lax.dot_general(query, keys, across, preferred_element_type=F32) * scale
    score = jnp.where(live_ref[...] > 0, score, -1e30)
    later = lax.dot_general(query, fresh, across, preferred_element_type=F32) * scale
    row = lax.broadcasted_iota(jnp.int32, later.shape, 0)
    column = lax.broadcasted_iota(jnp.int32, later.shape, 1)
    at_step = lax.rem(lax.div(row, 8), STEPS)
    later = jnp.where(column <= at_step, later, -1e30)
    top = jnp.maximum(jnp.max(score, -1, keepdims=True), jnp.max(later, -1, keepdims=True))
    score = jnp.exp(score - top)
    later = jnp.exp(later - top)
    total = jnp.sum(score, -1, keepdims=True) + jnp.sum(later, -1, keepdims=True)
    score = (score / total).astype(BF)
    later = (later / total).astype(BF)
    mixed = jnp.dot(score, keys[:, :LAT], preferred_element_type=F32)
    mixed = mixed + jnp.dot(later, fresh[:, :LAT], preferred_element_type=F32)
    out_ref[...] = mixed.astype(BF)


def attend(query, keys, fresh, live):
    count, block = query.shape[0], 128
    return pl.pallas_call(
        attend_kernel,
        out_shape=jax.ShapeDtypeStruct((count, LAT), BF),
        grid=(count // block,),
        in_specs=[
            pl.BlockSpec((block, WIDTH), lambda i: (i, 0)),
            pl.BlockSpec(keys.shape, lambda i: (0, 0)),
            pl.BlockSpec(fresh.shape, lambda i: (0, 0)),
            pl.BlockSpec(live.shape, lambda i: (0, 0)),
        ],
        out_specs=pl.BlockSpec((block, LAT), lambda i: (i, 0)),
        compiler_params=pltpu.CompilerParams(vmem_limit_bytes=24 << 20),
    )(query, keys, fresh, live)


def pick(index, values):
    ids = jnp.arange(values.shape[0], dtype=jnp.int32)
    return jnp.sum(jnp.where(index[..., None] == ids, values, 0), -1)


def groups_of(sides, first):
    found = []
    for core in range(2):
        for x in range(SIDE):
            for other in range(SIDE):
                ring = []
                for k in range(SIDE):
                    y, z = (k, other) if core == first else (other, k)
                    ring.append(((y * SIDE + z) * SIDE + x) * 2 + core)
                found.append(ring)
    return found


def shards(
    hidden, kv_down, kv_gain, uk_weight, uv_weight, queries, new_keys, lengths, assign, block_table
):
    pre_rank = lax.axis_index("pre")
    dec_rank = lax.axis_index("dec")
    both = ("pre", "dec")
    side_y, side_z = pre_rank // SIDE, pre_rank % SIDE
    swapped = side_z * SIDE + side_y
    residue = jnp.where(dec_rank % 2 == 0, pre_rank, swapped)

    counts = (lengths + (REQS - 1)) // REQS
    ends = jnp.cumsum(counts, 1)
    starts = ends - counts
    own_lengths = lax.dynamic_index_in_dim(lengths, dec_rank, 0, keepdims=False)
    own_starts = lax.dynamic_index_in_dim(starts, dec_rank, 0, keepdims=False)
    own_ends = lax.dynamic_index_in_dim(ends, dec_rank, 0, keepdims=False)

    packed = project(own_lengths, hidden[0].T, kv_down)

    packed = packed.reshape(SIDE, SIDE, PACK, WIDTH)
    packed = lax.all_to_all(packed, both, 0, 0, tiled=True, axis_index_groups=groups_of(SIDE, 0))
    packed = jnp.sum(packed.astype(F32), 0).astype(BF)
    packed = lax.all_to_all(packed, both, 0, 0, tiled=True, axis_index_groups=groups_of(SIDE, 1))
    projected = jnp.sum(packed.astype(F32), 0)

    row = jnp.arange(PACK, dtype=jnp.int32)
    inside = (row[:, None] >= own_starts) & (row[:, None] < own_ends)
    place = jnp.sum(jnp.where(inside, row[:, None] - own_starts, 0), 1)
    limit = jnp.sum(jnp.where(inside, own_lengths, 0), 1)
    position = place * REQS + residue
    valid = (position < limit)[:, None]
    half = ROPE // 2
    frequency = 10000.0 ** (-jnp.arange(half, dtype=F32) * 2.0 / ROPE)
    angles = position[:, None].astype(F32) * frequency[None, :]
    cosine, sine = jnp.cos(angles), jnp.sin(angles)
    projected = jnp.where(valid, projected, 0.0)
    latent = projected[:, :LAT]
    scaling = lax.rsqrt(jnp.mean(latent * latent, -1, keepdims=True) + EPS)
    first, second = projected[:, LAT : LAT + half], projected[:, LAT + half :]
    rows = jnp.concatenate(
        [
            latent * scaling * kv_gain,
            first * cosine - second * sine,
            second * cosine + first * sine,
        ],
        -1,
    ).astype(BF)

    local_queries = queries[0]
    absorbed = jnp.einsum(
        "bshk,hkl->bshl", local_queries[..., :HDIM], uk_weight, preferred_element_type=F32
    ).astype(BF)
    query_full = jnp.concatenate([absorbed, local_queries[..., HDIM:]], -1)
    query_full = query_full.reshape(REQS, -1, WIDTH)
    rows, query_full = lax.optimization_barrier((rows, query_full))
    everything = lax.all_gather(rows, "dec", axis=0, tiled=True)
    query_full = lax.all_to_all(query_full, "pre", 0, 0, tiled=True)

    slots = lax.dynamic_slice_in_dim(assign, dec_rank * REQS, REQS)
    slot_start = pick(slots, (starts + jnp.arange(starts.shape[0])[:, None] * PACK).reshape(-1))
    slot_count = pick(slots, counts.reshape(-1))
    slot_length = pick(slots, lengths.reshape(-1))
    slot_odd = (slots // REQS) % 2
    run = jnp.arange(RUN, dtype=jnp.int32)
    by_slot = jnp.where(run < slot_count[:, None], slot_start[:, None] + run, -1)
    table = block_table[0]
    pages = table.shape[0]
    page = jnp.arange(pages, dtype=jnp.int32)
    block = jnp.sum(jnp.where(table[None, :] == page[:, None], page[None, :], 0), 1)
    owner, part = block // NPG, block % NPG
    piece = part[:, None] * (RUN // NPG) + jnp.arange(RUN // NPG, dtype=jnp.int32)
    by_page = jnp.where(
        piece < pick(owner, slot_count)[:, None], pick(owner, slot_start)[:, None] + piece, -1
    )
    source = jnp.concatenate([by_slot, by_page.reshape(REQS, RUN)], 1).reshape(-1)
    selector = (source[:, None] == jnp.arange(everything.shape[0], dtype=jnp.int32)).astype(BF)
    outgoing = jnp.dot(selector, everything, preferred_element_type=F32).astype(BF)
    outgoing = outgoing.reshape(REQS, 2 * RUN, WIDTH)
    arrived = lax.all_to_all(outgoing, "pre", 0, 0, tiled=True)

    sender = jnp.arange(REQS, dtype=jnp.int32)
    sender_swapped = (sender % SIDE) * SIDE + sender // SIDE
    page_odd = pick(owner, slot_odd).reshape(REQS, NPG)
    page_odd = lax.dynamic_index_in_dim(page_odd, pre_rank, 0, keepdims=False)
    sent_residue = jnp.where(page_odd[None, :] == 0, sender[:, None], sender_swapped[:, None])
    target = (
        jnp.arange(NPG, dtype=jnp.int32)[None, :, None] * BLK
        + jnp.arange(RUN // NPG, dtype=jnp.int32)[None, None, :] * REQS
        + sent_residue[:, :, None]
    ).reshape(-1)
    to_place = (jnp.arange(TOK, dtype=jnp.int32)[:, None] == target[None, :]).astype(BF)
    cache = jnp.dot(
        to_place, arrived[:, RUN:].reshape(TOK, WIDTH), preferred_element_type=F32
    ).astype(BF)

    own_odd = lax.dynamic_index_in_dim(slot_odd, pre_rank, 0, keepdims=False)
    own_length = lax.dynamic_index_in_dim(slot_length, pre_rank, 0, keepdims=False)
    key_residue = jnp.where(own_odd == 0, sender, sender_swapped)
    key_position = run[None, :] * REQS + key_residue[:, None]
    live = (key_position < own_length).astype(jnp.int32).reshape(1, TOK)
    fresh = lax.dynamic_index_in_dim(new_keys[0], pre_rank, 0, keepdims=False)
    fresh = jnp.pad(fresh, ((0, 16 - STEPS), (0, 0)))
    mixed = attend(
        query_full.reshape(-1, WIDTH), arrived[:, :RUN].reshape(TOK, WIDTH), fresh, live
    )
    mixed = lax.all_to_all(mixed.reshape(REQS, -1, LAT), "pre", 0, 0, tiled=True)
    mixed = mixed.reshape(REQS, STEPS, -1, LAT)
    attended = jnp.einsum("bshl,hlv->bshv", mixed, uv_weight, preferred_element_type=F32).astype(BF)
    return (cache[None], attended[None])


def solution(mesh):
    return jax.shard_map(
        shards,
        mesh=mesh,
        in_specs=(
            P("dec", None, "pre"),
            P("pre", None),
            P(),
            P("pre", None, None),
            P("pre", None, None),
            P("dec", None, None, "pre", None),
            P("dec", None, None, None),
            P(),
            P(),
            P("dec", None),
        ),
        out_specs=(P("dec", "pre", None), P("dec", None, None, "pre", None)),
        check_vma=False,
    )
```

time: 374 us -> 193 us (0.52)
  waiting for transfers between devices: 285 us -> 96.5 us
  Pallas kernels: 0 us -> 20.2 us
  starting transfers between devices: 4.79 us -> 24.6 us
  local copies, waits for them, and re-layouts: 34.8 us -> 19.4 us
  matrix products: 22 us -> 8.43 us
    reduce_scatter x2 -> x0, waiting for transfers between devices: 179 us -> none  [the longest x1 97.3 us: shards(): lax.psum_scatter(jnp.dot(local_rows, kv_down, preferred_element_type=jnp....]
    all_gather x1, waiting for transfers between devices: 64.8 us -> 24.1 us  [shards(): everything = lax.all_gather(rows, 'dec', axis=0, tiled=True)]
    all_to_all x1 -> x5, waiting for transfers between devices: 41.2 us -> 72.3 us  [the longest x2 40 us: shards(): lax.all_to_all(packed, both, 0, 0, tiled=True, axis_index_groups=groups_o...]
    pallas_call x0 -> x2, Pallas kernels: none -> 20.2 us  [the longest x1 16.6 us: project(): pl.pallas_call(project_kernel, out_shape=jax.ShapeDtypeStruct((REQS, PACK...]
    all_to_all x1 -> x5, starting transfers between devices: 4.49 us -> 24.6 us  [the longest x2 10.5 us: shards(): lax.all_to_all(packed, both, 0, 0, tiled=True, axis_index_groups=groups_o...]
    dot_general x6 -> x3, matrix products: 21.7 us -> 8.14 us  [the longest x1 3.89 us: shards(): jnp.dot(selector, everything, preferred_element_type=F32).astype(BF)]
    gather x3 -> x0, local copies, waits for them, and re-layouts: 11.1 us -> none  [the longest x1 10.3 us: shards(): full_cache.reshape(page_count, BLK, row_width)[page_table]]
    scatter x1 -> x0, local copies, waits for them, and re-layouts: 9.84 us -> none  [shards(): placed = jnp.zeros((page_count, BLK, row_width), jnp.bfloat16).at[page_de...]
  transfers between devices with their start and end apart: 4 -> 6, of which waited for: 4 -> 6; matrix products, arithmetic and copies ran while one was open for 2% -> 5% of each run, Pallas kernels for 0% -> 0%
where the time goes in v1:
time: 193 us; the launch traced here: 192 us
  waiting for transfers between devices  96.5 us (50%)
  starting transfers between devices  24.6 us (13%)
  Pallas kernels  20.2 us (10%)
  local copies, waits for them, and re-layouts  19.4 us (10%)
  between operations  15 us (8%)
  matrix products  8.43 us (4%)
  other arithmetic  7.9 us (4%)
    all_to_all x2, waiting for transfers between devices, shards(): lax.all_to_all(packed, both, 0, 0, tiled=True, axis_index_groups=groups_o...  40 us
    all_gather x1, waiting for transfers between devices, shards(): everything = lax.all_gather(rows, 'dec', axis=0, tiled=True)  24.1 us
    pallas_call x1, Pallas kernels, project(): pl.pallas_call(project_kernel, out_shape=jax.ShapeDtypeStruct((REQS, PACK...  16.6 us
    all_to_all x1, waiting for transfers between devices, shards(): arrived = lax.all_to_all(outgoing, 'pre', 0, 0, tiled=True)  13.9 us
    all_to_all x1, waiting for transfers between devices, shards(): query_full = lax.all_to_all(query_full, 'pre', 0, 0, tiled=True)  10.9 us
    all_to_all x2, starting transfers between devices, shards(): lax.all_to_all(packed, both, 0, 0, tiled=True, axis_index_groups=groups_o...  10.5 us
    reshape x1, local copies, waits for them, and re-layouts, shards(): packed = packed.reshape(SIDE, SIDE, PACK, WIDTH)  7.67 us
    all_to_all x1, waiting for transfers between devices, shards(): lax.all_to_all(mixed.reshape(REQS, -1, LAT), 'pre', 0, 0, tiled=True)  7.49 us
  transfers between devices with their start and end apart: 6, of which 6 were waited for; matrix products, arithmetic and copies ran while one was open for 5% of the time, Pallas kernels for 0%

profile of v1, /device:TPU:0, one launch (start us, length us, event | category | flops | bytes accessed | tf_op | source)
XLA Modules:
  0.0 192.0 jit_solution(10521417545786077972)
XLA Ops:
  7.2 0.8 fusion.30.len_ref
  8.0 1.1 copy-done.2
  9.0 16.6 %shard_map.113 = bf16[16,256,576]{2,1,0:T(8,128)(2,1)S(1)} custom-call(s32[16]{0:T(128)S(1)} %fusion.30.len_ref, bf16[448,6144]{1,0:T(8,128)(2,1)} %bitcast.62, bf16[448,576]{1,0:T(8,128)(2,1)S(1)} %copy-done.2), custom_call_target="tpu_custom_call" | custom-call | flops 3170893824 | bytes 11534336 | tf_op jit(solution)/shard_map/pallas_call | solution.py:73
  25.7 2.3 %copy-done.1 = bf16[16,256,576]{2,1,0:T(8,128)(2,1)} copy-done((bf16[16,256,576]{2,1,0:T(8,128)(2,1)}, bf16[16,256,576]{2,1,0:T(8,128)(2,1)S(1)}, u32[]{:S(2)}) %copy-start.1) | copy-done | bytes 4718616
  28.0 7.7 %copy.73 = bf16[4,4,256,576]{2,3,1,0:T(8,128)(2,1)} copy(bf16[4,4,256,576]{3,2,1,0:T(8,128)(2,1)} %bitcast.52) | data formatting | bytes 9437184 | tf_op jit(solution)/shard_map/reshape | solution.py:176
  35.6 5.1 %all-to-all-start = ((bf16[4,4,256,576]{2,3,1,0:T(8,128)(2,1)}), bf16[4,4,256,576]{2,3,1,0:T(8,128)(2,1)}, u32[]{:S(2)}, u32[]{:S(2)}) async-start(bf16[4,4,256,576]{2,3,1,0:T(8,128)(2,1)} %copy.73), calls=%async_computation | async-start | bytes 9437184 | tf_op jit(solution)/shard_map/all_to_all | solution.py:177
  41.2 0.3 fusion.3
  41.5 1.2 copy.85
  42.8 28.6 %all-to-all-done = bf16[4,4,256,576]{2,3,1,0:T(8,128)(2,1)} async-done(((bf16[4,4,256,576]{2,3,1,0:T(8,128)(2,1)}), bf16[4,4,256,576]{2,3,1,0:T(8,128)(2,1)}, u32[]{:S(2)}, u32[]{:S(2)}) %all-to-all-start) | async-done | bytes 4718624 | tf_op jit(solution)/shard_map/all_to_all | solution.py:177
  71.4 4.4 %reduce_sum.119 = bf16[4,256,576]{1,2,0:T(8,128)(2,1)} reduce(bf16[4,4,256,576]{2,3,1,0:T(8,128)(2,1)} %all-to-all-done, bf16[]{:T(256)} %constant.161.clone.1), dimensions={0}, to_apply=%region_9.10 | reduce | flops 1769472 | bytes 5898242 | tf_op jit(solution)/shard_map/reduce_sum | solution.py:178
  75.8 5.4 %all-to-all-start.1 = ((bf16[4,256,576]{1,2,0:T(8,128)(2,1)}), bf16[4,256,576]{1,2,0:T(8,128)(2,1)S(1)}, u32[]{:S(2)}, u32[]{:S(2)}) async-start(bf16[4,256,576]{1,2,0:T(8,128)(2,1)} %reduce_sum.119), calls=%async_computation.1 | async-start | bytes 2359296 | tf_op jit(solution)/shard_map/all_to_all | solution.py:179
  81.4 11.4 %all-to-all-done.1 = bf16[4,256,576]{1,2,0:T(8,128)(2,1)S(1)} async-done(((bf16[4,256,576]{1,2,0:T(8,128)(2,1)}), bf16[4,256,576]{1,2,0:T(8,128)(2,1)S(1)}, u32[]{:S(2)}, u32[]{:S(2)}) %all-to-all-start.1) | async-done | bytes 1179680 | tf_op jit(solution)/shard_map/all_to_all | solution.py:179
  93.5 0.7 pad_maximum_fusion.1
  94.7 0.2 select_reduce_fusion.3
  96.0 24.1 %all-gather.2.cloned.1.call-done = bf16[2048,576]{0,1:T(8,128)(2,1)} async-done(((bf16[256,576]{0,1:T(8,128)(2,1)}), bf16[2048,576]{0,1:T(8,128)(2,1)}) %all-gather.2.cloned.1.call-update) | async-done | bytes 2359312 | tf_op jit(solution)/shard_map/all_gather | solution.py:212
  120.2 3.9 %fusion.2 = bf16[768,576]{0,1:T(8,128)(2,1)S(1)} fusion(bf16[2048,576]{0,1:T(8,128)(2,1)} %all-gather.2.cloned.1.call-done, s32[768]{0:T(1024)S(1)} %eq.65), kind=kOutput, calls=%fused_computation.4 | convolution fusion | flops 1813954560 | bytes 3247104 | tf_op jit(solution)/shard_map/dot_general | solution.py:233
  124.1 1.3 copy.76
  125.4 7.0 %all-to-all-start.2 = ((bf16[16,48,576]{2,1,0:T(8,128)(2,1)}), bf16[16,48,576]{2,1,0:T(8,128)(2,1)S(1)}, u32[]{:S(2)}, u32[]{:S(2)}) async-start(bf16[16,48,576]{2,1,0:T(8,128)(2,1)} %bitcast.16), calls=%async_computation.2 | async-start | bytes 1966080 | tf_op jit(solution)/shard_map/all_to_all | solution.py:235
  132.5 0.6 dynamic_slice.34
  133.1 0.7 dynamic-slice_bitcast_fusion
  133.8 0.6 dynamic_slice.35
  135.1 0.7 fusion.20
  135.9 13.9 %all-to-all-done.2 = bf16[16,48,576]{2,1,0:T(8,128)(2,1)S(1)} async-done(((bf16[16,48,576]{2,1,0:T(8,128)(2,1)}), bf16[16,48,576]{2,1,0:T(8,128)(2,1)S(1)}, u32[]{:S(2)}, u32[]{:S(2)}) %all-to-all-start.2) | async-done | bytes 884768 | tf_op jit(solution)/shard_map/all_to_all | solution.py:235
  149.8 3.6 %all-to-all-start.3 = ((bf16[16,32,576]{2,1,0:T(8,128)(2,1)}), bf16[16,32,576]{2,1,0:T(8,128)(2,1)S(1)}, u32[]{:S(2)}, u32[]{:S(2)}) async-start(bf16[16,32,576]{2,1,0:T(8,128)(2,1)} %bitcast.50), calls=%async_computation.3 | async-start | bytes 1310720 | tf_op jit(solution)/shard_map/all_to_all | solution.py:213
  153.5 0.9 fusion.34
  154.4 10.9 %all-to-all-done.3 = bf16[16,32,576]{2,1,0:T(8,128)(2,1)S(1)} async-done(((bf16[16,32,576]{2,1,0:T(8,128)(2,1)}), bf16[16,32,576]{2,1,0:T(8,128)(2,1)S(1)}, u32[]{:S(2)}, u32[]{:S(2)}) %all-to-all-start.3) | async-done | bytes 589856 | tf_op jit(solution)/shard_map/all_to_all | solution.py:213
  165.3 3.6 %shard_map.114 = bf16[512,512]{1,0:T(8,128)(2,1)} custom-call(bf16[512,576]{1,0:T(8,128)(2,1)S(1)} %bitcast.53, bf16[384,576]{1,0:T(8,128)(2,1)S(1)} %bitcast.54, bf16[16,576]{1,0:T(8,128)(2,1)S(1)} %pad.4.fresh_ref, s32[1,384]{1,0:T(1,128)S(1)} %reshape.280.live_ref), custom_call_target="tpu_custom_call" | custom-call | tf_op jit(solution)/shard_map/pallas_call | solution.py:124
  168.9 3.6 %all-to-all-start.4 = ((bf16[16,32,512]{2,1,0:T(8,128)(2,1)}), bf16[16,32,512]{2,1,0:T(8,128)(2,1)S(1)}, u32[]{:S(2)}, u32[]{:S(2)}) async-start(bf16[16,32,512]{2,1,0:T(8,128)(2,1)} %bitcast.24), calls=%async_computation.4 | async-start | bytes 1048576 | tf_op jit(solution)/shard_map/all_to_all | solution.py:262
  172.7 2.3 %fusion.4 = bf16[1,384,576]{1,2,0:T(8,128)(2,1)} fusion(bf16[384,576]{1,0:T(8,128)(2,1)} %bitcast.56, s32[384]{0:T(512)S(1)} %add.242), kind=kOutput, calls=%fused_computation.8 | convolution fusion | flops 170237952 | bytes 886272 | tf_op jit(solution)/shard_map/dot_general | solution.py:248
  175.0 7.5 %all-to-all-done.4 = bf16[16,32,512]{2,1,0:T(8,128)(2,1)S(1)} async-done(((bf16[16,32,512]{2,1,0:T(8,128)(2,1)}), bf16[16,32,512]{2,1,0:T(8,128)(2,1)S(1)}, u32[]{:S(2)}, u32[]{:S(2)}) %all-to-all-start.4) | async-done | bytes 524320 | tf_op jit(solution)/shard_map/all_to_all | solution.py:262
  182.5 1.9 %fusion.5 = bf16[1,16,4,8,128]{4,1,2,3,0:T(8,128)(2,1)S(1)} fusion(bf16[8,512,128]{2,1,0:T(8,128)(2,1)} %param.14, bf16[16,4,8,512]{3,2,1,0:T(8,128)(2,1)S(1)} %bitcast.55), kind=kOutput, calls=%fused_computation.10 | convolution fusion | flops 67174400 | bytes 1703936 | tf_op jit(solution)/shard_map/bshl,hlv->bshv/dot_general | solution.py:264
  184.4 0.8 copy.78
  (71 shorter events, 3.4 us)
Async XLA Ops:
  7.2 34.0 %copy-start = (bf16[8,128,512]{2,1,0:T(8,128)(2,1)S(1)}, bf16[8,128,512]{2,1,0:T(8,128)(2,1)}, u32[]{:S(2)}) copy-start(bf16[8,128,512]{2,1,0:T(8,128)(2,1)} %param.13) | copy-start | bytes 3145732
  8.0 1.1 copy-start.2
  25.6 2.3 %copy-start.1 = (bf16[16,256,576]{2,1,0:T(8,128)(2,1)}, bf16[16,256,576]{2,1,0:T(8,128)(2,1)S(1)}, u32[]{:S(2)}) copy-start(bf16[16,256,576]{2,1,0:T(8,128)(2,1)S(1)} %shard_map.113) | copy-start | bytes 14155780
  35.6 5.1 %copy-start.4 = (s32[8,16]{1,0:T(8,128)S(1)}, s32[8,16]{1,0:T(8,128)}, u32[]{:S(2)}) copy-start(s32[8,16]{1,0:T(8,128)} %param.17) | copy-start | bytes 1540
  35.6 5.3 %copy-start.3 = (bf16[1,16,4,8,192]{4,3,2,1,0:T(8,128)(2,1)S(1)}, bf16[1,16,4,8,192]{4,3,2,1,0:T(8,128)(2,1)}, u32[]{:S(2)}) copy-start(bf16[1,16,4,8,192]{4,3,2,1,0:T(8,128)(2,1)} %param.15) | copy-start | bytes 589828
  35.6 35.7 %all-to-all-start = ((bf16[4,4,256,576]{2,3,1,0:T(8,128)(2,1)}), bf16[4,4,256,576]{2,3,1,0:T(8,128)(2,1)}, u32[]{:S(2)}, u32[]{:S(2)}) async-start(bf16[4,4,256,576]{2,3,1,0:T(8,128)(2,1)} %copy.73), calls=%async_computation | async-start | bytes 9437184 | tf_op jit(solution)/shard_map/all_to_all | solution.py:177
  75.8 17.0 %all-to-all-start.1 = ((bf16[4,256,576]{1,2,0:T(8,128)(2,1)}), bf16[4,256,576]{1,2,0:T(8,128)(2,1)S(1)}, u32[]{:S(2)}, u32[]{:S(2)}) async-start(bf16[4,256,576]{1,2,0:T(8,128)(2,1)} %reduce_sum.119), calls=%async_computation.1 | async-start | bytes 2359296 | tf_op jit(solution)/shard_map/all_to_all | solution.py:179
  81.2 12.1 %copy-start.5 = (f32[512]{0:T(512)S(1)}, f32[512]{0:T(512)}, u32[]{:S(2)}) copy-start(f32[512]{0:T(512)} %param.12) | copy-start | bytes 6148
  81.2 39.0 %all-gather.2.cloned.1.call-start = ((), (), s32[]{:S(2)}) async-start(), calls=%async_computation.5 | async-start | bytes 2654208 | tf_op jit(solution)/shard_map/all_gather | solution.py:212
  81.4 13.1 %copy-start.6 = (s32[128]{0:T(128)S(1)}, s32[128]{0:T(128)}, u32[]{:S(2)}) copy-start(s32[128]{0:T(128)} %param.18) | copy-start | bytes 1540
  81.4 13.2 %copy-start.7 = (s32[1,96]{1,0:T(1,128)S(1)}, s32[1,96]{1,0:T(1,128)}, u32[]{:S(2)}) copy-start(s32[1,96]{1,0:T(1,128)} %param.19) | copy-start | bytes 1156
  125.4 24.4 %all-to-all-start.2 = ((bf16[16,48,576]{2,1,0:T(8,128)(2,1)}), bf16[16,48,576]{2,1,0:T(8,128)(2,1)S(1)}, u32[]{:S(2)}, u32[]{:S(2)}) async-start(bf16[16,48,576]{2,1,0:T(8,128)(2,1)} %bitcast.16), calls=%async_computation.2 | async-start | bytes 1966080 | tf_op jit(solution)/shard_map/all_to_all | solution.py:235
  149.8 15.5 %all-to-all-start.3 = ((bf16[16,32,576]{2,1,0:T(8,128)(2,1)}), bf16[16,32,576]{2,1,0:T(8,128)(2,1)S(1)}, u32[]{:S(2)}, u32[]{:S(2)}) async-start(bf16[16,32,576]{2,1,0:T(8,128)(2,1)} %bitcast.50), calls=%async_computation.3 | async-start | bytes 1310720 | tf_op jit(solution)/shard_map/all_to_all | solution.py:213
  168.9 13.6 %all-to-all-start.4 = ((bf16[16,32,512]{2,1,0:T(8,128)(2,1)}), bf16[16,32,512]{2,1,0:T(8,128)(2,1)S(1)}, u32[]{:S(2)}, u32[]{:S(2)}) async-start(bf16[16,32,512]{2,1,0:T(8,128)(2,1)} %bitcast.24), calls=%async_computation.4 | async-start | bytes 1048576 | tf_op jit(solution)/shard_map/all_to_all | solution.py:262
Sparse Core Ops, SparseCore 0:
  94.3 25.8 all-gather.1

commit v2 on v1

v2 whole, which is shorter than its diff:
```python
import functools
import math

import jax
import jax.numpy as jnp
from jax import lax
from jax.experimental import pallas as pl
from jax.experimental.pallas import tpu as pltpu
from jax.sharding import PartitionSpec as P

LAT = 512
ROPE = 64
WIDTH = LAT + ROPE
HDIM = 128
BLK = 64
TOK = 384
REQS = 16
RUN = TOK // REQS
NPG = TOK // BLK
PACK = 256
HOLD = 288
WINDOW = 32
PAIR = 2
SIDE = 4
STEPS = 4

EPS = 1e-06
BF = jnp.bfloat16
F32 = jnp.float32


def project_kernel(
    own_ref, len_ref, hid_ref, down_ref, out_ref, kept_ref, shift_ref, turned_ref, hold_ref, start_ref
):
    step = pl.program_id(0)
    packs = REQS // PAIR

    @pl.when(step == 0)
    def _():
        start_ref[0] = 0
        hold_ref[...] = jnp.zeros_like(hold_ref)
        turned_ref[...] = down_ref[...].astype(F32).T.astype(BF)
        shape = (REQS, WINDOW, TOK)
        offset = lax.broadcasted_iota(jnp.int32, shape, 2)
        offset = offset - lax.broadcasted_iota(jnp.int32, shape, 0)
        shift_ref[...] = offset - REQS * lax.broadcasted_iota(jnp.int32, shape, 1)

    @pl.when(step < packs)
    def _():
        for item in range(PAIR):
            start = start_ref[0]
            length = len_ref[lax.axis_index("dec"), step * PAIR + item]
            count = lax.div(length + (REQS - 1), REQS)
            lead = lax.rem(start, 8)
            base = pl.multiple_of(start - lead, 8)

            for tile in range(1, TOK // 128 + 1):
                tokens, window = 128 * tile, 8 * tile + 8

                @pl.when((count > 8 * tile - 8) & (count <= 8 * tile))
                def _():
                    hid = hid_ref[:, item * TOK : item * TOK + tokens]
                    token = lax.broadcasted_iota(jnp.int32, hid.shape, 1)
                    hid = jnp.where(token < count * REQS, hid, jnp.zeros((), BF))
                    chosen = jnp.where(shift_ref[:, :window, :tokens] == -REQS * lead, 1.0, 0.0)
                    chosen = chosen.reshape(REQS * window, tokens).astype(BF)
                    rows = lax.dot_general(
                        chosen, hid, (((1,), (1,)), ((), ())), preferred_element_type=F32
                    )
                    hold_ref[:, pl.ds(base, window), :] += rows.reshape(REQS, window, -1)

            start_ref[0] = start + count

    @pl.when(step >= packs)
    def _():
        target = step - packs
        for item in range(SIDE):
            rows = hold_ref[target * SIDE + item, :PACK, :].astype(BF)
            part = lax.dot_general(
                turned_ref[...], rows, (((1,), (1,)), ((), ())), preferred_element_type=F32
            )
            out_ref[0, item] = part.astype(BF)

            @pl.when(target == own_ref[0])
            def _():
                kept_ref[item] = part


def project(own, lengths, hidden_t, kv_down):
    depth = hidden_t.shape[0]
    packs = REQS // PAIR
    return pl.pallas_call(
        project_kernel,
        out_shape=(
            jax.ShapeDtypeStruct((SIDE, SIDE, WIDTH, PACK), BF),
            jax.ShapeDtypeStruct((SIDE, WIDTH, PACK), F32),
        ),
        grid_spec=pltpu.PrefetchScalarGridSpec(
            num_scalar_prefetch=2,
            grid=(packs + SIDE,),
            in_specs=[
                pl.BlockSpec((depth, PAIR * TOK), lambda i, *_: (0, jnp.minimum(i, packs - 1))),
                pl.BlockSpec((depth, WIDTH), lambda i, *_: (0, 0)),
            ],
            out_specs=(
                pl.BlockSpec(
                    (1, SIDE, WIDTH, PACK), lambda i, *_: (jnp.maximum(i - packs, 0), 0, 0, 0)
                ),
                pl.BlockSpec((SIDE, WIDTH, PACK), lambda i, *_: (0, 0, 0)),
            ),
            scratch_shapes=[
                pltpu.VMEM((REQS, WINDOW, TOK), jnp.int32),
                pltpu.VMEM((WIDTH, depth), BF),
                pltpu.VMEM((REQS, HOLD, depth), F32),
                pltpu.SMEM((1,), jnp.int32),
            ],
        ),
        compiler_params=pltpu.CompilerParams(vmem_limit_bytes=58 << 20),
        cost_estimate=pl.CostEstimate(
            flops=2 * REQS * TOK * depth * WIDTH, bytes_accessed=13 << 20, transcendentals=0
        ),
    )(own, lengths, hidden_t, kv_down)


def add_up(own, kept, parts):
    total = kept
    for k in range(SIDE):
        total = total + jnp.where(own == k, 0.0, parts[k].astype(F32))
    return total


def first_sum_kernel(own_ref, parts_ref, kept_ref, out_ref, kept_out_ref):
    total = add_up(own_ref[0], kept_ref[0], parts_ref[:, 0])
    out_ref[0] = total.astype(BF)

    @pl.when(pl.program_id(0) == own_ref[1])
    def _():
        kept_out_ref[...] = total


def first_sum(own, parts, kept):
    return pl.pallas_call(
        first_sum_kernel,
        out_shape=(
            jax.ShapeDtypeStruct((SIDE, WIDTH, PACK), BF),
            jax.ShapeDtypeStruct((WIDTH, PACK), F32),
        ),
        grid_spec=pltpu.PrefetchScalarGridSpec(
            num_scalar_prefetch=1,
            grid=(SIDE,),
            in_specs=[
                pl.BlockSpec((SIDE, 1, WIDTH, PACK), lambda i, _: (0, i, 0, 0)),
                pl.BlockSpec((1, WIDTH, PACK), lambda i, _: (i, 0, 0)),
            ],
            out_specs=(
                pl.BlockSpec((1, WIDTH, PACK), lambda i, _: (i, 0, 0)),
                pl.BlockSpec((WIDTH, PACK), lambda i, _: (0, 0)),
            ),
        ),
        compiler_params=pltpu.CompilerParams(vmem_limit_bytes=58 << 20),
    )(own, parts, kept)


def finish_kernel(own_ref, parts_ref, kept_ref, gain_ref, cosine_ref, sine_ref, valid_ref, out_ref):
    half = ROPE // 2
    valid = valid_ref[...] > 0
    total = add_up(own_ref[1], kept_ref[...], parts_ref)
    total = jnp.where(valid, total, 0.0)
    latent = total[:LAT]
    scaling = lax.rsqrt(jnp.sum(latent * latent, 0, keepdims=True) / LAT + EPS)
    out_ref[:LAT] = (latent * scaling * gain_ref[...]).astype(BF)
    first, second = total[LAT : LAT + half], total[LAT + half :]
    cosine, sine = cosine_ref[...], sine_ref[...]
    out_ref[LAT : LAT + half] = (first * cosine - second * sine).astype(BF)
    out_ref[LAT + half :] = (second * cosine + first * sine).astype(BF)


def finish(own, parts, kept, gain, cosine, sine, valid):
    return pl.pallas_call(
        finish_kernel,
        out_shape=jax.ShapeDtypeStruct((WIDTH, PACK), BF),
        in_specs=[pl.BlockSpec(memory_space=pltpu.SMEM)]
        + [pl.BlockSpec(memory_space=pltpu.VMEM)] * 6,
        out_specs=pl.BlockSpec(memory_space=pltpu.VMEM),
        compiler_params=pltpu.CompilerParams(vmem_limit_bytes=24 << 20),
    )(own, parts, kept, gain, cosine, sine, valid)


def select_kernel(source_ref, order_ref, rows_ref, out_ref):
    count = rows_ref.shape[1]
    row = lax.broadcasted_iota(jnp.int32, (count, TOK), 0)
    chosen = jnp.where(row == source_ref[...], 1.0, 0.0).astype(BF)
    mine = jnp.dot(rows_ref[...], chosen, preferred_element_type=F32).astype(BF)
    column = lax.broadcasted_iota(jnp.int32, (2 * TOK, TOK), 1)
    order = jnp.where(column == order_ref[...], 1.0, 0.0).astype(BF)
    out_ref[...] = lax.dot_general(
        order, mine, (((1,), (1,)), ((), ())), preferred_element_type=F32
    ).astype(BF)


def select(source, order, rows):
    return pl.pallas_call(
        select_kernel,
        out_shape=jax.ShapeDtypeStruct((2 * TOK, WIDTH), BF),
        compiler_params=pltpu.CompilerParams(vmem_limit_bytes=40 << 20),
    )(source, order, rows)


def attend_kernel(query_ref, keys_ref, fresh_ref, live_ref, out_ref):
    rows = query_ref.shape[0]
    query = query_ref[...]
    keys = keys_ref[...]
    fresh = fresh_ref[...]
    scale = 1.0 / math.sqrt(HDIM + ROPE)
    across = (((1,), (1,)), ((), ()))
    score = lax.dot_general(query, keys, across, preferred_element_type=F32) * scale
    score = jnp.where(live_ref[...] > 0, score, -1e30)
    later = lax.dot_general(query, fresh, across, preferred_element_type=F32) * scale
    row = lax.broadcasted_iota(jnp.int32, later.shape, 0)
    column = lax.broadcasted_iota(jnp.int32, later.shape, 1)
    at_step = lax.rem(lax.div(row, 8), STEPS)
    later = jnp.where(column <= at_step, later, -1e30)
    top = jnp.maximum(jnp.max(score, -1, keepdims=True), jnp.max(later, -1, keepdims=True))
    score = jnp.exp(score - top)
    later = jnp.exp(later - top)
    total = jnp.sum(score, -1, keepdims=True) + jnp.sum(later, -1, keepdims=True)
    score = (score / total).astype(BF)
    later = (later / total).astype(BF)
    mixed = jnp.dot(score, keys[:, :LAT], preferred_element_type=F32)
    mixed = mixed + jnp.dot(later, fresh[:, :LAT], preferred_element_type=F32)
    out_ref[...] = mixed.astype(BF)


def attend(query, keys, fresh, live):
    count, block = query.shape[0], 128
    return pl.pallas_call(
        attend_kernel,
        out_shape=jax.ShapeDtypeStruct((count, LAT), BF),
        grid=(count // block,),
        in_specs=[
            pl.BlockSpec((block, WIDTH), lambda i: (i, 0)),
            pl.BlockSpec(keys.shape, lambda i: (0, 0)),
            pl.BlockSpec(fresh.shape, lambda i: (0, 0)),
            pl.BlockSpec(live.shape, lambda i: (0, 0)),
        ],
        out_specs=pl.BlockSpec((block, LAT), lambda i: (i, 0)),
        compiler_params=pltpu.CompilerParams(vmem_limit_bytes=24 << 20),
    )(query, keys, fresh, live)


def pick(index, values):
    ids = jnp.arange(values.shape[0], dtype=jnp.int32)
    return jnp.sum(jnp.where(index[..., None] == ids, values, 0), -1)


def groups_of(first):
    found = []
    for core in range(2):
        for x in range(SIDE):
            for other in range(SIDE):
                ring = []
                for k in range(SIDE):
                    y, z = (k, other) if core == first else (other, k)
                    ring.append(((y * SIDE + z) * SIDE + x) * 2 + core)
                found.append(ring)
    return found


def shards(
    hidden, kv_down, kv_gain, uk_weight, uv_weight, queries, new_keys, lengths, assign, block_table
):
    pre_rank = lax.axis_index("pre")
    dec_rank = lax.axis_index("dec")
    both = ("pre", "dec")
    side_y, side_z = pre_rank // SIDE, pre_rank % SIDE
    swapped = side_z * SIDE + side_y
    residue = jnp.where(dec_rank % 2 == 0, pre_rank, swapped)

    counts = (lengths + (REQS - 1)) // REQS
    ends = jnp.cumsum(counts, 1)
    starts = ends - counts
    own_lengths = lax.dynamic_index_in_dim(lengths, dec_rank, 0, keepdims=False)
    own_starts = lax.dynamic_index_in_dim(starts, dec_rank, 0, keepdims=False)
    own_ends = lax.dynamic_index_in_dim(ends, dec_rank, 0, keepdims=False)

    even = dec_rank % 2 == 0
    own = jnp.stack([jnp.where(even, side_y, side_z), jnp.where(even, side_z, side_y)])
    packed, kept = project(own, lengths, hidden[0].T, kv_down)

    packed = lax.all_to_all(packed, both, 0, 0, tiled=True, axis_index_groups=groups_of(0))
    packed, kept = first_sum(own, packed, kept)
    packed = lax.all_to_all(packed, both, 0, 0, tiled=True, axis_index_groups=groups_of(1))

    row = jnp.arange(PACK, dtype=jnp.int32)
    inside = (row >= own_starts[:, None]) & (row < own_ends[:, None])
    place = jnp.sum(jnp.where(inside, row - own_starts[:, None], 0), 0)
    limit = jnp.sum(jnp.where(inside, own_lengths[:, None], 0), 0)
    position = place * REQS + residue
    valid = (position < limit).astype(jnp.int32)[None, :]
    half = ROPE // 2
    frequency = 10000.0 ** (-jnp.arange(half, dtype=F32) * 2.0 / ROPE)
    angles = position[None, :].astype(F32) * frequency[:, None]
    rows = finish(own, packed, kept, kv_gain[:, None], jnp.cos(angles), jnp.sin(angles), valid)

    local_queries = queries[0]
    absorbed = jnp.einsum(
        "bshk,hkl->bshl", local_queries[..., :HDIM], uk_weight, preferred_element_type=F32
    ).astype(BF)
    query_full = jnp.concatenate([absorbed, local_queries[..., HDIM:]], -1)
    query_full = query_full.reshape(REQS, -1, WIDTH)
    rows, query_full = lax.optimization_barrier((rows, query_full))
    everything = lax.all_gather(rows, "dec", axis=1, tiled=True)
    query_full = lax.all_to_all(query_full, "pre", 0, 0, tiled=True)
    everything, query_full = lax.optimization_barrier((everything, query_full))

    slots = lax.dynamic_slice_in_dim(assign, dec_rank * REQS, REQS)
    slot_start = pick(slots, (starts + jnp.arange(starts.shape[0])[:, None] * PACK).reshape(-1))
    slot_count = pick(slots, counts.reshape(-1))
    slot_length = pick(slots, lengths.reshape(-1))
    slot_odd = (slots // REQS) % 2
    run = jnp.arange(RUN, dtype=jnp.int32)
    by_slot = jnp.where(run < slot_count[:, None], slot_start[:, None] + run, -1)
    table = block_table[0]
    pages = table.shape[0]
    page = jnp.arange(pages, dtype=jnp.int32)
    block = jnp.sum(jnp.where(table[None, :] == page[:, None], page[None, :], 0), 1)
    owner, part = block // NPG, block % NPG
    piece = part[:, None] * (RUN // NPG) + jnp.arange(RUN // NPG, dtype=jnp.int32)
    by_page = (owner[:, None] * RUN + piece).reshape(REQS, RUN)
    in_order = jnp.arange(TOK, dtype=jnp.int32).reshape(REQS, RUN)
    order = jnp.concatenate([in_order, by_page], 1).reshape(-1, 1)
    outgoing = select(by_slot.reshape(1, -1), order, everything).reshape(REQS, 2 * RUN, WIDTH)
    arrived = lax.all_to_all(outgoing, "pre", 0, 0, tiled=True)

    sender = jnp.arange(REQS, dtype=jnp.int32)
    sender_swapped = (sender % SIDE) * SIDE + sender // SIDE
    page_odd = pick(owner, slot_odd).reshape(REQS, NPG)
    page_odd = lax.dynamic_index_in_dim(page_odd, pre_rank, 0, keepdims=False)
    sent_residue = jnp.where(page_odd[None, :] == 0, sender[:, None], sender_swapped[:, None])
    target = (
        jnp.arange(NPG, dtype=jnp.int32)[None, :, None] * BLK
        + jnp.arange(RUN // NPG, dtype=jnp.int32)[None, None, :] * REQS
        + sent_residue[:, :, None]
    ).reshape(REQS, RUN)
    target = jnp.concatenate([jnp.full((REQS, RUN), -1, jnp.int32), target], 1).reshape(-1)
    to_place = (jnp.arange(TOK, dtype=jnp.int32)[:, None] == target[None, :]).astype(BF)
    arrived = arrived.reshape(2 * TOK, WIDTH)
    cache = jnp.dot(to_place, arrived, preferred_element_type=F32).astype(BF)

    own_odd = lax.dynamic_index_in_dim(slot_odd, pre_rank, 0, keepdims=False)
    own_length = lax.dynamic_index_in_dim(slot_length, pre_rank, 0, keepdims=False)
    key_residue = jnp.where(own_odd == 0, sender, sender_swapped)
    key_position = run[None, :] * REQS + key_residue[:, None]
    live = (key_position < own_length).astype(jnp.int32)
    live = jnp.concatenate([live, jnp.zeros_like(live)], 1).reshape(1, 2 * TOK)
    fresh = lax.dynamic_index_in_dim(new_keys[0], pre_rank, 0, keepdims=False)
    fresh = jnp.pad(fresh, ((0, 16 - STEPS), (0, 0)))
    mixed = attend(query_full.reshape(-1, WIDTH), arrived, fresh, live)
    mixed = lax.all_to_all(mixed.reshape(REQS, -1, LAT), "pre", 0, 0, tiled=True)
    mixed = mixed.reshape(REQS, STEPS, -1, LAT)
    attended = jnp.einsum("bshl,hlv->bshv", mixed, uv_weight, preferred_element_type=F32).astype(BF)
    return (cache[None], attended[None])


def solution(mesh):
    return jax.shard_map(
        shards,
        mesh=mesh,
        in_specs=(
            P("dec", None, "pre"),
            P("pre", None),
            P(),
            P("pre", None, None),
            P("pre", None, None),
            P("dec", None, None, "pre", None),
            P("dec", None, None, None),
            P(),
            P(),
            P("dec", None),
        ),
        out_specs=(P("dec", "pre", None), P("dec", None, None, "pre", None)),
        check_vma=False,
    )
```

time: 193 us -> 173 us (0.90)
  Pallas kernels: 20.2 us -> 36.5 us
  waiting for transfers between devices: 96.5 us -> 82 us
  local copies, waits for them, and re-layouts: 19.4 us -> 7.79 us
  other arithmetic: 7.9 us -> 2.93 us
  matrix products: 8.43 us -> 3.69 us
    pallas_call x1 -> x4, Pallas kernels: 16.6 us -> 31.1 us  [the longest x1 20.6 us: project(): pl.pallas_call(project_kernel, out_shape=(jax.ShapeDtypeStruct((SIDE, SID...]
    all_gather x1, waiting for transfers between devices: 24.1 us -> 9.7 us  [shards(): everything = lax.all_gather(rows, 'dec', axis=1, tiled=True)]
    reshape x1 -> x2, local copies, waits for them, and re-layouts: 7.67 us -> 0.25 us  [the longest x1 0.17 us: shards(): order = jnp.concatenate([in_order, by_page], 1).reshape(-1, 1)]
    dot_general x2 -> x1, matrix products: 6.19 us -> 1.45 us  [shards(): cache = jnp.dot(to_place, arrived, preferred_element_type=F32).astype(BF)]
    reduce_sum x4 -> x1, other arithmetic: 4.77 us -> 0.09 us  [shards(): limit = jnp.sum(jnp.where(inside, own_lengths[:, None], 0), 0)]
    all_to_all x1, waiting for transfers between devices: 10.9 us -> 8.6 us  [shards(): query_full = lax.all_to_all(query_full, 'pre', 0, 0, tiled=True)]
    unnamed x18 -> x21, local copies, waits for them, and re-layouts: 4.3 us -> 2.68 us
where the time goes in v2:
time: 173 us
  waiting for transfers between devices  82 us (47%)
  Pallas kernels  36.5 us (21%)
  starting transfers between devices  24.8 us (14%)
  between operations  15 us (9%)
  local copies, waits for them, and re-layouts  7.79 us (5%)
  matrix products  3.69 us (2%)
  other arithmetic  2.93 us (2%)
    all_to_all x2, waiting for transfers between devices, shards(): lax.all_to_all(packed, both, 0, 0, tiled=True, axis_index_groups=groups_o...  39.6 us
    pallas_call x1, Pallas kernels, project(): pl.pallas_call(project_kernel, out_shape=(jax.ShapeDtypeStruct((SIDE, SID...  20.6 us
    all_to_all x1, waiting for transfers between devices, shards(): arrived = lax.all_to_all(outgoing, 'pre', 0, 0, tiled=True)  15.5 us
    all_to_all x2, starting transfers between devices, shards(): lax.all_to_all(packed, both, 0, 0, tiled=True, axis_index_groups=groups_o...  10.6 us
    all_gather x1, waiting for transfers between devices, shards(): everything = lax.all_gather(rows, 'dec', axis=1, tiled=True)  9.7 us
    all_to_all x1, waiting for transfers between devices, shards(): lax.all_to_all(mixed.reshape(REQS, -1, LAT), 'pre', 0, 0, tiled=True)  8.61 us
    all_to_all x1, waiting for transfers between devices, shards(): query_full = lax.all_to_all(query_full, 'pre', 0, 0, tiled=True)  8.6 us
    all_to_all x1, starting transfers between devices, shards(): arrived = lax.all_to_all(outgoing, 'pre', 0, 0, tiled=True)  6.98 us
  transfers between devices with their start and end apart: 6, of which 6 were waited for; matrix products, arithmetic and copies ran while one was open for 5% of the time, Pallas kernels for 0%

profile of v2, /device:TPU:0, one launch (start us, length us, event | category | flops | bytes accessed | tf_op | source)
XLA Modules:
  0.0 172.6 jit_solution(7528897536853239360)
XLA Ops:
  7.2 0.6 pad_add_fusion.1.own_ref
  7.8 20.6 %shard_map.113 = (bf16[4,4,576,256]{3,2,1,0:T(8,128)(2,1)}, f32[4,576,256]{2,1,0:T(8,128)}) custom-call(s32[2]{0:T(128)} %pad_add_fusion.1.own_ref, s32[8,16]{1,0:T(8,128)} %len_ref.1, bf16[448,6144]{1,0:T(8,128)(2,1)} %bitcast.67, bf16[448,576]{1,0:T(8,128)(2,1)} %down_ref.1), custom_call_target="tpu_custom_call" | custom-call | flops 3170893824 | bytes 13631488 | tf_op jit(solution)/shard_map/pallas_call | solution.py:92
  28.4 5.1 %all-to-all-start = ((bf16[4,4,576,256]{3,2,1,0:T(8,128)(2,1)}), bf16[4,4,576,256]{3,2,1,0:T(8,128)(2,1)}, u32[]{:S(2)}, u32[]{:S(2)}) async-start(bf16[4,4,576,256]{3,2,1,0:T(8,128)(2,1)} %get-tuple-element.10), calls=%async_computation | async-start | bytes 9437184 | tf_op jit(solution)/shard_map/all_to_all | solution.py:290
  33.6 0.2 reduce_window_sum.11
  33.9 0.2 copy.76
  34.1 0.3 fusion
  34.5 1.2 copy.75
  35.8 28.3 %all-to-all-done.parts_ref = bf16[4,4,576,256]{3,2,1,0:T(8,128)(2,1)} async-done(((bf16[4,4,576,256]{3,2,1,0:T(8,128)(2,1)}), bf16[4,4,576,256]{3,2,1,0:T(8,128)(2,1)}, u32[]{:S(2)}, u32[]{:S(2)}) %all-to-all-start) | async-done | bytes 4718624 | tf_op jit(solution)/shard_map/all_to_all | solution.py:290
  64.1 5.8 %shard_map.114 = (bf16[4,576,256]{2,1,0:T(8,128)(2,1)}, f32[576,256]{1,0:T(8,128)}) custom-call(s32[2]{0:T(128)} %pad_add_fusion.1.own_ref, bf16[4,4,576,256]{3,2,1,0:T(8,128)(2,1)} %all-to-all-done.parts_ref, f32[4,576,256]{2,1,0:T(8,128)} %get-tuple-element.11.kept_ref), custom_call_target="tpu_custom_call" | custom-call | tf_op jit(solution)/shard_map/pallas_call | solution.py:142
  70.0 5.5 %all-to-all-start.1 = ((bf16[4,576,256]{2,1,0:T(8,128)(2,1)}), bf16[4,576,256]{2,1,0:T(8,128)(2,1)S(1)}, u32[]{:S(2)}, u32[]{:S(2)}) async-start(bf16[4,576,256]{2,1,0:T(8,128)(2,1)} %get-tuple-element.12), calls=%async_computation.1 | async-start | bytes 2359296 | tf_op jit(solution)/shard_map/all_to_all | solution.py:292
  75.7 0.2 multiply_sine_fusion
  75.9 11.3 %all-to-all-done.1.parts_ref = bf16[4,576,256]{2,1,0:T(8,128)(2,1)S(1)} async-done(((bf16[4,576,256]{2,1,0:T(8,128)(2,1)}), bf16[4,576,256]{2,1,0:T(8,128)(2,1)S(1)}, u32[]{:S(2)}, u32[]{:S(2)}) %all-to-all-start.1) | async-done | bytes 1179680 | tf_op jit(solution)/shard_map/all_to_all | solution.py:292
  87.1 1.8 %shard_map.115 = bf16[576,256]{1,0:T(8,128)(2,1)} custom-call(s32[2]{0:T(128)S(1)} %copy-done.3, bf16[4,576,256]{2,1,0:T(8,128)(2,1)S(1)} %all-to-all-done.1.parts_ref, f32[576,256]{1,0:T(8,128)S(1)} %copy-done.2, f32[512,1]{1,0:T(8,128)S(1)} %copy.62.gain_ref, f32[32,256]{1,0:T(8,128)S(1)} %get-tuple-element.44.cosine_ref, ...), custom_call_target="tpu_custom_call" | custom-call | tf_op jit(solution)/shard_map/pallas_call | solution.py:179
  90.1 0.2 select_reduce_fusion.3
  90.4 3.6 %all-to-all-start.2 = ((bf16[16,32,576]{2,1,0:T(8,128)(2,1)}), bf16[16,32,576]{2,1,0:T(8,128)(2,1)S(1)}, u32[]{:S(2)}, u32[]{:S(2)}) async-start(bf16[16,32,576]{2,1,0:T(8,128)(2,1)} %bitcast.59), calls=%async_computation.2 | async-start | bytes 1310720 | tf_op jit(solution)/shard_map/all_to_all | solution.py:313
  94.3 0.2 reshape.323.order_ref
  94.5 0.6 dynamic_slice.35
  95.1 0.6 dynamic_slice.34
  96.4 8.6 %all-to-all-done.2 = bf16[16,32,576]{2,1,0:T(8,128)(2,1)S(1)} async-done(((bf16[16,32,576]{2,1,0:T(8,128)(2,1)}), bf16[16,32,576]{2,1,0:T(8,128)(2,1)S(1)}, u32[]{:S(2)}, u32[]{:S(2)}) %all-to-all-start.2) | async-done | bytes 589856 | tf_op jit(solution)/shard_map/all_to_all | solution.py:313
  105.0 9.7 %all-gather.2.cloned.1.call-done.rows_ref = bf16[576,2048]{1,0:T(8,128)(2,1)} async-done(((bf16[576,256]{1,0:T(8,128)(2,1)}), bf16[576,2048]{1,0:T(8,128)(2,1)}) %all-gather.2.cloned.1.call-update) | async-done | bytes 2359312 | tf_op jit(solution)/shard_map/all_gather | solution.py:312
  114.7 1.7 copy-done.1
  116.3 2.9 %shard_map.116 = bf16[768,576]{1,0:T(8,128)(2,1)} custom-call(s32[1,384]{1,0:T(1,128)S(1)} %select_n.183.source_ref, s32[768,1]{1,0:T(8,128)S(1)} %reshape.323.order_ref, bf16[576,2048]{1,0:T(8,128)(2,1)S(1)} %copy-done.1), custom_call_target="tpu_custom_call" | custom-call | tf_op jit(solution)/shard_map/pallas_call | solution.py:202
  119.3 7.0 %all-to-all-start.3 = ((bf16[16,48,576]{2,1,0:T(8,128)(2,1)}), bf16[16,48,576]{2,1,0:T(8,128)(2,1)S(1)}, u32[]{:S(2)}, u32[]{:S(2)}) async-start(bf16[16,48,576]{2,1,0:T(8,128)(2,1)} %bitcast.19), calls=%async_computation.3 | async-start | bytes 1966080 | tf_op jit(solution)/shard_map/all_to_all | solution.py:333
  126.3 0.7 add_compare_fusion
  127.4 0.7 dynamic-slice_bitcast_fusion
  128.2 15.5 %all-to-all-done.3 = bf16[16,48,576]{2,1,0:T(8,128)(2,1)S(1)} async-done(((bf16[16,48,576]{2,1,0:T(8,128)(2,1)}), bf16[16,48,576]{2,1,0:T(8,128)(2,1)S(1)}, u32[]{:S(2)}, u32[]{:S(2)}) %all-to-all-start.3) | async-done | bytes 884768 | tf_op jit(solution)/shard_map/all_to_all | solution.py:333
  143.7 5.3 %shard_map.117 = bf16[512,512]{1,0:T(8,128)(2,1)} custom-call(bf16[512,576]{1,0:T(8,128)(2,1)S(1)} %bitcast.57, bf16[768,576]{1,0:T(8,128)(2,1)S(1)} %bitcast.55, bf16[16,576]{1,0:T(8,128)(2,1)S(1)} %pad.7.fresh_ref, s32[1,768]{1,0:T(1,128)S(1)} %reshape.320.live_ref), custom_call_target="tpu_custom_call" | custom-call | tf_op jit(solution)/shard_map/pallas_call | solution.py:236
  149.0 3.6 %all-to-all-start.4 = ((bf16[16,32,512]{2,1,0:T(8,128)(2,1)}), bf16[16,32,512]{2,1,0:T(8,128)(2,1)S(1)}, u32[]{:S(2)}, u32[]{:S(2)}) async-start(bf16[16,32,512]{2,1,0:T(8,128)(2,1)} %bitcast.26), calls=%async_computation.4 | async-start | bytes 1048576 | tf_op jit(solution)/shard_map/all_to_all | solution.py:359
  153.0 1.5 fusion.1
  154.5 8.6 %all-to-all-done.4 = bf16[16,32,512]{2,1,0:T(8,128)(2,1)S(1)} async-done(((bf16[16,32,512]{2,1,0:T(8,128)(2,1)}), bf16[16,32,512]{2,1,0:T(8,128)(2,1)S(1)}, u32[]{:S(2)}, u32[]{:S(2)}) %all-to-all-start.4) | async-done | bytes 524320 | tf_op jit(solution)/shard_map/all_to_all | solution.py:359
  163.1 1.9 %fusion.2 = bf16[1,16,4,8,128]{4,1,2,3,0:T(8,128)(2,1)S(1)} fusion(bf16[8,512,128]{2,1,0:T(8,128)(2,1)} %param.14, bf16[16,4,8,512]{3,2,1,0:T(8,128)(2,1)S(1)} %bitcast.60), kind=kOutput, calls=%fused_computation.6 | convolution fusion | flops 67174400 | bytes 1703936 | tf_op jit(solution)/shard_map/bshl,hlv->bshv/dot_general | solution.py:361
  165.0 0.8 copy.67
  (77 shorter events, 2.9 us)
Async XLA Ops:
  7.2 26.9 %copy-start = (bf16[8,128,512]{2,1,0:T(8,128)(2,1)S(1)}, bf16[8,128,512]{2,1,0:T(8,128)(2,1)}, u32[]{:S(2)}) copy-start(bf16[8,128,512]{2,1,0:T(8,128)(2,1)} %param.13) | copy-start | bytes 3145732
  28.4 5.1 %copy-start.5 = (s32[8,16]{1,0:T(8,128)S(1)}, s32[8,16]{1,0:T(8,128)}, u32[]{:S(2)}) copy-start(s32[8,16]{1,0:T(8,128)} %len_ref.1) | copy-start | bytes 1540
  28.4 5.3 %copy-start.6 = (f32[512]{0:T(512)S(1)}, f32[512]{0:T(512)}, u32[]{:S(2)}) copy-start(f32[512]{0:T(512)} %param.12) | copy-start | bytes 6148
  28.4 5.5 %copy-start.4 = (bf16[1,16,4,8,192]{4,3,2,1,0:T(8,128)(2,1)S(1)}, bf16[1,16,4,8,192]{4,3,2,1,0:T(8,128)(2,1)}, u32[]{:S(2)}) copy-start(bf16[1,16,4,8,192]{4,3,2,1,0:T(8,128)(2,1)} %param.15) | copy-start | bytes 589828
  28.4 35.7 %all-to-all-start = ((bf16[4,4,576,256]{3,2,1,0:T(8,128)(2,1)}), bf16[4,4,576,256]{3,2,1,0:T(8,128)(2,1)}, u32[]{:S(2)}, u32[]{:S(2)}) async-start(bf16[4,4,576,256]{3,2,1,0:T(8,128)(2,1)} %get-tuple-element.10), calls=%async_computation | async-start | bytes 9437184 | tf_op jit(solution)/shard_map/all_to_all | solution.py:290
  70.0 17.1 %copy-start.2 = (f32[576,256]{1,0:T(8,128)S(1)}, f32[576,256]{1,0:T(8,128)}, u32[]{:S(2)}) copy-start(f32[576,256]{1,0:T(8,128)} %get-tuple-element.13.kept_ref) | copy-start | bytes 1769476
  70.0 17.1 %copy-start.3 = (s32[2]{0:T(128)S(1)}, s32[2]{0:T(128)}, u32[]{:S(2)}) copy-start(s32[2]{0:T(128)} %pad_add_fusion.1.own_ref) | copy-start | bytes 28
  70.0 17.1 %all-to-all-start.1 = ((bf16[4,576,256]{2,1,0:T(8,128)(2,1)}), bf16[4,576,256]{2,1,0:T(8,128)(2,1)S(1)}, u32[]{:S(2)}, u32[]{:S(2)}) async-start(bf16[4,576,256]{2,1,0:T(8,128)(2,1)} %get-tuple-element.12), calls=%async_computation.1 | async-start | bytes 2359296 | tf_op jit(solution)/shard_map/all_to_all | solution.py:292
  75.5 39.2 %all-gather.2.cloned.1.call-start = ((), (), s32[]{:S(2)}) async-start(), calls=%async_computation.5 | async-start | bytes 2654208 | tf_op jit(solution)/shard_map/all_gather | solution.py:312
  87.1 2.1 %copy-start.8 = (s32[1,96]{1,0:T(1,128)S(1)}, s32[1,96]{1,0:T(1,128)}, u32[]{:S(2)}) copy-start(s32[1,96]{1,0:T(1,128)} %param.19) | copy-start | bytes 1156
  87.1 2.8 %copy-start.7 = (s32[128]{0:T(128)S(1)}, s32[128]{0:T(128)}, u32[]{:S(2)}) copy-start(s32[128]{0:T(128)} %param.18) | copy-start | bytes 1540
  90.4 14.6 %all-to-all-start.2 = ((bf16[16,32,576]{2,1,0:T(8,128)(2,1)}), bf16[16,32,576]{2,1,0:T(8,128)(2,1)S(1)}, u32[]{:S(2)}, u32[]{:S(2)}) async-start(bf16[16,32,576]{2,1,0:T(8,128)(2,1)} %bitcast.59), calls=%async_computation.2 | async-start | bytes 1310720 | tf_op jit(solution)/shard_map/all_to_all | solution.py:313
  114.7 1.7 copy-start.1
  119.3 24.4 %all-to-all-start.3 = ((bf16[16,48,576]{2,1,0:T(8,128)(2,1)}), bf16[16,48,576]{2,1,0:T(8,128)(2,1)S(1)}, u32[]{:S(2)}, u32[]{:S(2)}) async-start(bf16[16,48,576]{2,1,0:T(8,128)(2,1)} %bitcast.19), calls=%async_computation.3 | async-start | bytes 1966080 | tf_op jit(solution)/shard_map/all_to_all | solution.py:333
  149.0 14.1 %all-to-all-start.4 = ((bf16[16,32,512]{2,1,0:T(8,128)(2,1)}), bf16[16,32,512]{2,1,0:T(8,128)(2,1)S(1)}, u32[]{:S(2)}, u32[]{:S(2)}) async-start(bf16[16,32,512]{2,1,0:T(8,128)(2,1)} %bitcast.26), calls=%async_computation.4 | async-start | bytes 1048576 | tf_op jit(solution)/shard_map/all_to_all | solution.py:359
Sparse Core Ops, SparseCore 0:
  89.1 25.5 all-gather.1

commit v3 on v2

v3 whole, which is shorter than its diff:
```python
import functools
import math

import jax
import jax.numpy as jnp
from jax import lax
from jax.experimental import pallas as pl
from jax.experimental.pallas import tpu as pltpu
from jax.sharding import PartitionSpec as P

LAT = 512
ROPE = 64
WIDTH = LAT + ROPE
HDIM = 128
BLK = 64
TOK = 384
REQS = 16
RUN = TOK // REQS
NPG = TOK // BLK
PACK = 256
HOLD = 288
AHEAD = 3
PAIR = 2
SIDE = 4
STEPS = 4

EPS = 1e-06
BF = jnp.bfloat16
F32 = jnp.float32


def project_kernel(
    len_ref, hid_ref, down_ref, out_ref, span_ref, sent_ref, shift_ref, turned_ref, hold_ref, in_sem, out_sem
):
    def load(part):
        where = pl.ds(part * PAIR * TOK, PAIR * TOK)
        return pltpu.make_async_copy(hid_ref.at[:, where], span_ref.at[:, where], in_sem.at[part])

    def store(residue):
        where = residue // SIDE, residue % SIDE
        return pltpu.make_async_copy(sent_ref.at[residue], out_ref.at[where], out_sem.at[residue])

    parts = REQS // PAIR
    for part in range(AHEAD):
        load(part).start()
    hold_ref[...] = jnp.zeros_like(hold_ref)
    turned_ref[...] = down_ref[...].astype(F32).T.astype(BF)
    shape = (REQS, 24, 256)
    offset = lax.broadcasted_iota(jnp.int32, shape, 2)
    offset = offset - lax.broadcasted_iota(jnp.int32, shape, 0)
    shift_ref[...] = offset - REQS * lax.broadcasted_iota(jnp.int32, shape, 1)

    start = 0
    for request in range(REQS):
        part = request // PAIR
        if request % PAIR == 0:
            load(part).wait()
            if part + AHEAD < parts:
                load(part + AHEAD).start()
        length = len_ref[lax.axis_index("dec"), request]
        count = lax.div(length + (REQS - 1), REQS)
        lead = lax.rem(start, 8)
        base = pl.multiple_of(start - lead, 8)

        for first, tokens, window in ((0, 256, 24), (256, 128, 16)):
            begin = request * TOK + first
            hid = span_ref[:, begin : begin + tokens]
            token = lax.broadcasted_iota(jnp.int32, hid.shape, 1)
            hid = jnp.where(token < count * REQS - first, hid, jnp.zeros((), BF))
            chosen = jnp.where(shift_ref[:, :window, :tokens] == -REQS * lead, 1.0, 0.0)
            chosen = chosen.reshape(REQS * window, tokens).astype(BF)
            rows = lax.dot_general(
                chosen, hid, (((1,), (1,)), ((), ())), preferred_element_type=F32
            )
            place = pl.ds(pl.multiple_of(base + first // REQS, 8), window)
            hold_ref[:, place, :] += rows.reshape(REQS, window, -1)

        start = start + count

    for residue in range(REQS):
        rows = hold_ref[residue, :PACK, :].astype(BF)
        sent_ref[residue] = lax.dot_general(
            turned_ref[...], rows, (((1,), (1,)), ((), ())), preferred_element_type=F32
        ).astype(BF)
        store(residue).start()
    for residue in range(REQS):
        store(residue).wait()


def project(lengths, hidden_t, kv_down):
    depth = hidden_t.shape[0]
    return pl.pallas_call(
        project_kernel,
        out_shape=jax.ShapeDtypeStruct((SIDE, SIDE, WIDTH, PACK), BF),
        in_specs=[
            pl.BlockSpec(memory_space=pltpu.SMEM),
            pl.BlockSpec(memory_space=pl.ANY),
            pl.BlockSpec(memory_space=pltpu.VMEM),
        ],
        out_specs=pl.BlockSpec(memory_space=pl.ANY),
        scratch_shapes=[
            pltpu.VMEM((depth, REQS * TOK), BF),
            pltpu.VMEM((REQS, WIDTH, PACK), BF),
            pltpu.VMEM((REQS, 24, 256), jnp.int32),
            pltpu.VMEM((WIDTH, depth), BF),
            pltpu.VMEM((REQS, HOLD, depth), F32),
            pltpu.SemaphoreType.DMA((REQS // PAIR,)),
            pltpu.SemaphoreType.DMA((REQS,)),
        ],
        compiler_params=pltpu.CompilerParams(vmem_limit_bytes=58 << 20),
        cost_estimate=pl.CostEstimate(
            flops=2 * REQS * TOK * depth * WIDTH, bytes_accessed=11 << 20, transcendentals=0
        ),
    )(lengths, hidden_t, kv_down)


def add_up(parts):
    total = parts[0].astype(F32)
    for k in range(1, SIDE):
        total = total + parts[k].astype(F32)
    return total


def first_sum_kernel(parts_ref, out_ref, sent_ref, out_sem):
    def store(part):
        return pltpu.make_async_copy(sent_ref.at[part], out_ref.at[part], out_sem.at[part])

    for part in range(SIDE):
        sent_ref[part] = add_up(parts_ref[:, part]).astype(BF)
        store(part).start()
    for part in range(SIDE):
        store(part).wait()


def first_sum(parts):
    return pl.pallas_call(
        first_sum_kernel,
        out_shape=jax.ShapeDtypeStruct((SIDE, WIDTH, PACK), BF),
        in_specs=[pl.BlockSpec(memory_space=pltpu.VMEM)],
        out_specs=pl.BlockSpec(memory_space=pl.ANY),
        scratch_shapes=[
            pltpu.VMEM((SIDE, WIDTH, PACK), BF),
            pltpu.SemaphoreType.DMA((SIDE,)),
        ],
        compiler_params=pltpu.CompilerParams(vmem_limit_bytes=16 << 20),
    )(parts)


def finish_kernel(parts_ref, gain_ref, cosine_ref, sine_ref, valid_ref, out_ref):
    half = ROPE // 2
    valid = valid_ref[...] > 0
    total = jnp.where(valid, add_up(parts_ref), 0.0)
    latent = total[:LAT]
    scaling = lax.rsqrt(jnp.sum(latent * latent, 0, keepdims=True) / LAT + EPS)
    out_ref[:LAT] = (latent * scaling * gain_ref[...]).astype(BF)
    first, second = total[LAT : LAT + half], total[LAT + half :]
    cosine, sine = cosine_ref[...], sine_ref[...]
    out_ref[LAT : LAT + half] = (first * cosine - second * sine).astype(BF)
    out_ref[LAT + half :] = (second * cosine + first * sine).astype(BF)


def finish(parts, gain, cosine, sine, valid):
    return pl.pallas_call(
        finish_kernel,
        out_shape=jax.ShapeDtypeStruct((WIDTH, PACK), BF),
        compiler_params=pltpu.CompilerParams(vmem_limit_bytes=24 << 20),
    )(parts, gain, cosine, sine, valid)


def select_kernel(source_ref, order_ref, rows_ref, out_ref):
    count = rows_ref.shape[1]
    row = lax.broadcasted_iota(jnp.int32, (count, TOK), 0)
    chosen = jnp.where(row == source_ref[...], 1.0, 0.0).astype(BF)
    mine = jnp.dot(rows_ref[...], chosen, preferred_element_type=F32).astype(BF)
    column = lax.broadcasted_iota(jnp.int32, (2 * TOK, TOK), 1)
    order = jnp.where(column == order_ref[...], 1.0, 0.0).astype(BF)
    out_ref[...] = lax.dot_general(
        order, mine, (((1,), (1,)), ((), ())), preferred_element_type=F32
    ).astype(BF)


def select(source, order, rows):
    return pl.pallas_call(
        select_kernel,
        out_shape=jax.ShapeDtypeStruct((2 * TOK, WIDTH), BF),
        compiler_params=pltpu.CompilerParams(vmem_limit_bytes=40 << 20),
    )(source, order, rows)


def attend_kernel(query_ref, keys_ref, fresh_ref, live_ref, out_ref):
    scale = 1.0 / math.sqrt(HDIM + ROPE)
    across = (((1,), (1,)), ((), ()))
    row = lax.broadcasted_iota(jnp.int32, (TOK, 2 * TOK), 0)
    column = lax.broadcasted_iota(jnp.int32, (TOK, 2 * TOK), 1)
    kept = jnp.where(row + RUN * lax.div(row, RUN) == column, 1.0, 0.0).astype(BF)
    keys = jnp.dot(kept, keys_ref[...], preferred_element_type=F32).astype(BF)
    fresh = fresh_ref[...]
    query = query_ref[...]
    score = lax.dot_general(query, keys, across, preferred_element_type=F32) * scale
    score = jnp.where(live_ref[...] > 0, score, -1e30)
    later = lax.dot_general(query, fresh, across, preferred_element_type=F32) * scale
    row = lax.broadcasted_iota(jnp.int32, later.shape, 0)
    column = lax.broadcasted_iota(jnp.int32, later.shape, 1)
    at_step = lax.rem(lax.div(row, 8), STEPS)
    later = jnp.where(column <= at_step, later, -1e30)
    top = jnp.maximum(jnp.max(score, -1, keepdims=True), jnp.max(later, -1, keepdims=True))
    score = jnp.exp(score - top)
    later = jnp.exp(later - top)
    total = jnp.sum(score, -1, keepdims=True) + jnp.sum(later, -1, keepdims=True)
    inverse = 1.0 / total
    score = (score * inverse).astype(BF)
    later = (later * inverse).astype(BF)
    mixed = jnp.dot(score, keys[:, :LAT], preferred_element_type=F32)
    mixed = mixed + jnp.dot(later, fresh[:, :LAT], preferred_element_type=F32)
    out_ref[...] = mixed.astype(BF)


def attend(query, keys, fresh, live):
    return pl.pallas_call(
        attend_kernel,
        out_shape=jax.ShapeDtypeStruct((query.shape[0], LAT), BF),
        compiler_params=pltpu.CompilerParams(vmem_limit_bytes=24 << 20),
    )(query, keys, fresh, live)


def pick(index, values):
    ids = jnp.arange(values.shape[0], dtype=jnp.int32)
    return jnp.sum(jnp.where(index[..., None] == ids, values, 0), -1)


def groups_of(first):
    found = []
    for core in range(2):
        for x in range(SIDE):
            for other in range(SIDE):
                ring = []
                for k in range(SIDE):
                    y, z = (k, other) if core == first else (other, k)
                    ring.append(((y * SIDE + z) * SIDE + x) * 2 + core)
                found.append(ring)
    return found


def shards(
    hidden, kv_down, kv_gain, uk_weight, uv_weight, queries, new_keys, lengths, assign, block_table
):
    pre_rank = lax.axis_index("pre")
    dec_rank = lax.axis_index("dec")
    both = ("pre", "dec")
    side_y, side_z = pre_rank // SIDE, pre_rank % SIDE
    swapped = side_z * SIDE + side_y
    residue = jnp.where(dec_rank % 2 == 0, pre_rank, swapped)

    counts = (lengths + (REQS - 1)) // REQS
    ends = jnp.cumsum(counts, 1)
    starts = ends - counts
    own_lengths = lax.dynamic_index_in_dim(lengths, dec_rank, 0, keepdims=False)
    own_starts = lax.dynamic_index_in_dim(starts, dec_rank, 0, keepdims=False)
    own_ends = lax.dynamic_index_in_dim(ends, dec_rank, 0, keepdims=False)

    packed = project(lengths, hidden[0].T, kv_down)

    packed = lax.all_to_all(packed, both, 0, 0, tiled=True, axis_index_groups=groups_of(0))
    packed = first_sum(packed)
    packed = lax.all_to_all(packed, both, 0, 0, tiled=True, axis_index_groups=groups_of(1))

    row = jnp.arange(PACK, dtype=jnp.int32)
    inside = (row >= own_starts[:, None]) & (row < own_ends[:, None])
    place = jnp.sum(jnp.where(inside, row - own_starts[:, None], 0), 0)
    limit = jnp.sum(jnp.where(inside, own_lengths[:, None], 0), 0)
    position = place * REQS + residue
    valid = (position < limit).astype(jnp.int32)[None, :]
    half = ROPE // 2
    frequency = 10000.0 ** (-jnp.arange(half, dtype=F32) * 2.0 / ROPE)
    angles = position[None, :].astype(F32) * frequency[:, None]
    rows = finish(packed, kv_gain[:, None], jnp.cos(angles), jnp.sin(angles), valid)

    local_queries = queries[0]
    absorbed = jnp.einsum(
        "bshk,hkl->bshl", local_queries[..., :HDIM], uk_weight, preferred_element_type=F32
    ).astype(BF)
    query_full = jnp.concatenate([absorbed, local_queries[..., HDIM:]], -1)
    query_full = query_full.reshape(REQS, -1, WIDTH)
    rows, query_full = lax.optimization_barrier((rows, query_full))
    everything = lax.all_gather(rows, "dec", axis=1, tiled=True)
    query_full = lax.all_to_all(query_full, "pre", 0, 0, tiled=True)
    everything, query_full = lax.optimization_barrier((everything, query_full))

    slots = lax.dynamic_slice_in_dim(assign, dec_rank * REQS, REQS)
    slot_start = pick(slots, (starts + jnp.arange(starts.shape[0])[:, None] * PACK).reshape(-1))
    slot_count = pick(slots, counts.reshape(-1))
    slot_length = pick(slots, lengths.reshape(-1))
    slot_odd = (slots // REQS) % 2
    run = jnp.arange(RUN, dtype=jnp.int32)
    by_slot = jnp.where(run < slot_count[:, None], slot_start[:, None] + run, -1)
    table = block_table[0]
    pages = table.shape[0]
    page = jnp.arange(pages, dtype=jnp.int32)
    block = jnp.sum(jnp.where(table[None, :] == page[:, None], page[None, :], 0), 1)
    owner, part = block // NPG, block % NPG
    piece = part[:, None] * (RUN // NPG) + jnp.arange(RUN // NPG, dtype=jnp.int32)
    by_page = (owner[:, None] * RUN + piece).reshape(REQS, RUN)
    in_order = jnp.arange(TOK, dtype=jnp.int32).reshape(REQS, RUN)
    order = jnp.concatenate([in_order, by_page], 1).reshape(-1, 1)
    outgoing = select(by_slot.reshape(1, -1), order, everything).reshape(REQS, 2 * RUN, WIDTH)
    arrived = lax.all_to_all(outgoing, "pre", 0, 0, tiled=True)

    sender = jnp.arange(REQS, dtype=jnp.int32)
    sender_swapped = (sender % SIDE) * SIDE + sender // SIDE
    page_odd = pick(owner, slot_odd).reshape(REQS, NPG)
    page_odd = lax.dynamic_index_in_dim(page_odd, pre_rank, 0, keepdims=False)
    sent_residue = jnp.where(page_odd[None, :] == 0, sender[:, None], sender_swapped[:, None])
    target = (
        jnp.arange(NPG, dtype=jnp.int32)[None, :, None] * BLK
        + jnp.arange(RUN // NPG, dtype=jnp.int32)[None, None, :] * REQS
        + sent_residue[:, :, None]
    ).reshape(REQS, RUN)
    target = jnp.concatenate([jnp.full((REQS, RUN), -1, jnp.int32), target], 1).reshape(-1)
    to_place = (jnp.arange(TOK, dtype=jnp.int32)[:, None] == target[None, :]).astype(BF)
    arrived = arrived.reshape(2 * TOK, WIDTH)
    cache = jnp.dot(to_place, arrived, preferred_element_type=F32).astype(BF)

    own_odd = lax.dynamic_index_in_dim(slot_odd, pre_rank, 0, keepdims=False)
    own_length = lax.dynamic_index_in_dim(slot_length, pre_rank, 0, keepdims=False)
    key_residue = jnp.where(own_odd == 0, sender, sender_swapped)
    key_position = run[None, :] * REQS + key_residue[:, None]
    live = (key_position < own_length).astype(jnp.int32).reshape(1, TOK)
    fresh = lax.dynamic_index_in_dim(new_keys[0], pre_rank, 0, keepdims=False)
    fresh = jnp.pad(fresh, ((0, 16 - STEPS), (0, 0)))
    mixed = attend(query_full.reshape(-1, WIDTH), arrived, fresh, live)
    mixed = lax.all_to_all(mixed.reshape(REQS, -1, LAT), "pre", 0, 0, tiled=True)
    mixed = mixed.reshape(REQS, STEPS, -1, LAT)
    attended = jnp.einsum("bshl,hlv->bshv", mixed, uv_weight, preferred_element_type=F32).astype(BF)
    return (cache[None], attended[None])


def solution(mesh):
    return jax.shard_map(
        shards,
        mesh=mesh,
        in_specs=(
            P("dec", None, "pre"),
            P("pre", None),
            P(),
            P("pre", None, None),
            P("pre", None, None),
            P("dec", None, None, "pre", None),
            P("dec", None, None, None),
            P(),
            P(),
            P("dec", None),
        ),
        out_specs=(P("dec", "pre", None), P("dec", None, None, "pre", None)),
        check_vma=False,
    )
```

time: 173 us -> 158 us (0.913)
  Pallas kernels: 36.5 us -> 21.3 us
    pallas_call x3, Pallas kernels: 31.7 us -> 17.2 us  [the longest x1 10.7 us: project(): pl.pallas_call(project_kernel, out_shape=jax.ShapeDtypeStruct((SIDE, SIDE...]
  transfers between devices with their start and end apart: 6 -> 6, of which waited for: 6 -> 6; matrix products, arithmetic and copies ran while one was open for 5% -> 6% of each run, Pallas kernels for 0% -> 0%
where the time goes in v3:
time: 158 us; the launch traced here: 157 us
  waiting for transfers between devices  82.1 us (52%)
  starting transfers between devices  24.8 us (16%)
  Pallas kernels  21.3 us (13%)
  between operations  14.9 us (9%)
  local copies, waits for them, and re-layouts  7.73 us (5%)
  matrix products  3.7 us (2%)
  other arithmetic  2.3 us (1%)
    all_to_all x2, waiting for transfers between devices, shards(): lax.all_to_all(packed, both, 0, 0, tiled=True, axis_index_groups=groups_o...  39.6 us
    all_to_all x1, waiting for transfers between devices, shards(): arrived = lax.all_to_all(outgoing, 'pre', 0, 0, tiled=True)  15.5 us
    pallas_call x1, Pallas kernels, project(): pl.pallas_call(project_kernel, out_shape=jax.ShapeDtypeStruct((SIDE, SIDE...  10.7 us
    all_to_all x2, starting transfers between devices, shards(): lax.all_to_all(packed, both, 0, 0, tiled=True, axis_index_groups=groups_o...  10.5 us
    all_gather x1, waiting for transfers between devices, shards(): everything = lax.all_gather(rows, 'dec', axis=1, tiled=True)  10.1 us
    all_to_all x1, waiting for transfers between devices, shards(): lax.all_to_all(mixed.reshape(REQS, -1, LAT), 'pre', 0, 0, tiled=True)  8.62 us
    all_to_all x1, waiting for transfers between devices, shards(): query_full = lax.all_to_all(query_full, 'pre', 0, 0, tiled=True)  8.36 us
    all_to_all x1, starting transfers between devices, shards(): arrived = lax.all_to_all(outgoing, 'pre', 0, 0, tiled=True)  6.99 us
  transfers between devices with their start and end apart: 6, of which 6 were waited for; matrix products, arithmetic and copies ran while one was open for 6% of the time, Pallas kernels for 0%

profile of v3, /device:TPU:0, one launch (start us, length us, event | category | flops | bytes accessed | tf_op | source)
XLA Modules:
  0.0 156.9 jit_solution(4252677059178959679)
XLA Ops:
  7.2 10.7 %shard_map.113 = bf16[4,4,576,256]{3,2,1,0:T(8,128)(2,1)} custom-call(s32[8,16]{1,0:T(8,128)} %len_ref.1, bf16[448,6144]{1,0:T(8,128)(2,1)} %bitcast.64, bf16[448,576]{1,0:T(8,128)(2,1)} %down_ref.1), custom_call_target="tpu_custom_call" | custom-call | flops 3170893824 | bytes 11534336 | tf_op jit(solution)/shard_map/pallas_call | solution.py:92
  17.9 5.1 %all-to-all-start = ((bf16[4,4,576,256]{3,2,1,0:T(8,128)(2,1)}), bf16[4,4,576,256]{3,2,1,0:T(8,128)(2,1)}, u32[]{:S(2)}, u32[]{:S(2)}) async-start(bf16[4,4,576,256]{3,2,1,0:T(8,128)(2,1)} %shard_map.113), calls=%async_computation | async-start | bytes 9437184 | tf_op jit(solution)/shard_map/all_to_all | solution.py:263
  23.1 0.2 reduce_window_sum.11
  23.2 0.1 copy.62.gain_ref
  23.4 0.2 copy.76
  23.6 0.3 fusion
  24.0 1.2 copy.75
  25.3 28.3 %all-to-all-done.parts_ref = bf16[4,4,576,256]{3,2,1,0:T(8,128)(2,1)} async-done(((bf16[4,4,576,256]{3,2,1,0:T(8,128)(2,1)}), bf16[4,4,576,256]{3,2,1,0:T(8,128)(2,1)}, u32[]{:S(2)}, u32[]{:S(2)}) %all-to-all-start) | async-done | bytes 4718624 | tf_op jit(solution)/shard_map/all_to_all | solution.py:263
  53.6 3.7 %shard_map.114 = bf16[4,576,256]{2,1,0:T(8,128)(2,1)} custom-call(bf16[4,4,576,256]{3,2,1,0:T(8,128)(2,1)} %all-to-all-done.parts_ref), custom_call_target="tpu_custom_call" | custom-call | tf_op jit(solution)/shard_map/pallas_call | solution.py:136
  57.3 5.4 %all-to-all-start.1 = ((bf16[4,576,256]{2,1,0:T(8,128)(2,1)}), bf16[4,576,256]{2,1,0:T(8,128)(2,1)S(1)}, u32[]{:S(2)}, u32[]{:S(2)}) async-start(bf16[4,576,256]{2,1,0:T(8,128)(2,1)} %shard_map.114), calls=%async_computation.1 | async-start | bytes 2359296 | tf_op jit(solution)/shard_map/all_to_all | solution.py:265
  62.9 0.2 multiply_sine_fusion
  63.1 11.2 %all-to-all-done.1.parts_ref = bf16[4,576,256]{2,1,0:T(8,128)(2,1)S(1)} async-done(((bf16[4,576,256]{2,1,0:T(8,128)(2,1)}), bf16[4,576,256]{2,1,0:T(8,128)(2,1)S(1)}, u32[]{:S(2)}, u32[]{:S(2)}) %all-to-all-start.1) | async-done | bytes 1179680 | tf_op jit(solution)/shard_map/all_to_all | solution.py:265
  74.3 1.1 shard_map.115
  76.5 0.2 select_reduce_fusion.3
  76.9 3.8 %all-to-all-start.2 = ((bf16[16,32,576]{2,1,0:T(8,128)(2,1)}), bf16[16,32,576]{2,1,0:T(8,128)(2,1)S(1)}, u32[]{:S(2)}, u32[]{:S(2)}) async-start(bf16[16,32,576]{2,1,0:T(8,128)(2,1)} %bitcast.51), calls=%async_computation.2 | async-start | bytes 1310720 | tf_op jit(solution)/shard_map/all_to_all | solution.py:286
  81.0 0.2 reshape.348.order_ref
  81.1 0.6 dynamic_slice.35
  81.7 0.6 dynamic_slice.34
  82.9 8.4 %all-to-all-done.2 = bf16[16,32,576]{2,1,0:T(8,128)(2,1)S(1)} async-done(((bf16[16,32,576]{2,1,0:T(8,128)(2,1)}), bf16[16,32,576]{2,1,0:T(8,128)(2,1)S(1)}, u32[]{:S(2)}, u32[]{:S(2)}) %all-to-all-start.2) | async-done | bytes 589856 | tf_op jit(solution)/shard_map/all_to_all | solution.py:286
  91.2 10.1 %all-gather.2.cloned.1.call-done.rows_ref = bf16[576,2048]{1,0:T(8,128)(2,1)} async-done(((bf16[576,256]{1,0:T(8,128)(2,1)}), bf16[576,2048]{1,0:T(8,128)(2,1)}) %all-gather.2.cloned.1.call-update) | async-done | bytes 2359312 | tf_op jit(solution)/shard_map/all_gather | solution.py:285
  101.3 1.7 %copy-done.1 = bf16[576,2048]{1,0:T(8,128)(2,1)S(1)} copy-done((bf16[576,2048]{1,0:T(8,128)(2,1)S(1)}, bf16[576,2048]{1,0:T(8,128)(2,1)}, u32[]{:S(2)}) %copy-start.1) | copy-done | bytes 2359320
  103.0 3.0 %shard_map.116 = bf16[768,576]{1,0:T(8,128)(2,1)} custom-call(s32[1,384]{1,0:T(1,128)S(1)} %select_n.175.source_ref, s32[768,1]{1,0:T(8,128)S(1)} %reshape.348.order_ref, bf16[576,2048]{1,0:T(8,128)(2,1)S(1)} %copy-done.1), custom_call_target="tpu_custom_call" | custom-call | tf_op jit(solution)/shard_map/pallas_call | solution.py:183
  106.0 7.0 %all-to-all-start.3 = ((bf16[16,48,576]{2,1,0:T(8,128)(2,1)}), bf16[16,48,576]{2,1,0:T(8,128)(2,1)S(1)}, u32[]{:S(2)}, u32[]{:S(2)}) async-start(bf16[16,48,576]{2,1,0:T(8,128)(2,1)} %bitcast.17), calls=%async_computation.3 | async-start | bytes 1966080 | tf_op jit(solution)/shard_map/all_to_all | solution.py:306
  113.0 0.7 fusion.9
  114.1 0.7 dynamic-slice_bitcast_fusion
  114.9 15.5 %all-to-all-done.3 = bf16[16,48,576]{2,1,0:T(8,128)(2,1)S(1)} async-done(((bf16[16,48,576]{2,1,0:T(8,128)(2,1)}), bf16[16,48,576]{2,1,0:T(8,128)(2,1)S(1)}, u32[]{:S(2)}, u32[]{:S(2)}) %all-to-all-start.3) | async-done | bytes 884768 | tf_op jit(solution)/shard_map/all_to_all | solution.py:306
  130.4 2.9 %shard_map.117 = bf16[512,512]{1,0:T(8,128)(2,1)} custom-call(bf16[512,576]{1,0:T(8,128)(2,1)S(1)} %bitcast.55, bf16[768,576]{1,0:T(8,128)(2,1)S(1)} %bitcast.53, bf16[16,576]{1,0:T(8,128)(2,1)S(1)} %pad.5.fresh_ref, s32[1,384]{1,0:T(1,128)S(1)} %reshape.345.live_ref), custom_call_target="tpu_custom_call" | custom-call | tf_op jit(solution)/shard_map/pallas_call | solution.py:219
  133.3 3.6 %all-to-all-start.4 = ((bf16[16,32,512]{2,1,0:T(8,128)(2,1)}), bf16[16,32,512]{2,1,0:T(8,128)(2,1)S(1)}, u32[]{:S(2)}, u32[]{:S(2)}) async-start(bf16[16,32,512]{2,1,0:T(8,128)(2,1)} %bitcast.24), calls=%async_computation.4 | async-start | bytes 1048576 | tf_op jit(solution)/shard_map/all_to_all | solution.py:331
  137.2 1.5 fusion.1
  138.7 8.6 %all-to-all-done.4 = bf16[16,32,512]{2,1,0:T(8,128)(2,1)S(1)} async-done(((bf16[16,32,512]{2,1,0:T(8,128)(2,1)}), bf16[16,32,512]{2,1,0:T(8,128)(2,1)S(1)}, u32[]{:S(2)}, u32[]{:S(2)}) %all-to-all-start.4) | async-done | bytes 524320 | tf_op jit(solution)/shard_map/all_to_all | solution.py:331
  147.3 1.9 %fusion.2 = bf16[1,16,4,8,128]{4,1,2,3,0:T(8,128)(2,1)S(1)} fusion(bf16[8,512,128]{2,1,0:T(8,128)(2,1)} %param.14, bf16[16,4,8,512]{3,2,1,0:T(8,128)(2,1)S(1)} %bitcast.57), kind=kOutput, calls=%fused_computation.6 | convolution fusion | flops 67174400 | bytes 1703936 | tf_op jit(solution)/shard_map/bshl,hlv->bshv/dot_general | solution.py:333
  149.3 0.8 copy.67
  (70 shorter events, 2.8 us)
Async XLA Ops:
  7.2 16.4 %copy-start = (bf16[8,128,512]{2,1,0:T(8,128)(2,1)S(1)}, bf16[8,128,512]{2,1,0:T(8,128)(2,1)}, u32[]{:S(2)}) copy-start(bf16[8,128,512]{2,1,0:T(8,128)(2,1)} %param.13) | copy-start | bytes 3145732
  17.9 5.2 %copy-start.3 = (s32[8,16]{1,0:T(8,128)S(1)}, s32[8,16]{1,0:T(8,128)}, u32[]{:S(2)}) copy-start(s32[8,16]{1,0:T(8,128)} %len_ref.1) | copy-start | bytes 1540
  17.9 5.3 %copy-start.4 = (f32[512]{0:T(512)S(1)}, f32[512]{0:T(512)}, u32[]{:S(2)}) copy-start(f32[512]{0:T(512)} %param.12) | copy-start | bytes 6148
  17.9 5.5 %copy-start.2 = (bf16[1,16,4,8,192]{4,3,2,1,0:T(8,128)(2,1)S(1)}, bf16[1,16,4,8,192]{4,3,2,1,0:T(8,128)(2,1)}, u32[]{:S(2)}) copy-start(bf16[1,16,4,8,192]{4,3,2,1,0:T(8,128)(2,1)} %param.15) | copy-start | bytes 589828
  17.9 35.7 %all-to-all-start = ((bf16[4,4,576,256]{3,2,1,0:T(8,128)(2,1)}), bf16[4,4,576,256]{3,2,1,0:T(8,128)(2,1)}, u32[]{:S(2)}, u32[]{:S(2)}) async-start(bf16[4,4,576,256]{3,2,1,0:T(8,128)(2,1)} %shard_map.113), calls=%async_computation | async-start | bytes 9437184 | tf_op jit(solution)/shard_map/all_to_all | solution.py:263
  57.3 17.0 %all-to-all-start.1 = ((bf16[4,576,256]{2,1,0:T(8,128)(2,1)}), bf16[4,576,256]{2,1,0:T(8,128)(2,1)S(1)}, u32[]{:S(2)}, u32[]{:S(2)}) async-start(bf16[4,576,256]{2,1,0:T(8,128)(2,1)} %shard_map.114), calls=%async_computation.1 | async-start | bytes 2359296 | tf_op jit(solution)/shard_map/all_to_all | solution.py:265
  62.7 12.9 %copy-start.6 = (s32[1,96]{1,0:T(1,128)S(1)}, s32[1,96]{1,0:T(1,128)}, u32[]{:S(2)}) copy-start(s32[1,96]{1,0:T(1,128)} %param.19) | copy-start | bytes 1156
  62.7 13.7 %copy-start.5 = (s32[128]{0:T(128)S(1)}, s32[128]{0:T(128)}, u32[]{:S(2)}) copy-start(s32[128]{0:T(128)} %param.18) | copy-start | bytes 1540
  62.7 38.6 %all-gather.2.cloned.1.call-start = ((), (), s32[]{:S(2)}) async-start(), calls=%async_computation.5 | async-start | bytes 2654208 | tf_op jit(solution)/shard_map/all_gather | solution.py:285
  76.9 14.4 %all-to-all-start.2 = ((bf16[16,32,576]{2,1,0:T(8,128)(2,1)}), bf16[16,32,576]{2,1,0:T(8,128)(2,1)S(1)}, u32[]{:S(2)}, u32[]{:S(2)}) async-start(bf16[16,32,576]{2,1,0:T(8,128)(2,1)} %bitcast.51), calls=%async_computation.2 | async-start | bytes 1310720 | tf_op jit(solution)/shard_map/all_to_all | solution.py:286
  101.3 1.7 %copy-start.1 = (bf16[576,2048]{1,0:T(8,128)(2,1)S(1)}, bf16[576,2048]{1,0:T(8,128)(2,1)}, u32[]{:S(2)}) copy-start(bf16[576,2048]{1,0:T(8,128)(2,1)} %all-gather.2.cloned.1.call-done.rows_ref) | copy-start | bytes 7077892
  106.0 24.4 %all-to-all-start.3 = ((bf16[16,48,576]{2,1,0:T(8,128)(2,1)}), bf16[16,48,576]{2,1,0:T(8,128)(2,1)S(1)}, u32[]{:S(2)}, u32[]{:S(2)}) async-start(bf16[16,48,576]{2,1,0:T(8,128)(2,1)} %bitcast.17), calls=%async_computation.3 | async-start | bytes 1966080 | tf_op jit(solution)/shard_map/all_to_all | solution.py:306
  133.3 14.1 %all-to-all-start.4 = ((bf16[16,32,512]{2,1,0:T(8,128)(2,1)}), bf16[16,32,512]{2,1,0:T(8,128)(2,1)S(1)}, u32[]{:S(2)}, u32[]{:S(2)}) async-start(bf16[16,32,512]{2,1,0:T(8,128)(2,1)} %bitcast.24), calls=%async_computation.4 | async-start | bytes 1048576 | tf_op jit(solution)/shard_map/all_to_all | solution.py:331
Sparse Core Ops, SparseCore 0:
  75.5 25.7 all-gather.1

commit v4 on v3

--- a/solution.py
+++ b/solution.py
@@ -152,50 +152,60 @@
     total = jnp.where(valid, add_up(parts_ref), 0.0)
     latent = total[:LAT]
     scaling = lax.rsqrt(jnp.sum(latent * latent, 0, keepdims=True) / LAT + EPS)
-    out_ref[:LAT] = (latent * scaling * gain_ref[...]).astype(BF)
+    latent = (latent * scaling * gain_ref[...]).astype(BF)
     first, second = total[LAT : LAT + half], total[LAT + half :]
     cosine, sine = cosine_ref[...], sine_ref[...]
-    out_ref[LAT : LAT + half] = (first * cosine - second * sine).astype(BF)
-    out_ref[LAT + half :] = (second * cosine + first * sine).astype(BF)
+    left = (first * cosine - second * sine).astype(BF)
+    right = (second * cosine + first * sine).astype(BF)
+    for copy in range(SIDE):
+        out_ref[copy, :LAT] = latent
+        out_ref[copy, LAT : LAT + half] = left
+        out_ref[copy, LAT + half :] = right
 
 
 def finish(parts, gain, cosine, sine, valid):
     return pl.pallas_call(
         finish_kernel,
-        out_shape=jax.ShapeDtypeStruct((WIDTH, PACK), BF),
+        out_shape=jax.ShapeDtypeStruct((SIDE, WIDTH, PACK), BF),
         compiler_params=pltpu.CompilerParams(vmem_limit_bytes=24 << 20),
     )(parts, gain, cosine, sine, valid)
 
 
-def select_kernel(source_ref, order_ref, rows_ref, out_ref):
-    count = rows_ref.shape[1]
-    row = lax.broadcasted_iota(jnp.int32, (count, TOK), 0)
-    chosen = jnp.where(row == source_ref[...], 1.0, 0.0).astype(BF)
-    mine = jnp.dot(rows_ref[...], chosen, preferred_element_type=F32).astype(BF)
+def select_kernel(source_ref, order_ref, near_ref, far_ref, query_ref, out_ref):
+    row = lax.broadcasted_iota(jnp.int32, (PACK, TOK), 0)
+    mine = jnp.zeros((WIDTH, TOK), F32)
+    for side, rows_ref in enumerate((near_ref, far_ref)):
+        for x in range(SIDE):
+            target = source_ref[side : side + 1, :] - x * PACK
+            chosen = jnp.where(row == target, 1.0, 0.0).astype(BF)
+            mine = mine + jnp.dot(rows_ref[x], chosen, preferred_element_type=F32)
     column = lax.broadcasted_iota(jnp.int32, (2 * TOK, TOK), 1)
     order = jnp.where(column == order_ref[...], 1.0, 0.0).astype(BF)
-    out_ref[...] = lax.dot_general(
-        order, mine, (((1,), (1,)), ((), ())), preferred_element_type=F32
+    picked = lax.dot_general(
+        order, mine.astype(BF), (((1,), (1,)), ((), ())), preferred_element_type=F32
     ).astype(BF)
-
-
-def select(source, order, rows):
+    out_ref[:, : 2 * RUN] = picked.reshape(REQS, 2 * RUN, WIDTH)
+    out_ref[:, 2 * RUN :] = query_ref[...]
+
+
+def select(source, order, near, far, query):
     return pl.pallas_call(
         select_kernel,
-        out_shape=jax.ShapeDtypeStruct((2 * TOK, WIDTH), BF),
+        out_shape=jax.ShapeDtypeStruct((REQS, 2 * RUN + query.shape[1], WIDTH), BF),
         compiler_params=pltpu.CompilerParams(vmem_limit_bytes=40 << 20),
-    )(source, order, rows)
-
-
-def attend_kernel(query_ref, keys_ref, fresh_ref, live_ref, out_ref):
+    )(source, order, near, far, query)
+
+
+def attend_kernel(arrived_ref, fresh_ref, live_ref, out_ref):
     scale = 1.0 / math.sqrt(HDIM + ROPE)
     across = (((1,), (1,)), ((), ()))
     row = lax.broadcasted_iota(jnp.int32, (TOK, 2 * TOK), 0)
     column = lax.broadcasted_iota(jnp.int32, (TOK, 2 * TOK), 1)
     kept = jnp.where(row + RUN * lax.div(row, RUN) == column, 1.0, 0.0).astype(BF)
-    keys = jnp.dot(kept, keys_ref[...], preferred_element_type=F32).astype(BF)
+    rows = arrived_ref[:, : 2 * RUN].reshape(2 * TOK, WIDTH)
+    keys = jnp.dot(kept, rows, preferred_element_type=F32).astype(BF)
     fresh = fresh_ref[...]
-    query = query_ref[...]
+    query = arrived_ref[:, 2 * RUN :].reshape(-1, WIDTH)
     score = lax.dot_general(query, keys, across, preferred_element_type=F32) * scale
     score = jnp.where(live_ref[...] > 0, score, -1e30)
     later = lax.dot_general(query, fresh, across, preferred_element_type=F32) * scale
@@ -215,12 +225,13 @@
     out_ref[...] = mixed.astype(BF)
 
 
-def attend(query, keys, fresh, live):
+def attend(arrived, fresh, live):
+    count = REQS * (arrived.shape[1] - 2 * RUN)
     return pl.pallas_call(
         attend_kernel,
-        out_shape=jax.ShapeDtypeStruct((query.shape[0], LAT), BF),
+        out_shape=jax.ShapeDtypeStruct((count, LAT), BF),
         compiler_params=pltpu.CompilerParams(vmem_limit_bytes=24 << 20),
-    )(query, keys, fresh, live)
+    )(arrived, fresh, live)
 
 
 def pick(index, values):
@@ -281,18 +292,20 @@
     ).astype(BF)
     query_full = jnp.concatenate([absorbed, local_queries[..., HDIM:]], -1)
     query_full = query_full.reshape(REQS, -1, WIDTH)
-    rows, query_full = lax.optimization_barrier((rows, query_full))
-    everything = lax.all_gather(rows, "dec", axis=1, tiled=True)
-    query_full = lax.all_to_all(query_full, "pre", 0, 0, tiled=True)
-    everything, query_full = lax.optimization_barrier((everything, query_full))
+
+    along_x = [[2 * x + core for x in range(SIDE)] for core in range(2)]
+    near = lax.all_to_all(rows, "dec", 0, 0, tiled=True, axis_index_groups=along_x)
+    far = lax.ppermute(near, "dec", [(d, d ^ 1) for d in range(2 * SIDE)])
 
     slots = lax.dynamic_slice_in_dim(assign, dec_rank * REQS, REQS)
-    slot_start = pick(slots, (starts + jnp.arange(starts.shape[0])[:, None] * PACK).reshape(-1))
+    slot_start = pick(slots, (starts + jnp.arange(starts.shape[0])[:, None] // 2 * PACK).reshape(-1))
     slot_count = pick(slots, counts.reshape(-1))
     slot_length = pick(slots, lengths.reshape(-1))
     slot_odd = (slots // REQS) % 2
     run = jnp.arange(RUN, dtype=jnp.int32)
     by_slot = jnp.where(run < slot_count[:, None], slot_start[:, None] + run, -1)
+    is_near = (slot_odd == dec_rank % 2)[:, None]
+    source = jnp.stack([jnp.where(is_near, by_slot, -1), jnp.where(is_near, -1, by_slot)])
     table = block_table[0]
     pages = table.shape[0]
     page = jnp.arange(pages, dtype=jnp.int32)
@@ -302,7 +315,7 @@
     by_page = (owner[:, None] * RUN + piece).reshape(REQS, RUN)
     in_order = jnp.arange(TOK, dtype=jnp.int32).reshape(REQS, RUN)
     order = jnp.concatenate([in_order, by_page], 1).reshape(-1, 1)
-    outgoing = select(by_slot.reshape(1, -1), order, everything).reshape(REQS, 2 * RUN, WIDTH)
+    outgoing = select(source.reshape(2, -1), order, near, far, query_full)
     arrived = lax.all_to_all(outgoing, "pre", 0, 0, tiled=True)
 
     sender = jnp.arange(REQS, dtype=jnp.int32)
@@ -317,8 +330,8 @@
     ).reshape(REQS, RUN)
     target = jnp.concatenate([jnp.full((REQS, RUN), -1, jnp.int32), target], 1).reshape(-1)
     to_place = (jnp.arange(TOK, dtype=jnp.int32)[:, None] == target[None, :]).astype(BF)
-    arrived = arrived.reshape(2 * TOK, WIDTH)
-    cache = jnp.dot(to_place, arrived, preferred_element_type=F32).astype(BF)
+    placed = arrived[:, : 2 * RUN].reshape(2 * TOK, WIDTH)
+    cache = jnp.dot(to_place, placed, preferred_element_type=F32).astype(BF)
 
     own_odd = lax.dynamic_index_in_dim(slot_odd, pre_rank, 0, keepdims=False)
     own_length = lax.dynamic_index_in_dim(slot_length, pre_rank, 0, keepdims=False)
@@ -327,7 +340,7 @@
     live = (key_position < own_length).astype(jnp.int32).reshape(1, TOK)
     fresh = lax.dynamic_index_in_dim(new_keys[0], pre_rank, 0, keepdims=False)
     fresh = jnp.pad(fresh, ((0, 16 - STEPS), (0, 0)))
-    mixed = attend(query_full.reshape(-1, WIDTH), arrived, fresh, live)
+    mixed = attend(arrived, fresh, live)
     mixed = lax.all_to_all(mixed.reshape(REQS, -1, LAT), "pre", 0, 0, tiled=True)
     mixed = mixed.reshape(REQS, STEPS, -1, LAT)
     attended = jnp.einsum("bshl,hlv->bshv", mixed, uv_weight, preferred_element_type=F32).astype(BF)

time: 158 us -> 144 us (0.911)
  between operations: 14.9 us -> 1.68 us
  waiting for transfers between devices: 82.1 us -> 85.8 us
  starting transfers between devices: 24.8 us -> 22.2 us
    all_gather x1 -> x0, waiting for transfers between devices: 10.1 us -> none  [shards(): everything = lax.all_gather(rows, 'dec', axis=1, tiled=True)]
    all_to_all x1, waiting for transfers between devices: 15.5 us -> 21.9 us  [shards(): arrived = lax.all_to_all(outgoing, 'pre', 0, 0, tiled=True)]
    all_to_all x1, waiting for transfers between devices: 8.36 us -> 12.6 us  [shards(): lax.all_to_all(rows, 'dec', 0, 0, tiled=True, axis_index_groups=along_x)]
    all_to_all x1, starting transfers between devices: 6.99 us -> 3.71 us  [shards(): arrived = lax.all_to_all(outgoing, 'pre', 0, 0, tiled=True)]
where the time goes in v4:
time: 144 us; the launch traced here: 143 us
  waiting for transfers between devices  85.8 us (60%)
  starting transfers between devices  22.2 us (15%)
  Pallas kernels  21.9 us (15%)
  local copies, waits for them, and re-layouts  7.05 us (5%)
  matrix products  2.46 us (2%)
  other arithmetic  2.26 us (2%)
  between operations  1.68 us (1%)
    all_to_all x2, waiting for transfers between devices, shards(): lax.all_to_all(packed, both, 0, 0, tiled=True, axis_index_groups=groups_o...  41 us
    all_to_all x1, waiting for transfers between devices, shards(): arrived = lax.all_to_all(outgoing, 'pre', 0, 0, tiled=True)  21.9 us
    all_to_all x1, waiting for transfers between devices, shards(): lax.all_to_all(rows, 'dec', 0, 0, tiled=True, axis_index_groups=along_x)  12.6 us
    pallas_call x1, Pallas kernels, project(): pl.pallas_call(project_kernel, out_shape=jax.ShapeDtypeStruct((SIDE, SIDE...  10.7 us
    all_to_all x2, starting transfers between devices, shards(): lax.all_to_all(packed, both, 0, 0, tiled=True, axis_index_groups=groups_o...  10.5 us
    all_to_all x1, waiting for transfers between devices, shards(): lax.all_to_all(mixed.reshape(REQS, -1, LAT), 'pre', 0, 0, tiled=True)  8.71 us
    all_to_all x1, starting transfers between devices, shards(): lax.all_to_all(rows, 'dec', 0, 0, tiled=True, axis_index_groups=along_x)  4.42 us
    all_to_all x1, starting transfers between devices, shards(): arrived = lax.all_to_all(outgoing, 'pre', 0, 0, tiled=True)  3.71 us
  transfers between devices with their start and end apart: 6, of which 6 were waited for; matrix products, arithmetic and copies ran while one was open for 6% of the time, Pallas kernels for 0%

profile of v4, /device:TPU:0, one launch (start us, length us, event | category | flops | bytes accessed | tf_op | source)
XLA Modules:
  0.0 143.4 jit_solution(10199130744435362284)
XLA Ops:
  0.6 10.7 %shard_map.113 = bf16[4,4,576,256]{3,2,1,0:T(8,128)(2,1)} custom-call(s32[8,16]{1,0:T(8,128)} %len_ref.1, bf16[448,6144]{1,0:T(8,128)(2,1)} %bitcast.67, bf16[448,576]{1,0:T(8,128)(2,1)} %down_ref.1), custom_call_target="tpu_custom_call" | custom-call | flops 3170893824 | bytes 11534336 | tf_op jit(solution)/shard_map/pallas_call | solution.py:92
  11.4 5.1 %all-to-all-start = ((bf16[4,4,576,256]{3,2,1,0:T(8,128)(2,1)}), bf16[4,4,576,256]{3,2,1,0:T(8,128)(2,1)}, u32[]{:S(2)}, u32[]{:S(2)}) async-start(bf16[4,4,576,256]{3,2,1,0:T(8,128)(2,1)} %shard_map.113), calls=%async_computation | async-start | bytes 9437184 | tf_op jit(solution)/shard_map/all_to_all | solution.py:274
  16.5 0.2 reduce_window_sum.11
  16.8 0.2 copy.63.gain_ref
  17.3 29.8 %all-to-all-done.parts_ref = bf16[4,4,576,256]{3,2,1,0:T(8,128)(2,1)} async-done(((bf16[4,4,576,256]{3,2,1,0:T(8,128)(2,1)}), bf16[4,4,576,256]{3,2,1,0:T(8,128)(2,1)}, u32[]{:S(2)}, u32[]{:S(2)}) %all-to-all-start) | async-done | bytes 4718624 | tf_op jit(solution)/shard_map/all_to_all | solution.py:274
  47.1 3.7 %shard_map.114 = bf16[4,576,256]{2,1,0:T(8,128)(2,1)} custom-call(bf16[4,4,576,256]{3,2,1,0:T(8,128)(2,1)} %all-to-all-done.parts_ref), custom_call_target="tpu_custom_call" | custom-call | tf_op jit(solution)/shard_map/pallas_call | solution.py:136
  50.7 5.4 %all-to-all-start.1 = ((bf16[4,576,256]{2,1,0:T(8,128)(2,1)}), bf16[4,576,256]{2,1,0:T(8,128)(2,1)S(1)}, u32[]{:S(2)}, u32[]{:S(2)}) async-start(bf16[4,576,256]{2,1,0:T(8,128)(2,1)} %shard_map.114), calls=%async_computation.1 | async-start | bytes 2359296 | tf_op jit(solution)/shard_map/all_to_all | solution.py:276
  56.3 0.2 multiply_sine_fusion
  56.5 11.3 %all-to-all-done.1.parts_ref = bf16[4,576,256]{2,1,0:T(8,128)(2,1)S(1)} async-done(((bf16[4,576,256]{2,1,0:T(8,128)(2,1)}), bf16[4,576,256]{2,1,0:T(8,128)(2,1)S(1)}, u32[]{:S(2)}, u32[]{:S(2)}) %all-to-all-start.1) | async-done | bytes 1179680 | tf_op jit(solution)/shard_map/all_to_all | solution.py:276
  67.7 1.4 shard_map.115
  69.1 4.4 %all-to-all-start.2 = ((bf16[4,576,256]{2,1,0:T(8,128)(2,1)}), bf16[4,576,256]{2,1,0:T(8,128)(2,1)S(1)}, u32[]{:S(2)}, u32[]{:S(2)}) async-start(bf16[4,576,256]{2,1,0:T(8,128)(2,1)} %shard_map.115), calls=%async_computation.2 | async-start | bytes 2359296 | tf_op jit(solution)/shard_map/all_to_all | solution.py:297
  73.6 0.2 select_reduce_fusion.3
  75.2 12.6 %all-to-all-done.2.near_ref = bf16[4,576,256]{2,1,0:T(8,128)(2,1)S(1)} async-done(((bf16[4,576,256]{2,1,0:T(8,128)(2,1)}), bf16[4,576,256]{2,1,0:T(8,128)(2,1)S(1)}, u32[]{:S(2)}, u32[]{:S(2)}) %all-to-all-start.2) | async-done | bytes 1179680 | tf_op jit(solution)/shard_map/all_to_all | solution.py:297
  88.0 0.2 reshape.446.order_ref
  88.2 0.2 copy.77
  88.4 0.3 fusion
  88.8 0.4 copy.76
  89.2 1.6 %collective-permute-done.far_ref = bf16[4,576,256]{2,1,0:T(8,128)(2,1)} collective-permute-done((bf16[4,576,256]{2,1,0:T(8,128)(2,1)S(1)}, bf16[4,576,256]{2,1,0:T(8,128)(2,1)}, u32[]{:S(2)}, u32[]{:S(2)}) %collective-permute-start) | collective-permute-done | bytes 1179680 | tf_op jit(solution)/shard_map/ppermute | solution.py:298
  90.7 3.3 %shard_map.116 = bf16[16,80,576]{2,1,0:T(8,128)(2,1)S(1)} custom-call(s32[2,384]{1,0:T(2,128)S(1)} %pad_add_fusion.1.source_ref, s32[768,1]{1,0:T(8,128)S(1)} %reshape.446.order_ref, bf16[4,576,256]{2,1,0:T(8,128)(2,1)S(1)} %all-to-all-done.2.near_ref, bf16[4,576,256]{2,1,0:T(8,128)(2,1)} %collective-permute-done.far_ref, bf16[16,32,576]{2,1,0:T(8,128)(2,1)S(1)} %bitcast.57), custom_call_target="tpu_custom_call" | custom-call | tf_op jit(solution)/shard_map/pallas_call | solution.py:192
  94.1 1.2 copy-done.1
  95.2 3.7 %all-to-all-start.3 = ((bf16[16,80,576]{2,1,0:T(8,128)(2,1)}), bf16[16,80,576]{2,1,0:T(8,128)(2,1)S(1)}, u32[]{:S(2)}, u32[]{:S(2)}) async-start(bf16[16,80,576]{2,1,0:T(8,128)(2,1)} %copy-done.1), calls=%async_computation.3 | async-start | bytes 3276800 | tf_op jit(solution)/shard_map/all_to_all | solution.py:319
  99.1 0.6 dynamic_slice.34
  99.9 0.6 dynamic_slice.35
  101.2 0.7 fusion.9
  102.0 0.7 dynamic-slice_bitcast_fusion
  102.8 21.9 %all-to-all-done.3.arrived_ref = bf16[16,80,576]{2,1,0:T(8,128)(2,1)S(1)} async-done(((bf16[16,80,576]{2,1,0:T(8,128)(2,1)}), bf16[16,80,576]{2,1,0:T(8,128)(2,1)S(1)}, u32[]{:S(2)}, u32[]{:S(2)}) %all-to-all-start.3) | async-done | bytes 1474592 | tf_op jit(solution)/shard_map/all_to_all | solution.py:319
  124.7 2.9 %shard_map.117 = bf16[512,512]{1,0:T(8,128)(2,1)} custom-call(bf16[16,80,576]{2,1,0:T(8,128)(2,1)S(1)} %all-to-all-done.3.arrived_ref, bf16[16,576]{1,0:T(8,128)(2,1)S(1)} %pad.5.fresh_ref, s32[1,384]{1,0:T(1,128)S(1)} %reshape.443.live_ref), custom_call_target="tpu_custom_call" | custom-call | tf_op jit(solution)/shard_map/pallas_call | solution.py:230
  127.6 3.6 %all-to-all-start.4 = ((bf16[16,32,512]{2,1,0:T(8,128)(2,1)}), bf16[16,32,512]{2,1,0:T(8,128)(2,1)S(1)}, u32[]{:S(2)}, u32[]{:S(2)}) async-start(bf16[16,32,512]{2,1,0:T(8,128)(2,1)} %bitcast.22), calls=%async_computation.4 | async-start | bytes 1048576 | tf_op jit(solution)/shard_map/all_to_all | solution.py:344
  131.7 1.4 %fusion.1 = bf16[1,384,576]{1,2,0:T(8,128)(2,1)} fusion(bf16[768,576]{1,0:T(8,128)(2,1)S(1)} %bitcast.60, s32[768]{0:T(1024)S(1)} %eq.106), kind=kOutput, calls=%fused_computation.3 | convolution fusion | flops 340254720 | bytes 1330176 | tf_op jit(solution)/shard_map/dot_general | solution.py:334
  133.2 8.7 %all-to-all-done.4 = bf16[16,32,512]{2,1,0:T(8,128)(2,1)S(1)} async-done(((bf16[16,32,512]{2,1,0:T(8,128)(2,1)}), bf16[16,32,512]{2,1,0:T(8,128)(2,1)S(1)}, u32[]{:S(2)}, u32[]{:S(2)}) %all-to-all-start.4) | async-done | bytes 524320 | tf_op jit(solution)/shard_map/all_to_all | solution.py:344
  141.9 0.7 fusion.2
  142.6 0.8 copy.68
  (80 shorter events, 3.3 us)
Async XLA Ops:
  0.6 87.8 %copy-start = (bf16[8,128,512]{2,1,0:T(8,128)(2,1)S(1)}, bf16[8,128,512]{2,1,0:T(8,128)(2,1)}, u32[]{:S(2)}) copy-start(bf16[8,128,512]{2,1,0:T(8,128)(2,1)} %param.13) | copy-start | bytes 3145732
  11.3 5.1 %copy-start.4 = (s32[8,16]{1,0:T(8,128)S(1)}, s32[8,16]{1,0:T(8,128)}, u32[]{:S(2)}) copy-start(s32[8,16]{1,0:T(8,128)} %len_ref.1) | copy-start | bytes 1540
  11.3 5.5 %copy-start.5 = (f32[512]{0:T(512)S(1)}, f32[512]{0:T(512)}, u32[]{:S(2)}) copy-start(f32[512]{0:T(512)} %param.12) | copy-start | bytes 6148
  11.3 5.8 %copy-start.6 = (s32[128]{0:T(128)S(1)}, s32[128]{0:T(128)}, u32[]{:S(2)}) copy-start(s32[128]{0:T(128)} %param.18) | copy-start | bytes 1540
  11.4 35.7 %all-to-all-start = ((bf16[4,4,576,256]{3,2,1,0:T(8,128)(2,1)}), bf16[4,4,576,256]{3,2,1,0:T(8,128)(2,1)}, u32[]{:S(2)}, u32[]{:S(2)}) async-start(bf16[4,4,576,256]{3,2,1,0:T(8,128)(2,1)} %shard_map.113), calls=%async_computation | async-start | bytes 9437184 | tf_op jit(solution)/shard_map/all_to_all | solution.py:274
  50.7 17.0 %all-to-all-start.1 = ((bf16[4,576,256]{2,1,0:T(8,128)(2,1)}), bf16[4,576,256]{2,1,0:T(8,128)(2,1)S(1)}, u32[]{:S(2)}, u32[]{:S(2)}) async-start(bf16[4,576,256]{2,1,0:T(8,128)(2,1)} %shard_map.114), calls=%async_computation.1 | async-start | bytes 2359296 | tf_op jit(solution)/shard_map/all_to_all | solution.py:276
  69.1 5.3 %copy-start.7 = (s32[1,96]{1,0:T(1,128)S(1)}, s32[1,96]{1,0:T(1,128)}, u32[]{:S(2)}) copy-start(s32[1,96]{1,0:T(1,128)} %param.19) | copy-start | bytes 1156
  69.1 19.1 %copy-start.3 = (bf16[1,16,4,8,192]{4,3,2,1,0:T(8,128)(2,1)S(1)}, bf16[1,16,4,8,192]{4,3,2,1,0:T(8,128)(2,1)}, u32[]{:S(2)}) copy-start(bf16[1,16,4,8,192]{4,3,2,1,0:T(8,128)(2,1)} %param.15) | copy-start | bytes 589828
  69.1 18.6 %all-to-all-start.2 = ((bf16[4,576,256]{2,1,0:T(8,128)(2,1)}), bf16[4,576,256]{2,1,0:T(8,128)(2,1)S(1)}, u32[]{:S(2)}, u32[]{:S(2)}) async-start(bf16[4,576,256]{2,1,0:T(8,128)(2,1)} %shard_map.115), calls=%async_computation.2 | async-start | bytes 2359296 | tf_op jit(solution)/shard_map/all_to_all | solution.py:297
  87.8 3.0 %collective-permute-start = (bf16[4,576,256]{2,1,0:T(8,128)(2,1)S(1)}, bf16[4,576,256]{2,1,0:T(8,128)(2,1)}, u32[]{:S(2)}, u32[]{:S(2)}) collective-permute-start(bf16[4,576,256]{2,1,0:T(8,128)(2,1)S(1)} %all-to-all-done.2.near_ref), channel_id=1, source_target_pairs={{0,1},{1,0},{2,3},{3,2},{4,5},{5,4},{6,7},{7,6},{8,9},{9,8},{10,11... | collective-permute-start | bytes 3538952 | tf_op jit(solution)/shard_map/ppermute | solution.py:298
  94.0 1.2 copy-start.1
  95.2 29.5 %all-to-all-start.3 = ((bf16[16,80,576]{2,1,0:T(8,128)(2,1)}), bf16[16,80,576]{2,1,0:T(8,128)(2,1)S(1)}, u32[]{:S(2)}, u32[]{:S(2)}) async-start(bf16[16,80,576]{2,1,0:T(8,128)(2,1)} %copy-done.1), calls=%async_computation.3 | async-start | bytes 3276800 | tf_op jit(solution)/shard_map/all_to_all | solution.py:319
  127.6 14.3 %all-to-all-start.4 = ((bf16[16,32,512]{2,1,0:T(8,128)(2,1)}), bf16[16,32,512]{2,1,0:T(8,128)(2,1)S(1)}, u32[]{:S(2)}, u32[]{:S(2)}) async-start(bf16[16,32,512]{2,1,0:T(8,128)(2,1)} %bitcast.22), calls=%async_computation.4 | async-start | bytes 1048576 | tf_op jit(solution)/shard_map/all_to_all | solution.py:344
  131.7 10.2 %copy-start.2 = (bf16[8,512,128]{2,1,0:T(8,128)(2,1)S(1)}, bf16[8,512,128]{2,1,0:T(8,128)(2,1)}, u32[]{:S(2)}) copy-start(bf16[8,512,128]{2,1,0:T(8,128)(2,1)} %param.14) | copy-start | bytes 3145732

commit v5 on v4

--- a/solution.py
+++ b/solution.py
@@ -27,6 +27,14 @@
 EPS = 1e-06
 BF = jnp.bfloat16
 F32 = jnp.float32
+
+
+def halfway(k):
+    return (k + SIDE // 2) % SIDE
+
+
+def turned(rank):
+    return halfway(rank // SIDE) * SIDE + halfway(rank % SIDE)
 
 
 def project_kernel(
@@ -121,28 +129,37 @@
     return total
 
 
-def first_sum_kernel(parts_ref, out_ref, sent_ref, out_sem):
+def first_sum_kernel(parts_ref, out_ref, held_ref, sent_ref, in_sem, out_sem):
+    def load(part):
+        return pltpu.make_async_copy(parts_ref.at[:, part], held_ref.at[part], in_sem.at[part])
+
     def store(part):
         return pltpu.make_async_copy(sent_ref.at[part], out_ref.at[part], out_sem.at[part])
 
     for part in range(SIDE):
-        sent_ref[part] = add_up(parts_ref[:, part]).astype(BF)
+        load(part).start()
+    for part in range(SIDE):
+        load(part).wait()
+        sent_ref[part] = add_up(held_ref.at[part]).astype(BF)
         store(part).start()
     for part in range(SIDE):
         store(part).wait()
 
 
 def first_sum(parts):
+    whole = pl.BlockSpec(memory_space=pl.ANY)
     return pl.pallas_call(
         first_sum_kernel,
         out_shape=jax.ShapeDtypeStruct((SIDE, WIDTH, PACK), BF),
-        in_specs=[pl.BlockSpec(memory_space=pltpu.VMEM)],
-        out_specs=pl.BlockSpec(memory_space=pl.ANY),
+        in_specs=[whole],
+        out_specs=whole,
         scratch_shapes=[
+            pltpu.VMEM((SIDE, SIDE, WIDTH, PACK), BF),
             pltpu.VMEM((SIDE, WIDTH, PACK), BF),
             pltpu.SemaphoreType.DMA((SIDE,)),
+            pltpu.SemaphoreType.DMA((SIDE,)),
         ],
-        compiler_params=pltpu.CompilerParams(vmem_limit_bytes=16 << 20),
+        compiler_params=pltpu.CompilerParams(vmem_limit_bytes=60 << 20),
     )(parts)
 
 
@@ -171,7 +188,22 @@
     )(parts, gain, cosine, sine, valid)
 
 
-def select_kernel(source_ref, order_ref, near_ref, far_ref, query_ref, out_ref):
+def select_kernel(
+    source_ref, order_ref, near_ref, far_ref, query_ref, out_ref, sent_ref, query_sem, out_sem
+):
+    half = REQS // 2
+    held = sent_ref.shape[1]
+
+    def ask(pair):
+        begin, source = 2 * pair, turned(2 * pair)
+        return pltpu.make_async_copy(
+            query_ref.at[pl.ds(source, 2)],
+            out_ref.at[pl.ds(begin, 2), pl.ds(held, query_ref.shape[1])],
+            query_sem.at[pair],
+        )
+
+    for pair in range(half):
+        ask(pair).start()
     row = lax.broadcasted_iota(jnp.int32, (PACK, TOK), 0)
     mine = jnp.zeros((WIDTH, TOK), F32)
     for side, rows_ref in enumerate((near_ref, far_ref)):
@@ -179,19 +211,40 @@
             target = source_ref[side : side + 1, :] - x * PACK
             chosen = jnp.where(row == target, 1.0, 0.0).astype(BF)
             mine = mine + jnp.dot(rows_ref[x], chosen, preferred_element_type=F32)
-    column = lax.broadcasted_iota(jnp.int32, (2 * TOK, TOK), 1)
-    order = jnp.where(column == order_ref[...], 1.0, 0.0).astype(BF)
-    picked = lax.dot_general(
-        order, mine.astype(BF), (((1,), (1,)), ((), ())), preferred_element_type=F32
-    ).astype(BF)
-    out_ref[:, : 2 * RUN] = picked.reshape(REQS, 2 * RUN, WIDTH)
-    out_ref[:, 2 * RUN :] = query_ref[...]
+    mine = mine.astype(BF)
+    column = lax.broadcasted_iota(jnp.int32, (TOK, TOK), 1)
+
+    def store(part):
+        where = pl.ds(part * half, half)
+        return pltpu.make_async_copy(
+            sent_ref.at[where], out_ref.at[where, pl.ds(0, held)], out_sem.at[part]
+        )
+
+    for part in range(2):
+        order = jnp.where(column == order_ref[part * TOK : (part + 1) * TOK, :], 1.0, 0.0)
+        picked = lax.dot_general(
+            order.astype(BF), mine, (((1,), (1,)), ((), ())), preferred_element_type=F32
+        ).astype(BF)
+        sent_ref[part * half : (part + 1) * half] = picked.reshape(half, held, WIDTH)
+        store(part).start()
+    for pair in range(half):
+        ask(pair).wait()
+    for part in range(2):
+        store(part).wait()
 
 
 def select(source, order, near, far, query):
+    vmem = pl.BlockSpec(memory_space=pltpu.VMEM)
     return pl.pallas_call(
         select_kernel,
         out_shape=jax.ShapeDtypeStruct((REQS, 2 * RUN + query.shape[1], WIDTH), BF),
+        in_specs=[vmem] * 5,
+        out_specs=pl.BlockSpec(memory_space=pl.ANY),
+        scratch_shapes=[
+            pltpu.VMEM((REQS, 2 * RUN, WIDTH), BF),
+            pltpu.SemaphoreType.DMA((REQS // 2,)),
+            pltpu.SemaphoreType.DMA((2,)),
+        ],
         compiler_params=pltpu.CompilerParams(vmem_limit_bytes=40 << 20),
     )(source, order, near, far, query)
 
@@ -222,7 +275,11 @@
     later = (later * inverse).astype(BF)
     mixed = jnp.dot(score, keys[:, :LAT], preferred_element_type=F32)
     mixed = mixed + jnp.dot(later, fresh[:, :LAT], preferred_element_type=F32)
-    out_ref[...] = mixed.astype(BF)
+    mixed = mixed.astype(BF)
+    share = 2 * (arrived_ref.shape[1] - 2 * RUN)
+    for pair in range(REQS // 2):
+        begin = turned(2 * pair) * share // 2
+        out_ref[begin : begin + share] = mixed[pair * share : (pair + 1) * share]
 
 
 def attend(arrived, fresh, live):
@@ -245,7 +302,8 @@
         for x in range(SIDE):
             for other in range(SIDE):
                 ring = []
-                for k in range(SIDE):
+                for place in range(SIDE):
+                    k = halfway(place)
                     y, z = (k, other) if core == first else (other, k)
                     ring.append(((y * SIDE + z) * SIDE + x) * 2 + core)
                 found.append(ring)
@@ -258,9 +316,11 @@
     pre_rank = lax.axis_index("pre")
     dec_rank = lax.axis_index("dec")
     both = ("pre", "dec")
-    side_y, side_z = pre_rank // SIDE, pre_rank % SIDE
-    swapped = side_z * SIDE + side_y
-    residue = jnp.where(dec_rank % 2 == 0, pre_rank, swapped)
+    all_pre = [[turned(rank) for rank in range(REQS)]]
+    side_y, side_z = halfway(pre_rank // SIDE), halfway(pre_rank % SIDE)
+    residue = jnp.where(
+        dec_rank % 2 == 0, side_y * SIDE + side_z, side_z * SIDE + side_y
+    )
 
     counts = (lengths + (REQS - 1)) // REQS
     ends = jnp.cumsum(counts, 1)
@@ -293,12 +353,13 @@
     query_full = jnp.concatenate([absorbed, local_queries[..., HDIM:]], -1)
     query_full = query_full.reshape(REQS, -1, WIDTH)
 
-    along_x = [[2 * x + core for x in range(SIDE)] for core in range(2)]
+    along_x = [[2 * halfway(x) + core for x in range(SIDE)] for core in range(2)]
     near = lax.all_to_all(rows, "dec", 0, 0, tiled=True, axis_index_groups=along_x)
     far = lax.ppermute(near, "dec", [(d, d ^ 1) for d in range(2 * SIDE)])
 
     slots = lax.dynamic_slice_in_dim(assign, dec_rank * REQS, REQS)
-    slot_start = pick(slots, (starts + jnp.arange(starts.shape[0])[:, None] // 2 * PACK).reshape(-1))
+    column = halfway(jnp.arange(starts.shape[0], dtype=jnp.int32)[:, None] // 2)
+    slot_start = pick(slots, (starts + column * PACK).reshape(-1))
     slot_count = pick(slots, counts.reshape(-1))
     slot_length = pick(slots, lengths.reshape(-1))
     slot_odd = (slots // REQS) % 2
@@ -314,9 +375,11 @@
     piece = part[:, None] * (RUN // NPG) + jnp.arange(RUN // NPG, dtype=jnp.int32)
     by_page = (owner[:, None] * RUN + piece).reshape(REQS, RUN)
     in_order = jnp.arange(TOK, dtype=jnp.int32).reshape(REQS, RUN)
-    order = jnp.concatenate([in_order, by_page], 1).reshape(-1, 1)
+    order = jnp.concatenate([in_order, by_page], 1)
+    order = order.reshape(SIDE, SIDE, -1)
+    order = jnp.roll(order, (SIDE // 2, SIDE // 2), (0, 1)).reshape(-1, 1)
     outgoing = select(source.reshape(2, -1), order, near, far, query_full)
-    arrived = lax.all_to_all(outgoing, "pre", 0, 0, tiled=True)
+    arrived = lax.all_to_all(outgoing, "pre", 0, 0, tiled=True, axis_index_groups=all_pre)
 
     sender = jnp.arange(REQS, dtype=jnp.int32)
     sender_swapped = (sender % SIDE) * SIDE + sender // SIDE
@@ -341,7 +404,8 @@
     fresh = lax.dynamic_index_in_dim(new_keys[0], pre_rank, 0, keepdims=False)
     fresh = jnp.pad(fresh, ((0, 16 - STEPS), (0, 0)))
     mixed = attend(arrived, fresh, live)
-    mixed = lax.all_to_all(mixed.reshape(REQS, -1, LAT), "pre", 0, 0, tiled=True)
+    mixed = mixed.reshape(REQS, -1, LAT)
+    mixed = lax.all_to_all(mixed, "pre", 0, 0, tiled=True)
     mixed = mixed.reshape(REQS, STEPS, -1, LAT)
     attended = jnp.einsum("bshl,hlv->bshv", mixed, uv_weight, preferred_element_type=F32).astype(BF)
     return (cache[None], attended[None])

time: 144 us -> 145 us (level)
  starting transfers between devices: 22.2 us -> 36.1 us
  waiting for transfers between devices: 85.8 us -> 72.2 us
    all_to_all x2, waiting for transfers between devices: 41 us -> 34.2 us  [shards(): lax.all_to_all(packed, both, 0, 0, tiled=True, axis_index_groups=groups_o...]
    all_to_all x2, starting transfers between devices: 7.31 us -> 13.8 us  [the longest x1 9.09 us: shards(): lax.all_to_all(outgoing, 'pre', 0, 0, tiled=True, axis_index_groups=all_pre)]
    all_to_all x2, waiting for transfers between devices: 30.6 us -> 25.2 us  [the longest x1 16.9 us: shards(): lax.all_to_all(outgoing, 'pre', 0, 0, tiled=True, axis_index_groups=all_pre)]
    all_to_all x2, starting transfers between devices: 10.5 us -> 15.7 us  [shards(): lax.all_to_all(packed, both, 0, 0, tiled=True, axis_index_groups=groups_o...]
    all_to_all x1, starting transfers between devices: 4.42 us -> 6.65 us  [shards(): lax.all_to_all(rows, 'dec', 0, 0, tiled=True, axis_index_groups=along_x)]
    all_to_all x1, waiting for transfers between devices: 12.6 us -> 11.1 us  [shards(): lax.all_to_all(rows, 'dec', 0, 0, tiled=True, axis_index_groups=along_x)]
where the time goes in v5:
time: 145 us; the launch traced here: 144 us
  waiting for transfers between devices  72.2 us (50%)
  starting transfers between devices  36.1 us (25%)
  Pallas kernels  22.3 us (15%)
  local copies, waits for them, and re-layouts  7.01 us (5%)
  matrix products  2.46 us (2%)
  other arithmetic  2.24 us (2%)
  between operations  1.66 us (1%)
    all_to_all x2, waiting for transfers between devices, shards(): lax.all_to_all(packed, both, 0, 0, tiled=True, axis_index_groups=groups_o...  34.2 us
    all_to_all x1, waiting for transfers between devices, shards(): lax.all_to_all(outgoing, 'pre', 0, 0, tiled=True, axis_index_groups=all_pre)  16.9 us
    all_to_all x2, starting transfers between devices, shards(): lax.all_to_all(packed, both, 0, 0, tiled=True, axis_index_groups=groups_o...  15.7 us
    all_to_all x1, waiting for transfers between devices, shards(): lax.all_to_all(rows, 'dec', 0, 0, tiled=True, axis_index_groups=along_x)  11.1 us
    pallas_call x1, Pallas kernels, project(): pl.pallas_call(project_kernel, out_shape=jax.ShapeDtypeStruct((SIDE, SIDE...  10.7 us
    all_to_all x1, starting transfers between devices, shards(): lax.all_to_all(outgoing, 'pre', 0, 0, tiled=True, axis_index_groups=all_pre)  9.09 us
    all_to_all x1, waiting for transfers between devices, shards(): mixed = lax.all_to_all(mixed, 'pre', 0, 0, tiled=True)  8.31 us
    all_to_all x1, starting transfers between devices, shards(): lax.all_to_all(rows, 'dec', 0, 0, tiled=True, axis_index_groups=along_x)  6.65 us
  transfers between devices with their start and end apart: 6, of which 6 were waited for; matrix products, arithmetic and copies ran while one was open for 6% of the time, Pallas kernels for 0%

profile of v5, /device:TPU:0, one launch (start us, length us, event | category | flops | bytes accessed | tf_op | source)
XLA Modules:
  0.0 144.1 jit_solution(12179392709938030214)
XLA Ops:
  0.6 10.7 %shard_map.113 = bf16[4,4,576,256]{3,2,1,0:T(8,128)(2,1)} custom-call(s32[8,16]{1,0:T(8,128)} %len_ref.1, bf16[448,6144]{1,0:T(8,128)(2,1)} %bitcast.71, bf16[448,576]{1,0:T(8,128)(2,1)} %down_ref.1), custom_call_target="tpu_custom_call" | custom-call | flops 3170893824 | bytes 11534336 | tf_op jit(solution)/shard_map/pallas_call | solution.py:100
  11.4 8.3 %all-to-all-start = ((bf16[4,4,576,256]{3,2,1,0:T(8,128)(2,1)}), bf16[4,4,576,256]{3,2,1,0:T(8,128)(2,1)}, u32[]{:S(2)}, u32[]{:S(2)}) async-start(bf16[4,4,576,256]{3,2,1,0:T(8,128)(2,1)} %shard_map.113), calls=%async_computation | async-start | bytes 9437184 | tf_op jit(solution)/shard_map/all_to_all | solution.py:334
  19.7 0.2 reduce_window_sum.11
  20.0 0.2 copy.65.gain_ref
  20.4 0.2 select_reduce_fusion.3
  21.4 25.9 %all-to-all-done.parts_ref = bf16[4,4,576,256]{3,2,1,0:T(8,128)(2,1)} async-done(((bf16[4,4,576,256]{3,2,1,0:T(8,128)(2,1)}), bf16[4,4,576,256]{3,2,1,0:T(8,128)(2,1)}, u32[]{:S(2)}, u32[]{:S(2)}) %all-to-all-start) | async-done | bytes 4718624 | tf_op jit(solution)/shard_map/all_to_all | solution.py:334
  47.4 3.3 %shard_map.114 = bf16[4,576,256]{2,1,0:T(8,128)(2,1)} custom-call(bf16[4,4,576,256]{3,2,1,0:T(8,128)(2,1)} %all-to-all-done.parts_ref), custom_call_target="tpu_custom_call" | custom-call | tf_op jit(solution)/shard_map/pallas_call | solution.py:151
  50.6 7.4 %all-to-all-start.1 = ((bf16[4,576,256]{2,1,0:T(8,128)(2,1)}), bf16[4,576,256]{2,1,0:T(8,128)(2,1)S(1)}, u32[]{:S(2)}, u32[]{:S(2)}) async-start(bf16[4,576,256]{2,1,0:T(8,128)(2,1)} %shard_map.114), calls=%async_computation.1 | async-start | bytes 2359296 | tf_op jit(solution)/shard_map/all_to_all | solution.py:336
  58.2 0.2 multiply_sine_fusion
  58.4 8.3 %all-to-all-done.1.parts_ref = bf16[4,576,256]{2,1,0:T(8,128)(2,1)S(1)} async-done(((bf16[4,576,256]{2,1,0:T(8,128)(2,1)}), bf16[4,576,256]{2,1,0:T(8,128)(2,1)S(1)}, u32[]{:S(2)}, u32[]{:S(2)}) %all-to-all-start.1) | async-done | bytes 1179680 | tf_op jit(solution)/shard_map/all_to_all | solution.py:336
  66.7 1.4 shard_map.115
  68.1 6.6 %all-to-all-start.2 = ((bf16[4,576,256]{2,1,0:T(8,128)(2,1)}), bf16[4,576,256]{2,1,0:T(8,128)(2,1)S(1)}, u32[]{:S(2)}, u32[]{:S(2)}) async-start(bf16[4,576,256]{2,1,0:T(8,128)(2,1)} %shard_map.115), calls=%async_computation.2 | async-start | bytes 2359296 | tf_op jit(solution)/shard_map/all_to_all | solution.py:357
  75.6 11.1 %all-to-all-done.2.near_ref = bf16[4,576,256]{2,1,0:T(8,128)(2,1)S(1)} async-done(((bf16[4,576,256]{2,1,0:T(8,128)(2,1)}), bf16[4,576,256]{2,1,0:T(8,128)(2,1)S(1)}, u32[]{:S(2)}, u32[]{:S(2)}) %all-to-all-start.2) | async-done | bytes 1179680 | tf_op jit(solution)/shard_map/all_to_all | solution.py:357
  86.8 0.2 reshape.468.order_ref
  87.0 0.2 copy.79
  87.2 0.3 fusion
  87.6 0.4 copy.78
  88.0 1.7 %collective-permute-done.far_ref = bf16[4,576,256]{2,1,0:T(8,128)(2,1)} collective-permute-done((bf16[4,576,256]{2,1,0:T(8,128)(2,1)S(1)}, bf16[4,576,256]{2,1,0:T(8,128)(2,1)}, u32[]{:S(2)}, u32[]{:S(2)}) %collective-permute-start) | collective-permute-done | bytes 1179680 | tf_op jit(solution)/shard_map/ppermute | solution.py:358
  89.7 4.1 %shard_map.116 = bf16[16,80,576]{2,1,0:T(8,128)(2,1)S(1)} custom-call(s32[2,384]{1,0:T(2,128)S(1)} %pad_add_fusion.3.source_ref, s32[768,1]{1,0:T(8,128)S(1)} %reshape.468.order_ref, bf16[4,576,256]{2,1,0:T(8,128)(2,1)S(1)} %all-to-all-done.2.near_ref, bf16[4,576,256]{2,1,0:T(8,128)(2,1)} %collective-permute-done.far_ref, bf16[16,32,576]{2,1,0:T(8,128)(2,1)S(1)} %bitcast.59), custom_call_target="tpu_custom_call" | custom-call | tf_op jit(solution)/shard_map/pallas_call | solution.py:238
  93.8 1.2 copy-done.1
  95.0 9.1 %all-to-all-start.3 = ((bf16[16,80,576]{2,1,0:T(8,128)(2,1)}), bf16[16,80,576]{2,1,0:T(8,128)(2,1)S(1)}, u32[]{:S(2)}, u32[]{:S(2)}) async-start(bf16[16,80,576]{2,1,0:T(8,128)(2,1)} %copy-done.1), calls=%async_computation.3 | async-start | bytes 3276800 | tf_op jit(solution)/shard_map/all_to_all | solution.py:382
  104.2 0.6 dynamic_slice.34
  105.0 0.6 dynamic_slice.35
  106.3 0.7 fusion.9
  107.1 0.7 dynamic-slice_bitcast_fusion
  107.9 16.9 %all-to-all-done.3.arrived_ref = bf16[16,80,576]{2,1,0:T(8,128)(2,1)S(1)} async-done(((bf16[16,80,576]{2,1,0:T(8,128)(2,1)}), bf16[16,80,576]{2,1,0:T(8,128)(2,1)S(1)}, u32[]{:S(2)}, u32[]{:S(2)}) %all-to-all-start.3) | async-done | bytes 1474592 | tf_op jit(solution)/shard_map/all_to_all | solution.py:382
  124.8 2.8 %shard_map.117 = bf16[512,512]{1,0:T(8,128)(2,1)} custom-call(bf16[16,80,576]{2,1,0:T(8,128)(2,1)S(1)} %all-to-all-done.3.arrived_ref, bf16[16,576]{1,0:T(8,128)(2,1)S(1)} %pad.5.fresh_ref, s32[1,384]{1,0:T(1,128)S(1)} %reshape.465.live_ref), custom_call_target="tpu_custom_call" | custom-call | tf_op jit(solution)/shard_map/pallas_call | solution.py:287
  127.6 4.7 %all-to-all-start.4 = ((bf16[16,32,512]{2,1,0:T(8,128)(2,1)}), bf16[16,32,512]{2,1,0:T(8,128)(2,1)S(1)}, u32[]{:S(2)}, u32[]{:S(2)}) async-start(bf16[16,32,512]{2,1,0:T(8,128)(2,1)} %bitcast.24), calls=%async_computation.4 | async-start | bytes 1048576 | tf_op jit(solution)/shard_map/all_to_all | solution.py:408
  132.8 1.4 fusion.1
  134.3 8.3 %all-to-all-done.4 = bf16[16,32,512]{2,1,0:T(8,128)(2,1)S(1)} async-done(((bf16[16,32,512]{2,1,0:T(8,128)(2,1)}), bf16[16,32,512]{2,1,0:T(8,128)(2,1)S(1)}, u32[]{:S(2)}, u32[]{:S(2)}) %all-to-all-start.4) | async-done | bytes 524320 | tf_op jit(solution)/shard_map/all_to_all | solution.py:408
  142.6 0.7 fusion.2
  143.3 0.8 copy.70
  (82 shorter events, 3.3 us)
Async XLA Ops:
  0.6 86.5 %copy-start = (bf16[8,128,512]{2,1,0:T(8,128)(2,1)S(1)}, bf16[8,128,512]{2,1,0:T(8,128)(2,1)}, u32[]{:S(2)}) copy-start(bf16[8,128,512]{2,1,0:T(8,128)(2,1)} %param.13) | copy-start | bytes 3145732
  11.3 8.4 %copy-start.4 = (s32[8,16]{1,0:T(8,128)S(1)}, s32[8,16]{1,0:T(8,128)}, u32[]{:S(2)}) copy-start(s32[8,16]{1,0:T(8,128)} %len_ref.1) | copy-start | bytes 1540
  11.3 8.7 %copy-start.5 = (f32[512]{0:T(512)S(1)}, f32[512]{0:T(512)}, u32[]{:S(2)}) copy-start(f32[512]{0:T(512)} %param.12) | copy-start | bytes 6148
  11.3 9.0 %copy-start.6 = (s32[128]{0:T(128)S(1)}, s32[128]{0:T(128)}, u32[]{:S(2)}) copy-start(s32[128]{0:T(128)} %param.18) | copy-start | bytes 1540
  11.4 10.0 %copy-start.7 = (s32[1,96]{1,0:T(1,128)S(1)}, s32[1,96]{1,0:T(1,128)}, u32[]{:S(2)}) copy-start(s32[1,96]{1,0:T(1,128)} %param.19) | copy-start | bytes 1156
  11.4 36.0 %all-to-all-start = ((bf16[4,4,576,256]{3,2,1,0:T(8,128)(2,1)}), bf16[4,4,576,256]{3,2,1,0:T(8,128)(2,1)}, u32[]{:S(2)}, u32[]{:S(2)}) async-start(bf16[4,4,576,256]{3,2,1,0:T(8,128)(2,1)} %shard_map.113), calls=%async_computation | async-start | bytes 9437184 | tf_op jit(solution)/shard_map/all_to_all | solution.py:334
  50.6 16.0 %all-to-all-start.1 = ((bf16[4,576,256]{2,1,0:T(8,128)(2,1)}), bf16[4,576,256]{2,1,0:T(8,128)(2,1)S(1)}, u32[]{:S(2)}, u32[]{:S(2)}) async-start(bf16[4,576,256]{2,1,0:T(8,128)(2,1)} %shard_map.114), calls=%async_computation.1 | async-start | bytes 2359296 | tf_op jit(solution)/shard_map/all_to_all | solution.py:336
  68.1 18.9 %copy-start.3 = (bf16[1,16,4,8,192]{4,3,2,1,0:T(8,128)(2,1)S(1)}, bf16[1,16,4,8,192]{4,3,2,1,0:T(8,128)(2,1)}, u32[]{:S(2)}) copy-start(bf16[1,16,4,8,192]{4,3,2,1,0:T(8,128)(2,1)} %param.15) | copy-start | bytes 589828
  68.1 18.6 %all-to-all-start.2 = ((bf16[4,576,256]{2,1,0:T(8,128)(2,1)}), bf16[4,576,256]{2,1,0:T(8,128)(2,1)S(1)}, u32[]{:S(2)}, u32[]{:S(2)}) async-start(bf16[4,576,256]{2,1,0:T(8,128)(2,1)} %shard_map.115), calls=%async_computation.2 | async-start | bytes 2359296 | tf_op jit(solution)/shard_map/all_to_all | solution.py:357
  86.7 3.0 %collective-permute-start = (bf16[4,576,256]{2,1,0:T(8,128)(2,1)S(1)}, bf16[4,576,256]{2,1,0:T(8,128)(2,1)}, u32[]{:S(2)}, u32[]{:S(2)}) collective-permute-start(bf16[4,576,256]{2,1,0:T(8,128)(2,1)S(1)} %all-to-all-done.2.near_ref), channel_id=1, source_target_pairs={{0,1},{1,0},{2,3},{3,2},{4,5},{5,4},{6,7},{7,6},{8,9},{9,8},{10,11... | collective-permute-start | bytes 3538952 | tf_op jit(solution)/shard_map/ppermute | solution.py:358
  93.8 1.2 copy-start.1
  95.0 29.8 %all-to-all-start.3 = ((bf16[16,80,576]{2,1,0:T(8,128)(2,1)}), bf16[16,80,576]{2,1,0:T(8,128)(2,1)S(1)}, u32[]{:S(2)}, u32[]{:S(2)}) async-start(bf16[16,80,576]{2,1,0:T(8,128)(2,1)} %copy-done.1), calls=%async_computation.3 | async-start | bytes 3276800 | tf_op jit(solution)/shard_map/all_to_all | solution.py:382
  127.6 15.0 %all-to-all-start.4 = ((bf16[16,32,512]{2,1,0:T(8,128)(2,1)}), bf16[16,32,512]{2,1,0:T(8,128)(2,1)S(1)}, u32[]{:S(2)}, u32[]{:S(2)}) async-start(bf16[16,32,512]{2,1,0:T(8,128)(2,1)} %bitcast.24), calls=%async_computation.4 | async-start | bytes 1048576 | tf_op jit(solution)/shard_map/all_to_all | solution.py:408
  132.8 9.8 %copy-start.2 = (bf16[8,512,128]{2,1,0:T(8,128)(2,1)S(1)}, bf16[8,512,128]{2,1,0:T(8,128)(2,1)}, u32[]{:S(2)}) copy-start(bf16[8,512,128]{2,1,0:T(8,128)(2,1)} %param.14) | copy-start | bytes 3145732

commit v6 on v4

--- a/solution.py
+++ b/solution.py
@@ -22,6 +22,7 @@
 AHEAD = 3
 PAIR = 2
 SIDE = 4
+HALF = 2
 STEPS = 4
 
 EPS = 1e-06
@@ -30,21 +31,21 @@
 
 
 def project_kernel(
-    len_ref, hid_ref, down_ref, out_ref, span_ref, sent_ref, shift_ref, turned_ref, hold_ref, in_sem, out_sem
+    len_ref, hid_ref, down_w_ref, up_ref, down_ref, wait_ref, own_ref,
+    span_ref, shift_ref, turned_ref, hold_ref, wait_hold_ref, own_hold_ref, in_sem, out_sem,
 ):
     def load(part):
         where = pl.ds(part * PAIR * TOK, PAIR * TOK)
         return pltpu.make_async_copy(hid_ref.at[:, where], span_ref.at[:, where], in_sem.at[part])
 
-    def store(residue):
-        where = residue // SIDE, residue % SIDE
-        return pltpu.make_async_copy(sent_ref.at[residue], out_ref.at[where], out_sem.at[residue])
+    keep_own = pltpu.make_async_copy(own_hold_ref, own_ref, out_sem.at[0])
+    keep_wait = pltpu.make_async_copy(wait_hold_ref, wait_ref, out_sem.at[1])
 
     parts = REQS // PAIR
     for part in range(AHEAD):
         load(part).start()
     hold_ref[...] = jnp.zeros_like(hold_ref)
-    turned_ref[...] = down_ref[...].astype(F32).T.astype(BF)
+    turned_ref[...] = down_w_ref[...].astype(F32).T.astype(BF)
     shape = (REQS, 24, 256)
     offset = lax.broadcasted_iota(jnp.int32, shape, 2)
     offset = offset - lax.broadcasted_iota(jnp.int32, shape, 0)
@@ -77,41 +78,87 @@
 
         start = start + count
 
-    for residue in range(REQS):
-        rows = hold_ref[residue, :PACK, :].astype(BF)
-        sent_ref[residue] = lax.dot_general(
-            turned_ref[...], rows, (((1,), (1,)), ((), ())), preferred_element_type=F32
-        ).astype(BF)
-        store(residue).start()
-    for residue in range(REQS):
-        store(residue).wait()
+    pre_rank, dec_rank = lax.axis_index("pre"), lax.axis_index("dec")
+    place = jnp.where(
+        lax.rem(dec_rank, 2) == 0, lax.div(pre_rank, SIDE), lax.rem(pre_rank, SIDE)
+    )
+    for away in (0, 1, 3, 2):
+        for item in range(SIDE):
+            residue = lax.rem(place + away, SIDE) * SIDE + item
+            rows = hold_ref[residue, :PACK, :].astype(BF)
+            part = lax.dot_general(
+                turned_ref[...], rows, (((1,), (1,)), ((), ())), preferred_element_type=F32
+            )
+            late, lane = item // HALF, item % HALF
+            if away == 0:
+                own_hold_ref[item] = part
+            elif away == 1 and late:
+                up_ref[1, lane] = part.astype(BF)
+            elif away == 1:
+                wait_hold_ref[0, lane] = part
+            elif away == 3 and late:
+                wait_hold_ref[1, lane] = part
+            elif away == 3:
+                down_ref[1, lane] = part.astype(BF)
+            elif late:
+                down_ref[0, lane] = part.astype(BF)
+            else:
+                up_ref[0, lane] = part.astype(BF)
+        if away == 0:
+            keep_own.start()
+        elif away == 3:
+            keep_wait.start()
+    keep_own.wait()
+    keep_wait.wait()
 
 
 def project(lengths, hidden_t, kv_down):
     depth = hidden_t.shape[0]
+    vmem = pl.BlockSpec(memory_space=pltpu.VMEM)
+    pair = (2, HALF, WIDTH, PACK)
     return pl.pallas_call(
         project_kernel,
-        out_shape=jax.ShapeDtypeStruct((SIDE, SIDE, WIDTH, PACK), BF),
+        out_shape=(
+            jax.ShapeDtypeStruct(pair, BF),
+            jax.ShapeDtypeStruct(pair, BF),
+            jax.ShapeDtypeStruct(pair, F32),
+            jax.ShapeDtypeStruct((SIDE, WIDTH, PACK), F32),
+        ),
         in_specs=[
             pl.BlockSpec(memory_space=pltpu.SMEM),
             pl.BlockSpec(memory_space=pl.ANY),
-            pl.BlockSpec(memory_space=pltpu.VMEM),
+            vmem,
         ],
-        out_specs=pl.BlockSpec(memory_space=pl.ANY),
+        out_specs=(vmem, vmem, pl.BlockSpec(memory_space=pl.ANY), pl.BlockSpec(memory_space=pl.ANY)),
         scratch_shapes=[
             pltpu.VMEM((depth, REQS * TOK), BF),
-            pltpu.VMEM((REQS, WIDTH, PACK), BF),
             pltpu.VMEM((REQS, 24, 256), jnp.int32),
             pltpu.VMEM((WIDTH, depth), BF),
             pltpu.VMEM((REQS, HOLD, depth), F32),
+            pltpu.VMEM(pair, F32),
+            pltpu.VMEM((SIDE, WIDTH, PACK), F32),
             pltpu.SemaphoreType.DMA((REQS // PAIR,)),
-            pltpu.SemaphoreType.DMA((REQS,)),
+            pltpu.SemaphoreType.DMA((2,)),
         ],
-        compiler_params=pltpu.CompilerParams(vmem_limit_bytes=58 << 20),
+        compiler_params=pltpu.CompilerParams(vmem_limit_bytes=50 << 20),
         cost_estimate=pl.CostEstimate(
             flops=2 * REQS * TOK * depth * WIDTH, bytes_accessed=11 << 20, transcendentals=0
         ),
     )(lengths, hidden_t, kv_down)
+
+
+def relay_kernel(wait_ref, from_below_ref, from_above_ref, up_ref, down_ref):
+    up_ref[...] = (wait_ref[0] + from_below_ref[0].astype(F32)).astype(BF)
+    down_ref[...] = (wait_ref[1] + from_above_ref[0].astype(F32)).astype(BF)
+
+
+def relay(wait, from_below, from_above):
+    shape = jax.ShapeDtypeStruct((HALF, WIDTH, PACK), BF)
+    return pl.pallas_call(
+        relay_kernel,
+        out_shape=(shape, shape),
+        compiler_params=pltpu.CompilerParams(vmem_limit_bytes=8 << 20),
+    )(wait, from_below, from_above)
 
 
 def add_up(parts):
@@ -121,29 +168,22 @@
     return total
 
 
-def first_sum_kernel(parts_ref, out_ref, sent_ref, out_sem):
-    def store(part):
-        return pltpu.make_async_copy(sent_ref.at[part], out_ref.at[part], out_sem.at[part])
-
-    for part in range(SIDE):
-        sent_ref[part] = add_up(parts_ref[:, part]).astype(BF)
-        store(part).start()
-    for part in range(SIDE):
-        store(part).wait()
-
-
-def first_sum(parts):
+def first_sum_kernel(own_ref, below_ref, above_ref, late_below_ref, late_above_ref, out_ref):
+    for item in range(HALF):
+        out_ref[item] = (
+            own_ref[item] + late_below_ref[item].astype(F32) + above_ref[1, item].astype(F32)
+        ).astype(BF)
+        out_ref[HALF + item] = (
+            own_ref[HALF + item] + below_ref[1, item].astype(F32) + late_above_ref[item].astype(F32)
+        ).astype(BF)
+
+
+def first_sum(own, below, above, late_below, late_above):
     return pl.pallas_call(
         first_sum_kernel,
         out_shape=jax.ShapeDtypeStruct((SIDE, WIDTH, PACK), BF),
-        in_specs=[pl.BlockSpec(memory_space=pltpu.VMEM)],
-        out_specs=pl.BlockSpec(memory_space=pl.ANY),
-        scratch_shapes=[
-            pltpu.VMEM((SIDE, WIDTH, PACK), BF),
-            pltpu.SemaphoreType.DMA((SIDE,)),
-        ],
-        compiler_params=pltpu.CompilerParams(vmem_limit_bytes=16 << 20),
-    )(parts)
+        compiler_params=pltpu.CompilerParams(vmem_limit_bytes=8 << 20),
+    )(own, below, above, late_below, late_above)
 
 
 def finish_kernel(parts_ref, gain_ref, cosine_ref, sine_ref, valid_ref, out_ref):
@@ -252,6 +292,16 @@
     return found
 
 
+def neighbours(step):
+    pairs = []
+    for pre in range(REQS):
+        y, z = pre // SIDE, pre % SIDE
+        for dec in range(2 * SIDE):
+            ny, nz = ((y + step) % SIDE, z) if dec % 2 == 0 else (y, (z + step) % SIDE)
+            pairs.append((pre * 2 * SIDE + dec, (ny * SIDE + nz) * 2 * SIDE + dec))
+    return pairs
+
+
 def shards(
     hidden, kv_down, kv_gain, uk_weight, uv_weight, queries, new_keys, lengths, assign, block_table
 ):
@@ -269,10 +319,14 @@
     own_starts = lax.dynamic_index_in_dim(starts, dec_rank, 0, keepdims=False)
     own_ends = lax.dynamic_index_in_dim(ends, dec_rank, 0, keepdims=False)
 
-    packed = project(lengths, hidden[0].T, kv_down)
-
-    packed = lax.all_to_all(packed, both, 0, 0, tiled=True, axis_index_groups=groups_of(0))
-    packed = first_sum(packed)
+    up, down, wait, own = project(lengths, hidden[0].T, kv_down)
+
+    below = lax.ppermute(up, both, neighbours(1))
+    above = lax.ppermute(down, both, neighbours(-1))
+    up, down = relay(wait, below, above)
+    late_below = lax.ppermute(up, both, neighbours(1))
+    late_above = lax.ppermute(down, both, neighbours(-1))
+    packed = first_sum(own, below, above, late_below, late_above)
     packed = lax.all_to_all(packed, both, 0, 0, tiled=True, axis_index_groups=groups_of(1))
 
     row = jnp.arange(PACK, dtype=jnp.int32)

time: 144 us -> 141 us (0.979)
  waiting for transfers between devices: 85.8 us -> 75.1 us
  local copies, waits for them, and re-layouts: 7.05 us -> 12.9 us
  starting transfers between devices: 22.2 us -> 24.9 us
    all_to_all x2 -> x1, waiting for transfers between devices: 41 us -> 11.3 us  [shards(): lax.all_to_all(packed, both, 0, 0, tiled=True, axis_index_groups=groups_o...]
    ppermute x0 -> x4, waiting for transfers between devices: none -> 21.7 us  [the longest x1 14.2 us: shards(): below = lax.ppermute(up, both, neighbours(1))]
    ppermute x0 -> x4, starting transfers between devices: none -> 6.54 us  [the longest x1 1.73 us: shards(): below = lax.ppermute(up, both, neighbours(1))]
    unnamed x19 -> x29, local copies, waits for them, and re-layouts: 2.18 us -> 7.35 us
    all_to_all x2 -> x1, starting transfers between devices: 10.5 us -> 5.44 us  [shards(): lax.all_to_all(packed, both, 0, 0, tiled=True, axis_index_groups=groups_o...]
    pallas_call x1 -> x2, Pallas kernels: 10.7 us -> 11.2 us  [the longest x1 10 us: project(): pl.pallas_call(project_kernel, out_shape=(jax.ShapeDtypeStruct(pair, BF),...]
  transfers between devices with their start and end apart: 6 -> 9, of which waited for: 6 -> 9; matrix products, arithmetic and copies ran while one was open for 6% -> 7% of each run, Pallas kernels for 0% -> 0%
where the time goes in v6:
time: 141 us
  waiting for transfers between devices  75.1 us (53%)
  starting transfers between devices  24.9 us (18%)
  Pallas kernels  21.4 us (15%)
  local copies, waits for them, and re-layouts  12.9 us (9%)
  matrix products  2.46 us (2%)
  other arithmetic  2.21 us (2%)
  between operations  1.61 us (1%)
    all_to_all x1, waiting for transfers between devices, shards(): arrived = lax.all_to_all(outgoing, 'pre', 0, 0, tiled=True)  21.3 us
    ppermute x1, waiting for transfers between devices, shards(): below = lax.ppermute(up, both, neighbours(1))  14.2 us
    all_to_all x1, waiting for transfers between devices, shards(): lax.all_to_all(packed, both, 0, 0, tiled=True, axis_index_groups=groups_o...  11.3 us
    all_to_all x1, waiting for transfers between devices, shards(): lax.all_to_all(rows, 'dec', 0, 0, tiled=True, axis_index_groups=along_x)  11.2 us
    pallas_call x1, Pallas kernels, project(): pl.pallas_call(project_kernel, out_shape=(jax.ShapeDtypeStruct(pair, BF),...  10 us
    all_to_all x1, waiting for transfers between devices, shards(): lax.all_to_all(mixed.reshape(REQS, -1, LAT), 'pre', 0, 0, tiled=True)  8.13 us
    unnamed x29, local copies, waits for them, and re-layouts  7.35 us
    ppermute x1, waiting for transfers between devices, shards(): late_below = lax.ppermute(up, both, neighbours(1))  6.69 us
  transfers between devices with their start and end apart: 9, of which 9 were waited for; matrix products, arithmetic and copies ran while one was open for 7% of the time, Pallas kernels for 0%

profile of v6, /device:TPU:0, one launch (start us, length us, event | category | flops | bytes accessed | tf_op | source)
XLA Modules:
  0.0 140.7 jit_solution(12283480830345734769)
XLA Ops:
  0.7 0.8 copy-done.5
  1.4 1.1 copy-done.7
  2.5 10.0 %shard_map.113 = (bf16[2,2,576,256]{3,2,1,0:T(8,128)(2,1)S(1)}, bf16[2,2,576,256]{3,2,1,0:T(8,128)(2,1)S(1)}, f32[2,2,576,256]{3,2,1,0:T(8,128)}, f32[4,576,256]{2,1,0:T(8,128)}) custom-call(s32[8,16]{1,0:T(8,128)S(1)} %copy-done.5, bf16[448,6144]{1,0:T(8,128)(2,1)} %bitcast.67, bf16[448,576]{1,0:T(8,128)(2,1)S(1)} %copy-done.7), custom_call_target="tpu_custom_call" | custom-call | flops 3170893824 | bytes 11534336 | tf_op jit(solution)/shard_map/pallas_call | solution.py:119
  12.5 1.7 %collective-permute-start = (bf16[2,2,576,256]{3,2,1,0:T(8,128)(2,1)S(1)}, bf16[2,2,576,256]{3,2,1,0:T(8,128)(2,1)S(1)}, u32[]{:S(2)}, u32[]{:S(2)}) collective-permute-start(bf16[2,2,576,256]{3,2,1,0:T(8,128)(2,1)S(1)} %get-tuple-element.9), channel_id=1, source_target_pairs={{0,32},{1,9},{2,34},{3,11},{4,36},{5,13},{6,38},{7,15},{8,40},{9,1... | collective-permute-start | bytes 3538952 | tf_op jit(solution)/shard_map/ppermute | solution.py:324
  14.3 1.6 %collective-permute-start.1 = (bf16[2,2,576,256]{3,2,1,0:T(8,128)(2,1)S(1)}, bf16[2,2,576,256]{3,2,1,0:T(8,128)(2,1)S(1)}, u32[]{:S(2)}, u32[]{:S(2)}) collective-permute-start(bf16[2,2,576,256]{3,2,1,0:T(8,128)(2,1)S(1)} %get-tuple-element.10), channel_id=1, source_target_pairs={{0,96},{1,25},{2,98},{3,27},{4,100},{5,29},{6,102},{7,31},{8,104},... | collective-permute-start | bytes 3538952 | tf_op jit(solution)/shard_map/ppermute | solution.py:325
  15.8 14.2 %collective-permute-done.from_below_ref.below_ref = bf16[2,2,576,256]{3,2,1,0:T(8,128)(2,1)S(1)} collective-permute-done((bf16[2,2,576,256]{3,2,1,0:T(8,128)(2,1)S(1)}, bf16[2,2,576,256]{3,2,1,0:T(8,128)(2,1)S(1)}, u32[]{:S(2)}, u32[]{:S(2)}) %collective-permute-start) | collective-permute-done | bytes 1179680 | tf_op jit(solution)/shard_map/ppermute | solution.py:324
  30.5 1.7 %copy-done.3 = f32[2,2,576,256]{3,2,1,0:T(8,128)S(1)} copy-done((f32[2,2,576,256]{3,2,1,0:T(8,128)S(1)}, f32[2,2,576,256]{3,2,1,0:T(8,128)}, u32[]{:S(2)}) %copy-start.3) | copy-done | bytes 2359320
  32.1 1.2 shard_map.114
  33.3 1.6 %collective-permute-start.2 = (bf16[2,576,256]{2,1,0:T(8,128)(2,1)}, bf16[2,576,256]{2,1,0:T(8,128)(2,1)}, u32[]{:S(2)}, u32[]{:S(2)}) collective-permute-start(bf16[2,576,256]{2,1,0:T(8,128)(2,1)} %get-tuple-element.12), channel_id=1, source_target_pairs={{0,32},{1,9},{2,34},{3,11},{4,36},{5,13},{6,38},{7,15},{8,40},{9,1... | collective-permute-start | bytes 1769480 | tf_op jit(solution)/shard_map/ppermute | solution.py:327
  34.9 1.7 %collective-permute-start.3 = (bf16[2,576,256]{2,1,0:T(8,128)(2,1)}, bf16[2,576,256]{2,1,0:T(8,128)(2,1)}, u32[]{:S(2)}, u32[]{:S(2)}) collective-permute-start(bf16[2,576,256]{2,1,0:T(8,128)(2,1)} %get-tuple-element.13), channel_id=1, source_target_pairs={{0,96},{1,25},{2,98},{3,27},{4,100},{5,29},{6,102},{7,31},{8,104},... | collective-permute-start | bytes 1769480 | tf_op jit(solution)/shard_map/ppermute | solution.py:328
  36.9 0.9 copy.63.gain_ref
  38.0 6.7 %collective-permute-done.2.late_below_ref = bf16[2,576,256]{2,1,0:T(8,128)(2,1)} collective-permute-done((bf16[2,576,256]{2,1,0:T(8,128)(2,1)}, bf16[2,576,256]{2,1,0:T(8,128)(2,1)}, u32[]{:S(2)}, u32[]{:S(2)}) %collective-permute-start.2) | collective-permute-done | bytes 589856 | tf_op jit(solution)/shard_map/ppermute | solution.py:327
  45.1 1.7 %copy-done.2 = f32[4,576,256]{2,1,0:T(8,128)S(1)} copy-done((f32[4,576,256]{2,1,0:T(8,128)S(1)}, f32[4,576,256]{2,1,0:T(8,128)}, u32[]{:S(2)}) %copy-start.2) | copy-done | bytes 2359320
  46.8 2.6 %shard_map.115 = bf16[4,576,256]{2,1,0:T(8,128)(2,1)} custom-call(f32[4,576,256]{2,1,0:T(8,128)S(1)} %copy-done.2, bf16[2,2,576,256]{3,2,1,0:T(8,128)(2,1)S(1)} %collective-permute-done.from_below_ref.below_ref, bf16[2,2,576,256]{3,2,1,0:T(8,128)(2,1)S(1)} %collective-permute-done.1.from_above_ref.above_ref, ...), custom_call_target="tpu_custom_call" | custom-call | tf_op jit(solution)/shard_map/pallas_call | solution.py:182
  49.4 5.4 %all-to-all-start = ((bf16[4,576,256]{2,1,0:T(8,128)(2,1)}), bf16[4,576,256]{2,1,0:T(8,128)(2,1)S(1)}, u32[]{:S(2)}, u32[]{:S(2)}) async-start(bf16[4,576,256]{2,1,0:T(8,128)(2,1)} %shard_map.115), calls=%async_computation | async-start | bytes 2359296 | tf_op jit(solution)/shard_map/all_to_all | solution.py:330
  55.2 11.3 %all-to-all-done.parts_ref = bf16[4,576,256]{2,1,0:T(8,128)(2,1)S(1)} async-done(((bf16[4,576,256]{2,1,0:T(8,128)(2,1)}), bf16[4,576,256]{2,1,0:T(8,128)(2,1)S(1)}, u32[]{:S(2)}, u32[]{:S(2)}) %all-to-all-start) | async-done | bytes 1179680 | tf_op jit(solution)/shard_map/all_to_all | solution.py:330
  66.4 1.4 %shard_map.116 = bf16[4,576,256]{2,1,0:T(8,128)(2,1)} custom-call(bf16[4,576,256]{2,1,0:T(8,128)(2,1)S(1)} %all-to-all-done.parts_ref, f32[512,1]{1,0:T(8,128)S(1)} %copy-done.4, f32[32,256]{1,0:T(8,128)S(1)} %get-tuple-element.43.cosine_ref, f32[32,256]{1,0:T(8,128)S(1)} %get-tuple-element.42.sine_ref, s32[1,256]{1,0:T(1,128)S(1)} %bitcast.58), custom_call_target="tpu_custom_call" | custom-call | tf_op jit(solution)/shard_map/pallas_call | solution.py:207
  67.9 4.4 %all-to-all-start.1 = ((bf16[4,576,256]{2,1,0:T(8,128)(2,1)}), bf16[4,576,256]{2,1,0:T(8,128)(2,1)S(1)}, u32[]{:S(2)}, u32[]{:S(2)}) async-start(bf16[4,576,256]{2,1,0:T(8,128)(2,1)} %shard_map.116), calls=%async_computation.1 | async-start | bytes 2359296 | tf_op jit(solution)/shard_map/all_to_all | solution.py:351
  73.9 11.2 %all-to-all-done.1.near_ref = bf16[4,576,256]{2,1,0:T(8,128)(2,1)S(1)} async-done(((bf16[4,576,256]{2,1,0:T(8,128)(2,1)}), bf16[4,576,256]{2,1,0:T(8,128)(2,1)S(1)}, u32[]{:S(2)}, u32[]{:S(2)}) %all-to-all-start.1) | async-done | bytes 1179680 | tf_op jit(solution)/shard_map/all_to_all | solution.py:351
  86.5 1.6 %collective-permute-done.4.far_ref = bf16[4,576,256]{2,1,0:T(8,128)(2,1)} collective-permute-done((bf16[4,576,256]{2,1,0:T(8,128)(2,1)S(1)}, bf16[4,576,256]{2,1,0:T(8,128)(2,1)}, u32[]{:S(2)}, u32[]{:S(2)}) %collective-permute-start.4) | collective-permute-done | bytes 1179680 | tf_op jit(solution)/shard_map/ppermute | solution.py:352
  88.1 3.3 %shard_map.117 = bf16[16,80,576]{2,1,0:T(8,128)(2,1)S(1)} custom-call(s32[2,384]{1,0:T(2,128)S(1)} %pad_add_fusion.1.source_ref, s32[768,1]{1,0:T(8,128)S(1)} %reshape.446.order_ref, bf16[4,576,256]{2,1,0:T(8,128)(2,1)S(1)} %all-to-all-done.1.near_ref, bf16[4,576,256]{2,1,0:T(8,128)(2,1)} %collective-permute-done.4.far_ref, bf16[16,32,576]{2,1,0:T(8,128)(2,1)S(1)} %bitcast.57), custom_call_target="tpu_custom_call" | custom-call | tf_op jit(solution)/shard_map/pallas_call | solution.py:232
  91.4 1.2 copy-done.1
  92.5 4.9 %all-to-all-start.2 = ((bf16[16,80,576]{2,1,0:T(8,128)(2,1)}), bf16[16,80,576]{2,1,0:T(8,128)(2,1)S(1)}, u32[]{:S(2)}, u32[]{:S(2)}) async-start(bf16[16,80,576]{2,1,0:T(8,128)(2,1)} %copy-done.1), calls=%async_computation.2 | async-start | bytes 3276800 | tf_op jit(solution)/shard_map/all_to_all | solution.py:373
  99.7 0.7 fusion.9
  100.5 0.7 dynamic-slice_bitcast_fusion
  101.3 21.3 %all-to-all-done.2.arrived_ref = bf16[16,80,576]{2,1,0:T(8,128)(2,1)S(1)} async-done(((bf16[16,80,576]{2,1,0:T(8,128)(2,1)}), bf16[16,80,576]{2,1,0:T(8,128)(2,1)S(1)}, u32[]{:S(2)}, u32[]{:S(2)}) %all-to-all-start.2) | async-done | bytes 1474592 | tf_op jit(solution)/shard_map/all_to_all | solution.py:373
  122.7 2.9 %shard_map.118 = bf16[512,512]{1,0:T(8,128)(2,1)} custom-call(bf16[16,80,576]{2,1,0:T(8,128)(2,1)S(1)} %all-to-all-done.2.arrived_ref, bf16[16,576]{1,0:T(8,128)(2,1)S(1)} %pad.5.fresh_ref, s32[1,384]{1,0:T(1,128)S(1)} %reshape.443.live_ref), custom_call_target="tpu_custom_call" | custom-call | tf_op jit(solution)/shard_map/pallas_call | solution.py:270
  125.5 3.6 %all-to-all-start.3 = ((bf16[16,32,512]{2,1,0:T(8,128)(2,1)}), bf16[16,32,512]{2,1,0:T(8,128)(2,1)S(1)}, u32[]{:S(2)}, u32[]{:S(2)}) async-start(bf16[16,32,512]{2,1,0:T(8,128)(2,1)} %bitcast.22), calls=%async_computation.3 | async-start | bytes 1048576 | tf_op jit(solution)/shard_map/all_to_all | solution.py:398
  129.6 1.4 %fusion.1 = bf16[1,384,576]{1,2,0:T(8,128)(2,1)} fusion(bf16[768,576]{1,0:T(8,128)(2,1)S(1)} %bitcast.60, s32[768]{0:T(1024)S(1)} %eq.106), kind=kOutput, calls=%fused_computation.3 | convolution fusion | flops 340254720 | bytes 1330176 | tf_op jit(solution)/shard_map/dot_general | solution.py:388
  131.1 8.1 %all-to-all-done.3 = bf16[16,32,512]{2,1,0:T(8,128)(2,1)S(1)} async-done(((bf16[16,32,512]{2,1,0:T(8,128)(2,1)}), bf16[16,32,512]{2,1,0:T(8,128)(2,1)S(1)}, u32[]{:S(2)}, u32[]{:S(2)}) %all-to-all-start.3) | async-done | bytes 524320 | tf_op jit(solution)/shard_map/all_to_all | solution.py:398
  139.2 0.7 fusion.2
  139.9 0.8 copy.68
  (97 shorter events, 6.9 us)
Async XLA Ops:
  0.6 85.1 %copy-start = (bf16[8,128,512]{2,1,0:T(8,128)(2,1)S(1)}, bf16[8,128,512]{2,1,0:T(8,128)(2,1)}, u32[]{:S(2)}) copy-start(bf16[8,128,512]{2,1,0:T(8,128)(2,1)} %param.13) | copy-start | bytes 3145732
  0.6 0.8 copy-start.5
  1.4 1.1 copy-start.7
  12.5 17.5 %collective-permute-start = (bf16[2,2,576,256]{3,2,1,0:T(8,128)(2,1)S(1)}, bf16[2,2,576,256]{3,2,1,0:T(8,128)(2,1)S(1)}, u32[]{:S(2)}, u32[]{:S(2)}) collective-permute-start(bf16[2,2,576,256]{3,2,1,0:T(8,128)(2,1)S(1)} %get-tuple-element.9), channel_id=1, source_target_pairs={{0,32},{1,9},{2,34},{3,11},{4,36},{5,13},{6,38},{7,15},{8,40},{9,1... | collective-permute-start | bytes 3538952 | tf_op jit(solution)/shard_map/ppermute | solution.py:324
  14.3 16.2 %collective-permute-start.1 = (bf16[2,2,576,256]{3,2,1,0:T(8,128)(2,1)S(1)}, bf16[2,2,576,256]{3,2,1,0:T(8,128)(2,1)S(1)}, u32[]{:S(2)}, u32[]{:S(2)}) collective-permute-start(bf16[2,2,576,256]{3,2,1,0:T(8,128)(2,1)S(1)} %get-tuple-element.10), channel_id=1, source_target_pairs={{0,96},{1,25},{2,98},{3,27},{4,100},{5,29},{6,102},{7,31},{8,104},... | collective-permute-start | bytes 3538952 | tf_op jit(solution)/shard_map/ppermute | solution.py:325
  30.5 1.7 %copy-start.3 = (f32[2,2,576,256]{3,2,1,0:T(8,128)S(1)}, f32[2,2,576,256]{3,2,1,0:T(8,128)}, u32[]{:S(2)}) copy-start(f32[2,2,576,256]{3,2,1,0:T(8,128)} %get-tuple-element.11.wait_ref) | copy-start | bytes 7077892
  32.1 4.7 %copy-start.6 = (s32[8,16]{1,0:T(8,128)S(1)}, s32[8,16]{1,0:T(8,128)}, u32[]{:S(2)}) copy-start(s32[8,16]{1,0:T(8,128)} %len_ref.1) | copy-start | bytes 1540
  32.1 4.8 %copy-start.10 = (f32[512]{0:T(512)S(1)}, f32[512]{0:T(512)}, u32[]{:S(2)}) copy-start(f32[512]{0:T(512)} %param.12) | copy-start | bytes 6148
  32.1 5.8 %copy-start.11 = (s32[128]{0:T(128)S(1)}, s32[128]{0:T(128)}, u32[]{:S(2)}) copy-start(s32[128]{0:T(128)} %param.18) | copy-start | bytes 1540
  33.3 11.4 %collective-permute-start.2 = (bf16[2,576,256]{2,1,0:T(8,128)(2,1)}, bf16[2,576,256]{2,1,0:T(8,128)(2,1)}, u32[]{:S(2)}, u32[]{:S(2)}) collective-permute-start(bf16[2,576,256]{2,1,0:T(8,128)(2,1)} %get-tuple-element.12), channel_id=1, source_target_pairs={{0,32},{1,9},{2,34},{3,11},{4,36},{5,13},{6,38},{7,15},{8,40},{9,1... | collective-permute-start | bytes 1769480 | tf_op jit(solution)/shard_map/ppermute | solution.py:327
  34.9 10.2 %collective-permute-start.3 = (bf16[2,576,256]{2,1,0:T(8,128)(2,1)}, bf16[2,576,256]{2,1,0:T(8,128)(2,1)}, u32[]{:S(2)}, u32[]{:S(2)}) collective-permute-start(bf16[2,576,256]{2,1,0:T(8,128)(2,1)} %get-tuple-element.13), channel_id=1, source_target_pairs={{0,96},{1,25},{2,98},{3,27},{4,100},{5,29},{6,102},{7,31},{8,104},... | collective-permute-start | bytes 1769480 | tf_op jit(solution)/shard_map/ppermute | solution.py:328
  45.1 1.7 %copy-start.2 = (f32[4,576,256]{2,1,0:T(8,128)S(1)}, f32[4,576,256]{2,1,0:T(8,128)}, u32[]{:S(2)}) copy-start(f32[4,576,256]{2,1,0:T(8,128)} %get-tuple-element.8.own_ref) | copy-start | bytes 7077892
  49.4 17.0 %copy-start.4 = (f32[512,1]{1,0:T(8,128)S(1)}, f32[512,1]{1,0:T(8,128)}, u32[]{:S(2)}) copy-start(f32[512,1]{1,0:T(8,128)} %copy.63.gain_ref) | copy-start | bytes 6148
  49.4 17.0 %all-to-all-start = ((bf16[4,576,256]{2,1,0:T(8,128)(2,1)}), bf16[4,576,256]{2,1,0:T(8,128)(2,1)S(1)}, u32[]{:S(2)}, u32[]{:S(2)}) async-start(bf16[4,576,256]{2,1,0:T(8,128)(2,1)} %shard_map.115), calls=%async_computation | async-start | bytes 2359296 | tf_op jit(solution)/shard_map/all_to_all | solution.py:330
  67.9 5.3 %copy-start.12 = (s32[1,96]{1,0:T(1,128)S(1)}, s32[1,96]{1,0:T(1,128)}, u32[]{:S(2)}) copy-start(s32[1,96]{1,0:T(1,128)} %param.19) | copy-start | bytes 1156
  67.9 17.6 %copy-start.9 = (bf16[1,16,4,8,192]{4,3,2,1,0:T(8,128)(2,1)S(1)}, bf16[1,16,4,8,192]{4,3,2,1,0:T(8,128)(2,1)}, u32[]{:S(2)}) copy-start(bf16[1,16,4,8,192]{4,3,2,1,0:T(8,128)(2,1)} %param.15) | copy-start | bytes 589828
  67.9 17.2 %all-to-all-start.1 = ((bf16[4,576,256]{2,1,0:T(8,128)(2,1)}), bf16[4,576,256]{2,1,0:T(8,128)(2,1)S(1)}, u32[]{:S(2)}, u32[]{:S(2)}) async-start(bf16[4,576,256]{2,1,0:T(8,128)(2,1)} %shard_map.116), calls=%async_computation.1 | async-start | bytes 2359296 | tf_op jit(solution)/shard_map/all_to_all | solution.py:351
  85.1 3.0 %collective-permute-start.4 = (bf16[4,576,256]{2,1,0:T(8,128)(2,1)S(1)}, bf16[4,576,256]{2,1,0:T(8,128)(2,1)}, u32[]{:S(2)}, u32[]{:S(2)}) collective-permute-start(bf16[4,576,256]{2,1,0:T(8,128)(2,1)S(1)} %all-to-all-done.1.near_ref), channel_id=1, source_target_pairs={{0,1},{1,0},{2,3},{3,2},{4,5},{5,4},{6,7},{7,6},{8,9},{9,8},{10,11... | collective-permute-start | bytes 3538952 | tf_op jit(solution)/shard_map/ppermute | solution.py:352
  91.4 1.2 copy-start.1
  92.5 30.1 %all-to-all-start.2 = ((bf16[16,80,576]{2,1,0:T(8,128)(2,1)}), bf16[16,80,576]{2,1,0:T(8,128)(2,1)S(1)}, u32[]{:S(2)}, u32[]{:S(2)}) async-start(bf16[16,80,576]{2,1,0:T(8,128)(2,1)} %copy-done.1), calls=%async_computation.2 | async-start | bytes 3276800 | tf_op jit(solution)/shard_map/all_to_all | solution.py:373
  125.5 13.7 %all-to-all-start.3 = ((bf16[16,32,512]{2,1,0:T(8,128)(2,1)}), bf16[16,32,512]{2,1,0:T(8,128)(2,1)S(1)}, u32[]{:S(2)}, u32[]{:S(2)}) async-start(bf16[16,32,512]{2,1,0:T(8,128)(2,1)} %bitcast.22), calls=%async_computation.3 | async-start | bytes 1048576 | tf_op jit(solution)/shard_map/all_to_all | solution.py:398
  129.6 9.6 %copy-start.8 = (bf16[8,512,128]{2,1,0:T(8,128)(2,1)S(1)}, bf16[8,512,128]{2,1,0:T(8,128)(2,1)}, u32[]{:S(2)}) copy-start(bf16[8,512,128]{2,1,0:T(8,128)(2,1)} %param.14) | copy-start | bytes 3145732

commit v7 on v6

--- a/solution.py
+++ b/solution.py
@@ -147,6 +147,24 @@
     )(lengths, hidden_t, kv_down)
 
 
+def stage_kernel(share_ref, out_ref, sem):
+    copy = pltpu.make_async_copy(share_ref, out_ref, sem)
+    copy.start()
+    copy.wait()
+
+
+def stage(share):
+    return pl.pallas_call(
+        stage_kernel,
+        out_shape=jax.ShapeDtypeStruct(share.shape, F32),
+        in_specs=[pl.BlockSpec(memory_space=pl.ANY)],
+        out_specs=pl.BlockSpec(memory_space=pltpu.VMEM),
+        scratch_shapes=[pltpu.SemaphoreType.DMA],
+        compiler_params=pltpu.CompilerParams(vmem_limit_bytes=8 << 20),
+        cost_estimate=pl.CostEstimate(flops=0, bytes_accessed=5 << 20, transcendentals=0),
+    )(share)
+
+
 def relay_kernel(wait_ref, from_below_ref, from_above_ref, up_ref, down_ref):
     up_ref[...] = (wait_ref[0] + from_below_ref[0].astype(F32)).astype(BF)
     down_ref[...] = (wait_ref[1] + from_above_ref[0].astype(F32)).astype(BF)
@@ -323,10 +341,11 @@
 
     below = lax.ppermute(up, both, neighbours(1))
     above = lax.ppermute(down, both, neighbours(-1))
-    up, down = relay(wait, below, above)
+    up, down = relay(stage(wait), below, above)
+    own, up, down = lax.optimization_barrier((own, up, down))
     late_below = lax.ppermute(up, both, neighbours(1))
     late_above = lax.ppermute(down, both, neighbours(-1))
-    packed = first_sum(own, below, above, late_below, late_above)
+    packed = first_sum(stage(own), below, above, late_below, late_above)
     packed = lax.all_to_all(packed, both, 0, 0, tiled=True, axis_index_groups=groups_of(1))
 
     row = jnp.arange(PACK, dtype=jnp.int32)

time: 141 us -> 138 us (0.979)
  waiting for transfers between devices: 75.1 us -> 71.4 us
    ppermute x1, waiting for transfers between devices: 14.2 us -> 12.3 us  [shards(): below = lax.ppermute(up, both, neighbours(1))]
    ppermute x1, waiting for transfers between devices: 6.69 us -> 4.85 us  [shards(): late_below = lax.ppermute(up, both, neighbours(1))]
where the time goes in v7:
time: 138 us; the launch traced here: 137 us
  waiting for transfers between devices  71.4 us (52%)
  starting transfers between devices  24.9 us (18%)
  Pallas kernels  21.8 us (16%)
  local copies, waits for them, and re-layouts  12.9 us (9%)
  matrix products  2.46 us (2%)
  other arithmetic  2.21 us (2%)
  between operations  1.66 us (1%)
    all_to_all x1, waiting for transfers between devices, shards(): arrived = lax.all_to_all(outgoing, 'pre', 0, 0, tiled=True)  21.3 us
    ppermute x1, waiting for transfers between devices, shards(): below = lax.ppermute(up, both, neighbours(1))  12.3 us
    all_to_all x1, waiting for transfers between devices, shards(): lax.all_to_all(packed, both, 0, 0, tiled=True, axis_index_groups=groups_o...  11.3 us
    all_to_all x1, waiting for transfers between devices, shards(): lax.all_to_all(rows, 'dec', 0, 0, tiled=True, axis_index_groups=along_x)  11.2 us
    pallas_call x1, Pallas kernels, project(): pl.pallas_call(project_kernel, out_shape=(jax.ShapeDtypeStruct(pair, BF),...  10 us
    all_to_all x1, waiting for transfers between devices, shards(): lax.all_to_all(mixed.reshape(REQS, -1, LAT), 'pre', 0, 0, tiled=True)  8.13 us
    unnamed x29, local copies, waits for them, and re-layouts  7.35 us
    all_to_all x1, starting transfers between devices, shards(): lax.all_to_all(packed, both, 0, 0, tiled=True, axis_index_groups=groups_o...  5.44 us
  transfers between devices with their start and end apart: 9, of which 9 were waited for; matrix products, arithmetic and copies ran while one was open for 7% of the time, Pallas kernels for 0%

profile of v7, /device:TPU:0, one launch (start us, length us, event | category | flops | bytes accessed | tf_op | source)
XLA Modules:
  0.0 137.4 jit_solution(868397416872849362)
XLA Ops:
  0.7 0.8 copy-done.5
  1.4 1.1 copy-done.7
  2.5 10.0 %shard_map.113 = (bf16[2,2,576,256]{3,2,1,0:T(8,128)(2,1)S(1)}, bf16[2,2,576,256]{3,2,1,0:T(8,128)(2,1)S(1)}, f32[2,2,576,256]{3,2,1,0:T(8,128)}, f32[4,576,256]{2,1,0:T(8,128)}) custom-call(s32[8,16]{1,0:T(8,128)S(1)} %copy-done.5, bf16[448,6144]{1,0:T(8,128)(2,1)} %bitcast.67, bf16[448,576]{1,0:T(8,128)(2,1)S(1)} %copy-done.7), custom_call_target="tpu_custom_call" | custom-call | flops 3170893824 | bytes 11534336 | tf_op jit(solution)/shard_map/pallas_call | solution.py:119
  12.5 1.7 %collective-permute-start = (bf16[2,2,576,256]{3,2,1,0:T(8,128)(2,1)S(1)}, bf16[2,2,576,256]{3,2,1,0:T(8,128)(2,1)S(1)}, u32[]{:S(2)}, u32[]{:S(2)}) collective-permute-start(bf16[2,2,576,256]{3,2,1,0:T(8,128)(2,1)S(1)} %get-tuple-element.13), channel_id=1, source_target_pairs={{0,32},{1,9},{2,34},{3,11},{4,36},{5,13},{6,38},{7,15},{8,40},{9,1... | collective-permute-start | bytes 3538952 | tf_op jit(solution)/shard_map/ppermute | solution.py:342
  14.3 1.6 %collective-permute-start.1 = (bf16[2,2,576,256]{3,2,1,0:T(8,128)(2,1)S(1)}, bf16[2,2,576,256]{3,2,1,0:T(8,128)(2,1)S(1)}, u32[]{:S(2)}, u32[]{:S(2)}) collective-permute-start(bf16[2,2,576,256]{3,2,1,0:T(8,128)(2,1)S(1)} %get-tuple-element.14), channel_id=1, source_target_pairs={{0,96},{1,25},{2,98},{3,27},{4,100},{5,29},{6,102},{7,31},{8,104},... | collective-permute-start | bytes 3538952 | tf_op jit(solution)/shard_map/ppermute | solution.py:343
  15.8 1.7 %copy-done.3 = f32[2,2,576,256]{3,2,1,0:T(8,128)S(1)} copy-done((f32[2,2,576,256]{3,2,1,0:T(8,128)S(1)}, f32[2,2,576,256]{3,2,1,0:T(8,128)}, u32[]{:S(2)}) %copy-start.3) | copy-done | bytes 2359320
  17.7 12.3 %collective-permute-done.from_below_ref.below_ref = bf16[2,2,576,256]{3,2,1,0:T(8,128)(2,1)S(1)} collective-permute-done((bf16[2,2,576,256]{3,2,1,0:T(8,128)(2,1)S(1)}, bf16[2,2,576,256]{3,2,1,0:T(8,128)(2,1)S(1)}, u32[]{:S(2)}, u32[]{:S(2)}) %collective-permute-start) | collective-permute-done | bytes 1179680 | tf_op jit(solution)/shard_map/ppermute | solution.py:342
  30.5 1.2 shard_map.115
  31.7 1.6 %collective-permute-start.2 = (bf16[2,576,256]{2,1,0:T(8,128)(2,1)}, bf16[2,576,256]{2,1,0:T(8,128)(2,1)}, u32[]{:S(2)}, u32[]{:S(2)}) collective-permute-start(bf16[2,576,256]{2,1,0:T(8,128)(2,1)} %get-tuple-element.18), channel_id=1, source_target_pairs={{0,32},{1,9},{2,34},{3,11},{4,36},{5,13},{6,38},{7,15},{8,40},{9,1... | collective-permute-start | bytes 1769480 | tf_op jit(solution)/shard_map/ppermute | solution.py:346
  33.3 1.7 %collective-permute-start.3 = (bf16[2,576,256]{2,1,0:T(8,128)(2,1)}, bf16[2,576,256]{2,1,0:T(8,128)(2,1)}, u32[]{:S(2)}, u32[]{:S(2)}) collective-permute-start(bf16[2,576,256]{2,1,0:T(8,128)(2,1)} %get-tuple-element.19), channel_id=1, source_target_pairs={{0,96},{1,25},{2,98},{3,27},{4,100},{5,29},{6,102},{7,31},{8,104},... | collective-permute-start | bytes 1769480 | tf_op jit(solution)/shard_map/ppermute | solution.py:347
  35.3 0.9 copy.63.gain_ref
  36.4 1.7 %copy-done.2 = f32[4,576,256]{2,1,0:T(8,128)S(1)} copy-done((f32[4,576,256]{2,1,0:T(8,128)S(1)}, f32[4,576,256]{2,1,0:T(8,128)}, u32[]{:S(2)}) %copy-start.2) | copy-done | bytes 2359320
  38.2 4.8 %collective-permute-done.2.late_below_ref = bf16[2,576,256]{2,1,0:T(8,128)(2,1)} collective-permute-done((bf16[2,576,256]{2,1,0:T(8,128)(2,1)}, bf16[2,576,256]{2,1,0:T(8,128)(2,1)}, u32[]{:S(2)}, u32[]{:S(2)}) %collective-permute-start.2) | collective-permute-done | bytes 589856 | tf_op jit(solution)/shard_map/ppermute | solution.py:346
  43.5 2.6 %shard_map.117 = bf16[4,576,256]{2,1,0:T(8,128)(2,1)} custom-call(f32[4,576,256]{2,1,0:T(8,128)S(1)} %shard_map.116.own_ref, bf16[2,2,576,256]{3,2,1,0:T(8,128)(2,1)S(1)} %collective-permute-done.from_below_ref.below_ref, bf16[2,2,576,256]{3,2,1,0:T(8,128)(2,1)S(1)} %collective-permute-done.1.from_above_ref.above_ref, ...), custom_call_target="tpu_custom_call" | custom-call | tf_op jit(solution)/shard_map/pallas_call | solution.py:200
  46.1 5.4 %all-to-all-start = ((bf16[4,576,256]{2,1,0:T(8,128)(2,1)}), bf16[4,576,256]{2,1,0:T(8,128)(2,1)S(1)}, u32[]{:S(2)}, u32[]{:S(2)}) async-start(bf16[4,576,256]{2,1,0:T(8,128)(2,1)} %shard_map.117), calls=%async_computation | async-start | bytes 2359296 | tf_op jit(solution)/shard_map/all_to_all | solution.py:349
  51.9 11.3 %all-to-all-done.parts_ref = bf16[4,576,256]{2,1,0:T(8,128)(2,1)S(1)} async-done(((bf16[4,576,256]{2,1,0:T(8,128)(2,1)}), bf16[4,576,256]{2,1,0:T(8,128)(2,1)S(1)}, u32[]{:S(2)}, u32[]{:S(2)}) %all-to-all-start) | async-done | bytes 1179680 | tf_op jit(solution)/shard_map/all_to_all | solution.py:349
  63.1 1.4 %shard_map.118 = bf16[4,576,256]{2,1,0:T(8,128)(2,1)} custom-call(bf16[4,576,256]{2,1,0:T(8,128)(2,1)S(1)} %all-to-all-done.parts_ref, f32[512,1]{1,0:T(8,128)S(1)} %copy-done.4, f32[32,256]{1,0:T(8,128)S(1)} %get-tuple-element.49.cosine_ref, f32[32,256]{1,0:T(8,128)S(1)} %get-tuple-element.48.sine_ref, s32[1,256]{1,0:T(1,128)S(1)} %bitcast.58), custom_call_target="tpu_custom_call" | custom-call | tf_op jit(solution)/shard_map/pallas_call | solution.py:225
  64.6 4.4 %all-to-all-start.1 = ((bf16[4,576,256]{2,1,0:T(8,128)(2,1)}), bf16[4,576,256]{2,1,0:T(8,128)(2,1)S(1)}, u32[]{:S(2)}, u32[]{:S(2)}) async-start(bf16[4,576,256]{2,1,0:T(8,128)(2,1)} %shard_map.118), calls=%async_computation.1 | async-start | bytes 2359296 | tf_op jit(solution)/shard_map/all_to_all | solution.py:370
  70.6 11.2 %all-to-all-done.1.near_ref = bf16[4,576,256]{2,1,0:T(8,128)(2,1)S(1)} async-done(((bf16[4,576,256]{2,1,0:T(8,128)(2,1)}), bf16[4,576,256]{2,1,0:T(8,128)(2,1)S(1)}, u32[]{:S(2)}, u32[]{:S(2)}) %all-to-all-start.1) | async-done | bytes 1179680 | tf_op jit(solution)/shard_map/all_to_all | solution.py:370
  83.2 1.6 %collective-permute-done.4.far_ref = bf16[4,576,256]{2,1,0:T(8,128)(2,1)} collective-permute-done((bf16[4,576,256]{2,1,0:T(8,128)(2,1)S(1)}, bf16[4,576,256]{2,1,0:T(8,128)(2,1)}, u32[]{:S(2)}, u32[]{:S(2)}) %collective-permute-start.4) | collective-permute-done | bytes 1179680 | tf_op jit(solution)/shard_map/ppermute | solution.py:371
  84.7 3.3 %shard_map.119 = bf16[16,80,576]{2,1,0:T(8,128)(2,1)S(1)} custom-call(s32[2,384]{1,0:T(2,128)S(1)} %pad_add_fusion.1.source_ref, s32[768,1]{1,0:T(8,128)S(1)} %reshape.446.order_ref, bf16[4,576,256]{2,1,0:T(8,128)(2,1)S(1)} %all-to-all-done.1.near_ref, bf16[4,576,256]{2,1,0:T(8,128)(2,1)} %collective-permute-done.4.far_ref, bf16[16,32,576]{2,1,0:T(8,128)(2,1)S(1)} %bitcast.57), custom_call_target="tpu_custom_call" | custom-call | tf_op jit(solution)/shard_map/pallas_call | solution.py:250
  88.1 1.2 copy-done.1
  89.2 4.9 %all-to-all-start.2 = ((bf16[16,80,576]{2,1,0:T(8,128)(2,1)}), bf16[16,80,576]{2,1,0:T(8,128)(2,1)S(1)}, u32[]{:S(2)}, u32[]{:S(2)}) async-start(bf16[16,80,576]{2,1,0:T(8,128)(2,1)} %copy-done.1), calls=%async_computation.2 | async-start | bytes 3276800 | tf_op jit(solution)/shard_map/all_to_all | solution.py:392
  96.4 0.7 fusion.9
  97.2 0.7 dynamic-slice_bitcast_fusion
  98.0 21.3 %all-to-all-done.2.arrived_ref = bf16[16,80,576]{2,1,0:T(8,128)(2,1)S(1)} async-done(((bf16[16,80,576]{2,1,0:T(8,128)(2,1)}), bf16[16,80,576]{2,1,0:T(8,128)(2,1)S(1)}, u32[]{:S(2)}, u32[]{:S(2)}) %all-to-all-start.2) | async-done | bytes 1474592 | tf_op jit(solution)/shard_map/all_to_all | solution.py:392
  119.4 2.9 %shard_map.120 = bf16[512,512]{1,0:T(8,128)(2,1)} custom-call(bf16[16,80,576]{2,1,0:T(8,128)(2,1)S(1)} %all-to-all-done.2.arrived_ref, bf16[16,576]{1,0:T(8,128)(2,1)S(1)} %pad.5.fresh_ref, s32[1,384]{1,0:T(1,128)S(1)} %reshape.443.live_ref), custom_call_target="tpu_custom_call" | custom-call | tf_op jit(solution)/shard_map/pallas_call | solution.py:288
  122.2 3.6 %all-to-all-start.3 = ((bf16[16,32,512]{2,1,0:T(8,128)(2,1)}), bf16[16,32,512]{2,1,0:T(8,128)(2,1)S(1)}, u32[]{:S(2)}, u32[]{:S(2)}) async-start(bf16[16,32,512]{2,1,0:T(8,128)(2,1)} %bitcast.22), calls=%async_computation.3 | async-start | bytes 1048576 | tf_op jit(solution)/shard_map/all_to_all | solution.py:417
  126.3 1.4 %fusion.1 = bf16[1,384,576]{1,2,0:T(8,128)(2,1)} fusion(bf16[768,576]{1,0:T(8,128)(2,1)S(1)} %bitcast.60, s32[768]{0:T(1024)S(1)} %eq.106), kind=kOutput, calls=%fused_computation.3 | convolution fusion | flops 340254720 | bytes 1330176 | tf_op jit(solution)/shard_map/dot_general | solution.py:407
  127.8 8.1 %all-to-all-done.3 = bf16[16,32,512]{2,1,0:T(8,128)(2,1)S(1)} async-done(((bf16[16,32,512]{2,1,0:T(8,128)(2,1)}), bf16[16,32,512]{2,1,0:T(8,128)(2,1)S(1)}, u32[]{:S(2)}, u32[]{:S(2)}) %all-to-all-start.3) | async-done | bytes 524320 | tf_op jit(solution)/shard_map/all_to_all | solution.py:417
  135.9 0.7 fusion.2
  136.6 0.8 copy.68
  (99 shorter events, 7.2 us)
Async XLA Ops:
  0.6 81.8 %copy-start = (bf16[8,128,512]{2,1,0:T(8,128)(2,1)S(1)}, bf16[8,128,512]{2,1,0:T(8,128)(2,1)}, u32[]{:S(2)}) copy-start(bf16[8,128,512]{2,1,0:T(8,128)(2,1)} %param.13) | copy-start | bytes 3145732
  0.6 0.8 copy-start.5
  1.4 1.1 copy-start.7
  12.5 17.5 %collective-permute-start = (bf16[2,2,576,256]{3,2,1,0:T(8,128)(2,1)S(1)}, bf16[2,2,576,256]{3,2,1,0:T(8,128)(2,1)S(1)}, u32[]{:S(2)}, u32[]{:S(2)}) collective-permute-start(bf16[2,2,576,256]{3,2,1,0:T(8,128)(2,1)S(1)} %get-tuple-element.13), channel_id=1, source_target_pairs={{0,32},{1,9},{2,34},{3,11},{4,36},{5,13},{6,38},{7,15},{8,40},{9,1... | collective-permute-start | bytes 3538952 | tf_op jit(solution)/shard_map/ppermute | solution.py:342
  14.3 16.2 %collective-permute-start.1 = (bf16[2,2,576,256]{3,2,1,0:T(8,128)(2,1)S(1)}, bf16[2,2,576,256]{3,2,1,0:T(8,128)(2,1)S(1)}, u32[]{:S(2)}, u32[]{:S(2)}) collective-permute-start(bf16[2,2,576,256]{3,2,1,0:T(8,128)(2,1)S(1)} %get-tuple-element.14), channel_id=1, source_target_pairs={{0,96},{1,25},{2,98},{3,27},{4,100},{5,29},{6,102},{7,31},{8,104},... | collective-permute-start | bytes 3538952 | tf_op jit(solution)/shard_map/ppermute | solution.py:343
  15.8 1.7 %copy-start.3 = (f32[2,2,576,256]{3,2,1,0:T(8,128)S(1)}, f32[2,2,576,256]{3,2,1,0:T(8,128)}, u32[]{:S(2)}) copy-start(f32[2,2,576,256]{3,2,1,0:T(8,128)} %get-tuple-element.12.share_ref) | copy-start | bytes 7077892
  17.7 17.5 %copy-start.6 = (s32[8,16]{1,0:T(8,128)S(1)}, s32[8,16]{1,0:T(8,128)}, u32[]{:S(2)}) copy-start(s32[8,16]{1,0:T(8,128)} %len_ref.1) | copy-start | bytes 1540
  17.7 17.5 %copy-start.10 = (f32[512]{0:T(512)S(1)}, f32[512]{0:T(512)}, u32[]{:S(2)}) copy-start(f32[512]{0:T(512)} %param.12) | copy-start | bytes 6148
  17.7 18.6 %copy-start.11 = (s32[128]{0:T(128)S(1)}, s32[128]{0:T(128)}, u32[]{:S(2)}) copy-start(s32[128]{0:T(128)} %param.18) | copy-start | bytes 1540
  31.7 11.4 %collective-permute-start.2 = (bf16[2,576,256]{2,1,0:T(8,128)(2,1)}, bf16[2,576,256]{2,1,0:T(8,128)(2,1)}, u32[]{:S(2)}, u32[]{:S(2)}) collective-permute-start(bf16[2,576,256]{2,1,0:T(8,128)(2,1)} %get-tuple-element.18), channel_id=1, source_target_pairs={{0,32},{1,9},{2,34},{3,11},{4,36},{5,13},{6,38},{7,15},{8,40},{9,1... | collective-permute-start | bytes 1769480 | tf_op jit(solution)/shard_map/ppermute | solution.py:346
  33.3 10.2 %collective-permute-start.3 = (bf16[2,576,256]{2,1,0:T(8,128)(2,1)}, bf16[2,576,256]{2,1,0:T(8,128)(2,1)}, u32[]{:S(2)}, u32[]{:S(2)}) collective-permute-start(bf16[2,576,256]{2,1,0:T(8,128)(2,1)} %get-tuple-element.19), channel_id=1, source_target_pairs={{0,96},{1,25},{2,98},{3,27},{4,100},{5,29},{6,102},{7,31},{8,104},... | collective-permute-start | bytes 1769480 | tf_op jit(solution)/shard_map/ppermute | solution.py:347
  36.4 1.7 %copy-start.2 = (f32[4,576,256]{2,1,0:T(8,128)S(1)}, f32[4,576,256]{2,1,0:T(8,128)}, u32[]{:S(2)}) copy-start(f32[4,576,256]{2,1,0:T(8,128)} %get-tuple-element.17.share_ref) | copy-start | bytes 7077892
  46.1 17.0 %copy-start.4 = (f32[512,1]{1,0:T(8,128)S(1)}, f32[512,1]{1,0:T(8,128)}, u32[]{:S(2)}) copy-start(f32[512,1]{1,0:T(8,128)} %copy.63.gain_ref) | copy-start | bytes 6148
  46.1 17.0 %all-to-all-start = ((bf16[4,576,256]{2,1,0:T(8,128)(2,1)}), bf16[4,576,256]{2,1,0:T(8,128)(2,1)S(1)}, u32[]{:S(2)}, u32[]{:S(2)}) async-start(bf16[4,576,256]{2,1,0:T(8,128)(2,1)} %shard_map.117), calls=%async_computation | async-start | bytes 2359296 | tf_op jit(solution)/shard_map/all_to_all | solution.py:349
  64.6 5.3 %copy-start.12 = (s32[1,96]{1,0:T(1,128)S(1)}, s32[1,96]{1,0:T(1,128)}, u32[]{:S(2)}) copy-start(s32[1,96]{1,0:T(1,128)} %param.19) | copy-start | bytes 1156
  64.6 17.6 %copy-start.9 = (bf16[1,16,4,8,192]{4,3,2,1,0:T(8,128)(2,1)S(1)}, bf16[1,16,4,8,192]{4,3,2,1,0:T(8,128)(2,1)}, u32[]{:S(2)}) copy-start(bf16[1,16,4,8,192]{4,3,2,1,0:T(8,128)(2,1)} %param.15) | copy-start | bytes 589828
  64.6 17.2 %all-to-all-start.1 = ((bf16[4,576,256]{2,1,0:T(8,128)(2,1)}), bf16[4,576,256]{2,1,0:T(8,128)(2,1)S(1)}, u32[]{:S(2)}, u32[]{:S(2)}) async-start(bf16[4,576,256]{2,1,0:T(8,128)(2,1)} %shard_map.118), calls=%async_computation.1 | async-start | bytes 2359296 | tf_op jit(solution)/shard_map/all_to_all | solution.py:370
  81.8 3.0 %collective-permute-start.4 = (bf16[4,576,256]{2,1,0:T(8,128)(2,1)S(1)}, bf16[4,576,256]{2,1,0:T(8,128)(2,1)}, u32[]{:S(2)}, u32[]{:S(2)}) collective-permute-start(bf16[4,576,256]{2,1,0:T(8,128)(2,1)S(1)} %all-to-all-done.1.near_ref), channel_id=1, source_target_pairs={{0,1},{1,0},{2,3},{3,2},{4,5},{5,4},{6,7},{7,6},{8,9},{9,8},{10,11... | collective-permute-start | bytes 3538952 | tf_op jit(solution)/shard_map/ppermute | solution.py:371
  88.1 1.2 copy-start.1
  89.2 30.1 %all-to-all-start.2 = ((bf16[16,80,576]{2,1,0:T(8,128)(2,1)}), bf16[16,80,576]{2,1,0:T(8,128)(2,1)S(1)}, u32[]{:S(2)}, u32[]{:S(2)}) async-start(bf16[16,80,576]{2,1,0:T(8,128)(2,1)} %copy-done.1), calls=%async_computation.2 | async-start | bytes 3276800 | tf_op jit(solution)/shard_map/all_to_all | solution.py:392
  122.2 13.7 %all-to-all-start.3 = ((bf16[16,32,512]{2,1,0:T(8,128)(2,1)}), bf16[16,32,512]{2,1,0:T(8,128)(2,1)S(1)}, u32[]{:S(2)}, u32[]{:S(2)}) async-start(bf16[16,32,512]{2,1,0:T(8,128)(2,1)} %bitcast.22), calls=%async_computation.3 | async-start | bytes 1048576 | tf_op jit(solution)/shard_map/all_to_all | solution.py:417
  126.3 9.6 %copy-start.8 = (bf16[8,512,128]{2,1,0:T(8,128)(2,1)S(1)}, bf16[8,512,128]{2,1,0:T(8,128)(2,1)}, u32[]{:S(2)}) copy-start(bf16[8,512,128]{2,1,0:T(8,128)(2,1)} %param.14) | copy-start | bytes 3145732

commit v8 on v7

--- a/solution.py
+++ b/solution.py
@@ -79,12 +79,12 @@
         start = start + count
 
     pre_rank, dec_rank = lax.axis_index("pre"), lax.axis_index("dec")
-    place = jnp.where(
-        lax.rem(dec_rank, 2) == 0, lax.div(pre_rank, SIDE), lax.rem(pre_rank, SIDE)
-    )
+    along_y, along_z = lax.div(pre_rank, SIDE), lax.rem(pre_rank, SIDE)
+    even = lax.rem(dec_rank, 2) == 0
+    place, other = jnp.where(even, along_y, along_z), jnp.where(even, along_z, along_y)
     for away in (0, 1, 3, 2):
         for item in range(SIDE):
-            residue = lax.rem(place + away, SIDE) * SIDE + item
+            residue = lax.rem(place + away, SIDE) * SIDE + lax.rem(other + item, SIDE)
             rows = hold_ref[residue, :PACK, :].astype(BF)
             part = lax.dot_general(
                 turned_ref[...], rows, (((1,), (1,)), ((), ())), preferred_element_type=F32
@@ -140,7 +140,7 @@
             pltpu.SemaphoreType.DMA((REQS // PAIR,)),
             pltpu.SemaphoreType.DMA((2,)),
         ],
-        compiler_params=pltpu.CompilerParams(vmem_limit_bytes=50 << 20),
+        compiler_params=pltpu.CompilerParams(vmem_limit_bytes=58 << 20),
         cost_estimate=pl.CostEstimate(
             flops=2 * REQS * TOK * depth * WIDTH, bytes_accessed=11 << 20, transcendentals=0
         ),
@@ -179,35 +179,40 @@
     )(wait, from_below, from_above)
 
 
-def add_up(parts):
-    total = parts[0].astype(F32)
-    for k in range(1, SIDE):
-        total = total + parts[k].astype(F32)
-    return total
-
-
-def first_sum_kernel(own_ref, below_ref, above_ref, late_below_ref, late_above_ref, out_ref):
-    for item in range(HALF):
-        out_ref[item] = (
-            own_ref[item] + late_below_ref[item].astype(F32) + above_ref[1, item].astype(F32)
-        ).astype(BF)
-        out_ref[HALF + item] = (
-            own_ref[HALF + item] + below_ref[1, item].astype(F32) + late_above_ref[item].astype(F32)
-        ).astype(BF)
+def first_sum_kernel(
+    own_ref, below_ref, above_ref, late_below_ref, late_above_ref, kept_ref, *out_refs
+):
+    for item in range(SIDE):
+        lane = item % HALF
+        if item < HALF:
+            more = late_below_ref[lane].astype(F32) + above_ref[1, lane].astype(F32)
+        else:
+            more = below_ref[1, lane].astype(F32) + late_above_ref[lane].astype(F32)
+        total = own_ref[item] + more
+        if item == 0:
+            kept_ref[...] = total
+        else:
+            out_refs[item - 1][...] = total.astype(BF)
 
 
 def first_sum(own, below, above, late_below, late_above):
+    share = (WIDTH, PACK)
     return pl.pallas_call(
         first_sum_kernel,
-        out_shape=jax.ShapeDtypeStruct((SIDE, WIDTH, PACK), BF),
+        out_shape=(jax.ShapeDtypeStruct(share, F32),)
+        + (jax.ShapeDtypeStruct(share, BF),) * (SIDE - 1),
         compiler_params=pltpu.CompilerParams(vmem_limit_bytes=8 << 20),
     )(own, below, above, late_below, late_above)
 
 
-def finish_kernel(parts_ref, gain_ref, cosine_ref, sine_ref, valid_ref, out_ref):
+def finish_kernel(
+    kept_ref, one_ref, two_ref, three_ref, gain_ref, cosine_ref, sine_ref, valid_ref, out_ref):
     half = ROPE // 2
     valid = valid_ref[...] > 0
-    total = jnp.where(valid, add_up(parts_ref), 0.0)
+    total = kept_ref[...]
+    for share_ref in (one_ref, two_ref, three_ref):
+        total = total + share_ref[...].astype(F32)
+    total = jnp.where(valid, total, 0.0)
     latent = total[:LAT]
     scaling = lax.rsqrt(jnp.sum(latent * latent, 0, keepdims=True) / LAT + EPS)
     latent = (latent * scaling * gain_ref[...]).astype(BF)
@@ -221,12 +226,12 @@
         out_ref[copy, LAT + half :] = right
 
 
-def finish(parts, gain, cosine, sine, valid):
+def finish(kept, one, two, three, gain, cosine, sine, valid):
     return pl.pallas_call(
         finish_kernel,
         out_shape=jax.ShapeDtypeStruct((SIDE, WIDTH, PACK), BF),
         compiler_params=pltpu.CompilerParams(vmem_limit_bytes=24 << 20),
-    )(parts, gain, cosine, sine, valid)
+    )(kept, one, two, three, gain, cosine, sine, valid)
 
 
 def select_kernel(source_ref, order_ref, near_ref, far_ref, query_ref, out_ref):
@@ -297,25 +302,13 @@
     return jnp.sum(jnp.where(index[..., None] == ids, values, 0), -1)
 
 
-def groups_of(first):
-    found = []
-    for core in range(2):
-        for x in range(SIDE):
-            for other in range(SIDE):
-                ring = []
-                for k in range(SIDE):
-                    y, z = (k, other) if core == first else (other, k)
-                    ring.append(((y * SIDE + z) * SIDE + x) * 2 + core)
-                found.append(ring)
-    return found
-
-
-def neighbours(step):
+def neighbours(step, turn=0):
     pairs = []
     for pre in range(REQS):
         y, z = pre // SIDE, pre % SIDE
         for dec in range(2 * SIDE):
-            ny, nz = ((y + step) % SIDE, z) if dec % 2 == 0 else (y, (z + step) % SIDE)
+            up_y = dec % 2 == turn
+            ny, nz = ((y + step) % SIDE, z) if up_y else (y, (z + step) % SIDE)
             pairs.append((pre * 2 * SIDE + dec, (ny * SIDE + nz) * 2 * SIDE + dec))
     return pairs
 
@@ -345,8 +338,8 @@
     own, up, down = lax.optimization_barrier((own, up, down))
     late_below = lax.ppermute(up, both, neighbours(1))
     late_above = lax.ppermute(down, both, neighbours(-1))
-    packed = first_sum(stage(own), below, above, late_below, late_above)
-    packed = lax.all_to_all(packed, both, 0, 0, tiled=True, axis_index_groups=groups_of(1))
+    kept, *shares = first_sum(stage(own), below, above, late_below, late_above)
+    shares = [lax.ppermute(part, both, neighbours(k + 1, 1)) for k, part in enumerate(shares)]
 
     row = jnp.arange(PACK, dtype=jnp.int32)
     inside = (row >= own_starts[:, None]) & (row < own_ends[:, None])
@@ -357,7 +350,7 @@
     half = ROPE // 2
     frequency = 10000.0 ** (-jnp.arange(half, dtype=F32) * 2.0 / ROPE)
     angles = position[None, :].astype(F32) * frequency[:, None]
-    rows = finish(packed, kv_gain[:, None], jnp.cos(angles), jnp.sin(angles), valid)
+    rows = finish(kept, *shares, kv_gain[:, None], jnp.cos(angles), jnp.sin(angles), valid)
 
     local_queries = queries[0]
     absorbed = jnp.einsum(

time: 138 us -> 137 us (level)
  waiting for transfers between devices: 71.4 us -> 67.4 us
  Pallas kernels: 21.8 us -> 24.4 us
  starting transfers between devices: 24.9 us -> 27.4 us
  local copies, waits for them, and re-layouts: 12.9 us -> 10.8 us
    all_to_all x1 -> x0, waiting for transfers between devices: 11.3 us -> none  [shards(): lax.all_to_all(packed, both, 0, 0, tiled=True, axis_index_groups=groups_o...]
    ppermute x0 -> x3, waiting for transfers between devices: none -> 6.64 us  [shards(): lax.ppermute(part, both, neighbours(k + 1, 1))]
    ppermute x0 -> x3, starting transfers between devices: none -> 6.58 us  [shards(): lax.ppermute(part, both, neighbours(k + 1, 1))]
    all_to_all x1 -> x0, starting transfers between devices: 5.44 us -> none  [shards(): lax.all_to_all(packed, both, 0, 0, tiled=True, axis_index_groups=groups_o...]
    pallas_call x1, Pallas kernels: 10 us -> 11.7 us  [project(): pl.pallas_call(project_kernel, out_shape=(jax.ShapeDtypeStruct(pair, BF),...]
    pallas_call x1, Pallas kernels: 1.22 us -> 2.81 us  [relay(): pl.pallas_call(relay_kernel, out_shape=(shape, shape), compiler_params=pl...]
    unnamed x29 -> x23, local copies, waits for them, and re-layouts: 7.35 us -> 5.9 us
  transfers between devices with their start and end apart: 9 -> 11, of which waited for: 9 -> 10; matrix products, arithmetic and copies ran while one was open for 7% -> 7% of each run, Pallas kernels for 0% -> 0%
where the time goes in v8:
time: 137 us; the launch traced here: 136 us
  waiting for transfers between devices  67.4 us (49%)
  starting transfers between devices  27.4 us (20%)
  Pallas kernels  24.4 us (18%)
  local copies, waits for them, and re-layouts  10.8 us (8%)
  matrix products  2.46 us (2%)
  other arithmetic  2.28 us (2%)
  between operations  1.66 us (1%)
    all_to_all x1, waiting for transfers between devices, shards(): arrived = lax.all_to_all(outgoing, 'pre', 0, 0, tiled=True)  21.3 us
    ppermute x1, waiting for transfers between devices, shards(): below = lax.ppermute(up, both, neighbours(1))  11.9 us
    pallas_call x1, Pallas kernels, project(): pl.pallas_call(project_kernel, out_shape=(jax.ShapeDtypeStruct(pair, BF),...  11.7 us
    all_to_all x1, waiting for transfers between devices, shards(): lax.all_to_all(rows, 'dec', 0, 0, tiled=True, axis_index_groups=along_x)  11.4 us
    all_to_all x1, waiting for transfers between devices, shards(): lax.all_to_all(mixed.reshape(REQS, -1, LAT), 'pre', 0, 0, tiled=True)  8.13 us
    ppermute x3, waiting for transfers between devices, shards(): lax.ppermute(part, both, neighbours(k + 1, 1))  6.64 us
    ppermute x3, starting transfers between devices, shards(): lax.ppermute(part, both, neighbours(k + 1, 1))  6.58 us
    all_to_all x1, starting transfers between devices, shards(): arrived = lax.all_to_all(outgoing, 'pre', 0, 0, tiled=True)  6.31 us
  transfers between devices with their start and end apart: 11, of which 10 were waited for; matrix products, arithmetic and copies ran while one was open for 7% of the time, Pallas kernels for 0%

profile of v8, /device:TPU:0, one launch (start us, length us, event | category | flops | bytes accessed | tf_op | source)
XLA Modules:
  0.0 136.4 jit_solution(1181970954224821638)
XLA Ops:
  0.7 11.7 %shard_map.113 = (bf16[2,2,576,256]{3,2,1,0:T(8,128)(2,1)}, bf16[2,2,576,256]{3,2,1,0:T(8,128)(2,1)}, f32[2,2,576,256]{3,2,1,0:T(8,128)}, f32[4,576,256]{2,1,0:T(8,128)}) custom-call(s32[8,16]{1,0:T(8,128)} %len_ref.1, bf16[448,6144]{1,0:T(8,128)(2,1)} %bitcast.67, bf16[448,576]{1,0:T(8,128)(2,1)} %down_w_ref.1), custom_call_target="tpu_custom_call" | custom-call | flops 3170893824 | bytes 11534336 | tf_op jit(solution)/shard_map/pallas_call | solution.py:119
  12.4 1.7 %collective-permute-start = (bf16[2,2,576,256]{3,2,1,0:T(8,128)(2,1)}, bf16[2,2,576,256]{3,2,1,0:T(8,128)(2,1)}, u32[]{:S(2)}, u32[]{:S(2)}) collective-permute-start(bf16[2,2,576,256]{3,2,1,0:T(8,128)(2,1)} %get-tuple-element.17), channel_id=1, source_target_pairs={{0,32},{1,9},{2,34},{3,11},{4,36},{5,13},{6,38},{7,15},{8,40},{9,1... | collective-permute-start | bytes 3538952 | tf_op jit(solution)/shard_map/ppermute | solution.py:335
  14.1 1.6 %collective-permute-start.1 = (bf16[2,2,576,256]{3,2,1,0:T(8,128)(2,1)}, bf16[2,2,576,256]{3,2,1,0:T(8,128)(2,1)}, u32[]{:S(2)}, u32[]{:S(2)}) collective-permute-start(bf16[2,2,576,256]{3,2,1,0:T(8,128)(2,1)} %get-tuple-element.18), channel_id=1, source_target_pairs={{0,96},{1,25},{2,98},{3,27},{4,100},{5,29},{6,102},{7,31},{8,104},... | collective-permute-start | bytes 3538952 | tf_op jit(solution)/shard_map/ppermute | solution.py:336
  15.9 1.7 %copy-done.3 = f32[2,2,576,256]{3,2,1,0:T(8,128)S(1)} copy-done((f32[2,2,576,256]{3,2,1,0:T(8,128)S(1)}, f32[2,2,576,256]{3,2,1,0:T(8,128)}, u32[]{:S(2)}) %copy-start.3) | copy-done | bytes 2359320
  18.3 11.9 %collective-permute-done.from_below_ref.below_ref = bf16[2,2,576,256]{3,2,1,0:T(8,128)(2,1)} collective-permute-done((bf16[2,2,576,256]{3,2,1,0:T(8,128)(2,1)}, bf16[2,2,576,256]{3,2,1,0:T(8,128)(2,1)}, u32[]{:S(2)}, u32[]{:S(2)}) %collective-permute-start) | collective-permute-done | bytes 1179680 | tf_op jit(solution)/shard_map/ppermute | solution.py:335
  30.6 2.8 %shard_map.115 = (bf16[2,576,256]{2,1,0:T(8,128)(2,1)}, bf16[2,576,256]{2,1,0:T(8,128)(2,1)}) custom-call(f32[2,2,576,256]{3,2,1,0:T(8,128)S(1)} %shard_map.114.wait_ref, bf16[2,2,576,256]{3,2,1,0:T(8,128)(2,1)} %collective-permute-done.from_below_ref.below_ref, bf16[2,2,576,256]{3,2,1,0:T(8,128)(2,1)} %collective-permute-done.1.from_above_ref.above_ref), custom_call_target="tpu_custom_call" | custom-call | tf_op jit(solution)/shard_map/pallas_call | solution.py:175
  33.5 1.6 %collective-permute-start.2 = (bf16[2,576,256]{2,1,0:T(8,128)(2,1)}, bf16[2,576,256]{2,1,0:T(8,128)(2,1)S(1)}, u32[]{:S(2)}, u32[]{:S(2)}) collective-permute-start(bf16[2,576,256]{2,1,0:T(8,128)(2,1)} %get-tuple-element.22), channel_id=1, source_target_pairs={{0,32},{1,9},{2,34},{3,11},{4,36},{5,13},{6,38},{7,15},{8,40},{9,1... | collective-permute-start | bytes 1769480 | tf_op jit(solution)/shard_map/ppermute | solution.py:339
  35.0 1.7 %collective-permute-start.3 = (bf16[2,576,256]{2,1,0:T(8,128)(2,1)}, bf16[2,576,256]{2,1,0:T(8,128)(2,1)S(1)}, u32[]{:S(2)}, u32[]{:S(2)}) collective-permute-start(bf16[2,576,256]{2,1,0:T(8,128)(2,1)} %get-tuple-element.23), channel_id=1, source_target_pairs={{0,96},{1,25},{2,98},{3,27},{4,100},{5,29},{6,102},{7,31},{8,104},... | collective-permute-start | bytes 1769480 | tf_op jit(solution)/shard_map/ppermute | solution.py:340
  37.2 1.7 %copy-done.2 = f32[4,576,256]{2,1,0:T(8,128)S(1)} copy-done((f32[4,576,256]{2,1,0:T(8,128)S(1)}, f32[4,576,256]{2,1,0:T(8,128)}, u32[]{:S(2)}) %copy-start.2) | copy-done | bytes 2359320
  39.1 5.7 %collective-permute-done.2.late_below_ref = bf16[2,576,256]{2,1,0:T(8,128)(2,1)S(1)} collective-permute-done((bf16[2,576,256]{2,1,0:T(8,128)(2,1)}, bf16[2,576,256]{2,1,0:T(8,128)(2,1)S(1)}, u32[]{:S(2)}, u32[]{:S(2)}) %collective-permute-start.2) | collective-permute-done | bytes 589856 | tf_op jit(solution)/shard_map/ppermute | solution.py:339
  45.1 2.0 %shard_map.117 = (f32[576,256]{1,0:T(8,128)S(1)}, bf16[576,256]{1,0:T(8,128)(2,1)S(1)}, bf16[576,256]{1,0:T(8,128)(2,1)S(1)}, bf16[576,256]{1,0:T(8,128)(2,1)S(1)}) custom-call(f32[4,576,256]{2,1,0:T(8,128)S(1)} %shard_map.116.own_ref, bf16[2,2,576,256]{3,2,1,0:T(8,128)(2,1)} %collective-permute-done.from_below_ref.below_ref, ...), custom_call_target="tpu_custom_call" | custom-call | tf_op jit(solution)/shard_map/pallas_call | solution.py:200
  47.1 2.0 %collective-permute-start.4 = (bf16[576,256]{1,0:T(8,128)(2,1)S(1)}, bf16[576,256]{1,0:T(8,128)(2,1)S(1)}, u32[]{:S(2)}, u32[]{:S(2)}) collective-permute-start(bf16[576,256]{1,0:T(8,128)(2,1)S(1)} %get-tuple-element.25), channel_id=1, source_target_pairs={{0,8},{1,33},{2,10},{3,35},{4,12},{5,37},{6,14},{7,39},{8,16},{9,4... | collective-permute-start | bytes 884744 | tf_op jit(solution)/shard_map/ppermute | solution.py:342
  49.1 3.6 %collective-permute-start.5 = (bf16[576,256]{1,0:T(8,128)(2,1)S(1)}, bf16[576,256]{1,0:T(8,128)(2,1)S(1)}, u32[]{:S(2)}, u32[]{:S(2)}) collective-permute-start(bf16[576,256]{1,0:T(8,128)(2,1)S(1)} %get-tuple-element.26), channel_id=1, source_target_pairs={{0,16},{1,65},{2,18},{3,67},{4,20},{5,69},{6,22},{7,71},{8,24},{9,... | collective-permute-start | bytes 884744 | tf_op jit(solution)/shard_map/ppermute | solution.py:342
  52.7 1.0 collective-permute-start.6
  53.9 2.0 %collective-permute-done.4.one_ref = bf16[576,256]{1,0:T(8,128)(2,1)S(1)} collective-permute-done((bf16[576,256]{1,0:T(8,128)(2,1)S(1)}, bf16[576,256]{1,0:T(8,128)(2,1)S(1)}, u32[]{:S(2)}, u32[]{:S(2)}) %collective-permute-start.4) | collective-permute-done | bytes 294944 | tf_op jit(solution)/shard_map/ppermute | solution.py:342
  55.9 4.6 %collective-permute-done.5.two_ref = bf16[576,256]{1,0:T(8,128)(2,1)S(1)} collective-permute-done((bf16[576,256]{1,0:T(8,128)(2,1)S(1)}, bf16[576,256]{1,0:T(8,128)(2,1)S(1)}, u32[]{:S(2)}, u32[]{:S(2)}) %collective-permute-start.5) | collective-permute-done | bytes 294944 | tf_op jit(solution)/shard_map/ppermute | solution.py:342
  60.5 1.4 %shard_map.118 = bf16[4,576,256]{2,1,0:T(8,128)(2,1)} custom-call(f32[576,256]{1,0:T(8,128)S(1)} %get-tuple-element.24.kept_ref, bf16[576,256]{1,0:T(8,128)(2,1)S(1)} %collective-permute-done.4.one_ref, bf16[576,256]{1,0:T(8,128)(2,1)S(1)} %collective-permute-done.5.two_ref, bf16[576,256]{1,0:T(8,128)(2,1)S(1)} %collective-permute-done.6.three_ref, ...), custom_call_target="tpu_custom_call" | custom-call | tf_op jit(solution)/shard_map/pallas_call | solution.py:230
  61.9 4.4 %all-to-all-start = ((bf16[4,576,256]{2,1,0:T(8,128)(2,1)}), bf16[4,576,256]{2,1,0:T(8,128)(2,1)S(1)}, u32[]{:S(2)}, u32[]{:S(2)}) async-start(bf16[4,576,256]{2,1,0:T(8,128)(2,1)} %shard_map.118), calls=%async_computation | async-start | bytes 2359296 | tf_op jit(solution)/shard_map/all_to_all | solution.py:363
  68.0 11.4 %all-to-all-done.near_ref = bf16[4,576,256]{2,1,0:T(8,128)(2,1)S(1)} async-done(((bf16[4,576,256]{2,1,0:T(8,128)(2,1)}), bf16[4,576,256]{2,1,0:T(8,128)(2,1)S(1)}, u32[]{:S(2)}, u32[]{:S(2)}) %all-to-all-start) | async-done | bytes 1179680 | tf_op jit(solution)/shard_map/all_to_all | solution.py:363
  80.8 1.6 %collective-permute-done.7.far_ref = bf16[4,576,256]{2,1,0:T(8,128)(2,1)} collective-permute-done((bf16[4,576,256]{2,1,0:T(8,128)(2,1)S(1)}, bf16[4,576,256]{2,1,0:T(8,128)(2,1)}, u32[]{:S(2)}, u32[]{:S(2)}) %collective-permute-start.7) | collective-permute-done | bytes 1179680 | tf_op jit(solution)/shard_map/ppermute | solution.py:364
  82.4 3.3 %shard_map.119 = bf16[16,80,576]{2,1,0:T(8,128)(2,1)S(1)} custom-call(s32[2,384]{1,0:T(2,128)S(1)} %pad_add_fusion.1.source_ref, s32[768,1]{1,0:T(8,128)S(1)} %reshape.446.order_ref, bf16[4,576,256]{2,1,0:T(8,128)(2,1)S(1)} %all-to-all-done.near_ref, bf16[4,576,256]{2,1,0:T(8,128)(2,1)} %collective-permute-done.7.far_ref, bf16[16,32,576]{2,1,0:T(8,128)(2,1)S(1)} %bitcast.57), custom_call_target="tpu_custom_call" | custom-call | tf_op jit(solution)/shard_map/pallas_call | solution.py:255
  85.7 1.2 copy-done.1
  86.9 6.3 %all-to-all-start.1 = ((bf16[16,80,576]{2,1,0:T(8,128)(2,1)}), bf16[16,80,576]{2,1,0:T(8,128)(2,1)S(1)}, u32[]{:S(2)}, u32[]{:S(2)}) async-start(bf16[16,80,576]{2,1,0:T(8,128)(2,1)} %copy-done.1), calls=%async_computation.1 | async-start | bytes 3276800 | tf_op jit(solution)/shard_map/all_to_all | solution.py:385
  95.5 0.8 fusion.9
  96.3 0.7 dynamic-slice_bitcast_fusion
  97.1 21.3 %all-to-all-done.1.arrived_ref = bf16[16,80,576]{2,1,0:T(8,128)(2,1)S(1)} async-done(((bf16[16,80,576]{2,1,0:T(8,128)(2,1)}), bf16[16,80,576]{2,1,0:T(8,128)(2,1)S(1)}, u32[]{:S(2)}, u32[]{:S(2)}) %all-to-all-start.1) | async-done | bytes 1474592 | tf_op jit(solution)/shard_map/all_to_all | solution.py:385
  118.4 2.9 %shard_map.120 = bf16[512,512]{1,0:T(8,128)(2,1)} custom-call(bf16[16,80,576]{2,1,0:T(8,128)(2,1)S(1)} %all-to-all-done.1.arrived_ref, bf16[16,576]{1,0:T(8,128)(2,1)S(1)} %pad.5.fresh_ref, s32[1,384]{1,0:T(1,128)S(1)} %reshape.443.live_ref), custom_call_target="tpu_custom_call" | custom-call | tf_op jit(solution)/shard_map/pallas_call | solution.py:293
  121.3 3.6 %all-to-all-start.2 = ((bf16[16,32,512]{2,1,0:T(8,128)(2,1)}), bf16[16,32,512]{2,1,0:T(8,128)(2,1)S(1)}, u32[]{:S(2)}, u32[]{:S(2)}) async-start(bf16[16,32,512]{2,1,0:T(8,128)(2,1)} %bitcast.22), calls=%async_computation.2 | async-start | bytes 1048576 | tf_op jit(solution)/shard_map/all_to_all | solution.py:410
  125.4 1.4 %fusion.1 = bf16[1,384,576]{1,2,0:T(8,128)(2,1)} fusion(bf16[768,576]{1,0:T(8,128)(2,1)S(1)} %bitcast.60, s32[768]{0:T(1024)S(1)} %eq.106), kind=kOutput, calls=%fused_computation.3 | convolution fusion | flops 340254720 | bytes 1330176 | tf_op jit(solution)/shard_map/dot_general | solution.py:400
  126.8 8.1 %all-to-all-done.2 = bf16[16,32,512]{2,1,0:T(8,128)(2,1)S(1)} async-done(((bf16[16,32,512]{2,1,0:T(8,128)(2,1)}), bf16[16,32,512]{2,1,0:T(8,128)(2,1)S(1)}, u32[]{:S(2)}, u32[]{:S(2)}) %all-to-all-start.2) | async-done | bytes 524320 | tf_op jit(solution)/shard_map/all_to_all | solution.py:410
  135.0 0.7 fusion.2
  135.7 0.8 copy.68
  (97 shorter events, 7.8 us)
Async XLA Ops:
  0.6 79.4 %copy-start = (bf16[8,128,512]{2,1,0:T(8,128)(2,1)S(1)}, bf16[8,128,512]{2,1,0:T(8,128)(2,1)}, u32[]{:S(2)}) copy-start(bf16[8,128,512]{2,1,0:T(8,128)(2,1)} %param.13) | copy-start | bytes 3145732
  0.6 15.0 %copy-start.6 = (s32[8,16]{1,0:T(8,128)S(1)}, s32[8,16]{1,0:T(8,128)}, u32[]{:S(2)}) copy-start(s32[8,16]{1,0:T(8,128)} %len_ref.1) | copy-start | bytes 1540
  12.4 17.8 %collective-permute-start = (bf16[2,2,576,256]{3,2,1,0:T(8,128)(2,1)}, bf16[2,2,576,256]{3,2,1,0:T(8,128)(2,1)}, u32[]{:S(2)}, u32[]{:S(2)}) collective-permute-start(bf16[2,2,576,256]{3,2,1,0:T(8,128)(2,1)} %get-tuple-element.17), channel_id=1, source_target_pairs={{0,32},{1,9},{2,34},{3,11},{4,36},{5,13},{6,38},{7,15},{8,40},{9,1... | collective-permute-start | bytes 3538952 | tf_op jit(solution)/shard_map/ppermute | solution.py:335
  14.1 16.5 %collective-permute-start.1 = (bf16[2,2,576,256]{3,2,1,0:T(8,128)(2,1)}, bf16[2,2,576,256]{3,2,1,0:T(8,128)(2,1)}, u32[]{:S(2)}, u32[]{:S(2)}) collective-permute-start(bf16[2,2,576,256]{3,2,1,0:T(8,128)(2,1)} %get-tuple-element.18), channel_id=1, source_target_pairs={{0,96},{1,25},{2,98},{3,27},{4,100},{5,29},{6,102},{7,31},{8,104},... | collective-permute-start | bytes 3538952 | tf_op jit(solution)/shard_map/ppermute | solution.py:336
  15.9 1.7 %copy-start.3 = (f32[2,2,576,256]{3,2,1,0:T(8,128)S(1)}, f32[2,2,576,256]{3,2,1,0:T(8,128)}, u32[]{:S(2)}) copy-start(f32[2,2,576,256]{3,2,1,0:T(8,128)} %get-tuple-element.16.share_ref) | copy-start | bytes 7077892
  17.5 0.7 copy-start.8
  18.3 18.6 %copy-start.7 = (f32[512]{0:T(512)S(1)}, f32[512]{0:T(512)}, u32[]{:S(2)}) copy-start(f32[512]{0:T(512)} %param.12) | copy-start | bytes 6148
  33.5 11.3 %collective-permute-start.2 = (bf16[2,576,256]{2,1,0:T(8,128)(2,1)}, bf16[2,576,256]{2,1,0:T(8,128)(2,1)S(1)}, u32[]{:S(2)}, u32[]{:S(2)}) collective-permute-start(bf16[2,576,256]{2,1,0:T(8,128)(2,1)} %get-tuple-element.22), channel_id=1, source_target_pairs={{0,32},{1,9},{2,34},{3,11},{4,36},{5,13},{6,38},{7,15},{8,40},{9,1... | collective-permute-start | bytes 1769480 | tf_op jit(solution)/shard_map/ppermute | solution.py:339
  35.0 10.1 %collective-permute-start.3 = (bf16[2,576,256]{2,1,0:T(8,128)(2,1)}, bf16[2,576,256]{2,1,0:T(8,128)(2,1)S(1)}, u32[]{:S(2)}, u32[]{:S(2)}) collective-permute-start(bf16[2,576,256]{2,1,0:T(8,128)(2,1)} %get-tuple-element.23), channel_id=1, source_target_pairs={{0,96},{1,25},{2,98},{3,27},{4,100},{5,29},{6,102},{7,31},{8,104},... | collective-permute-start | bytes 1769480 | tf_op jit(solution)/shard_map/ppermute | solution.py:340
  37.2 1.7 %copy-start.2 = (f32[4,576,256]{2,1,0:T(8,128)S(1)}, f32[4,576,256]{2,1,0:T(8,128)}, u32[]{:S(2)}) copy-start(f32[4,576,256]{2,1,0:T(8,128)} %get-tuple-element.21.share_ref) | copy-start | bytes 7077892
  47.1 8.8 %collective-permute-start.4 = (bf16[576,256]{1,0:T(8,128)(2,1)S(1)}, bf16[576,256]{1,0:T(8,128)(2,1)S(1)}, u32[]{:S(2)}, u32[]{:S(2)}) collective-permute-start(bf16[576,256]{1,0:T(8,128)(2,1)S(1)} %get-tuple-element.25), channel_id=1, source_target_pairs={{0,8},{1,33},{2,10},{3,35},{4,12},{5,37},{6,14},{7,39},{8,16},{9,4... | collective-permute-start | bytes 884744 | tf_op jit(solution)/shard_map/ppermute | solution.py:342
  49.1 11.4 %collective-permute-start.5 = (bf16[576,256]{1,0:T(8,128)(2,1)S(1)}, bf16[576,256]{1,0:T(8,128)(2,1)S(1)}, u32[]{:S(2)}, u32[]{:S(2)}) collective-permute-start(bf16[576,256]{1,0:T(8,128)(2,1)S(1)} %get-tuple-element.26), channel_id=1, source_target_pairs={{0,16},{1,65},{2,18},{3,67},{4,20},{5,69},{6,22},{7,71},{8,24},{9,... | collective-permute-start | bytes 884744 | tf_op jit(solution)/shard_map/ppermute | solution.py:342
  52.7 7.9 %collective-permute-start.6 = (bf16[576,256]{1,0:T(8,128)(2,1)S(1)}, bf16[576,256]{1,0:T(8,128)(2,1)S(1)}, u32[]{:S(2)}, u32[]{:S(2)}) collective-permute-start(bf16[576,256]{1,0:T(8,128)(2,1)S(1)} %get-tuple-element.27), channel_id=1, source_target_pairs={{0,24},{1,97},{2,26},{3,99},{4,28},{5,101},{6,30},{7,103},{8,0},{9... | collective-permute-start | bytes 884744 | tf_op jit(solution)/shard_map/ppermute | solution.py:342
  61.9 5.3 %copy-start.9 = (s32[1,96]{1,0:T(1,128)S(1)}, s32[1,96]{1,0:T(1,128)}, u32[]{:S(2)}) copy-start(s32[1,96]{1,0:T(1,128)} %param.19) | copy-start | bytes 1156
  61.9 17.9 %copy-start.5 = (bf16[1,16,4,8,192]{4,3,2,1,0:T(8,128)(2,1)S(1)}, bf16[1,16,4,8,192]{4,3,2,1,0:T(8,128)(2,1)}, u32[]{:S(2)}) copy-start(bf16[1,16,4,8,192]{4,3,2,1,0:T(8,128)(2,1)} %param.15) | copy-start | bytes 589828
  61.9 17.5 %all-to-all-start = ((bf16[4,576,256]{2,1,0:T(8,128)(2,1)}), bf16[4,576,256]{2,1,0:T(8,128)(2,1)S(1)}, u32[]{:S(2)}, u32[]{:S(2)}) async-start(bf16[4,576,256]{2,1,0:T(8,128)(2,1)} %shard_map.118), calls=%async_computation | async-start | bytes 2359296 | tf_op jit(solution)/shard_map/all_to_all | solution.py:363
  79.4 3.0 %collective-permute-start.7 = (bf16[4,576,256]{2,1,0:T(8,128)(2,1)S(1)}, bf16[4,576,256]{2,1,0:T(8,128)(2,1)}, u32[]{:S(2)}, u32[]{:S(2)}) collective-permute-start(bf16[4,576,256]{2,1,0:T(8,128)(2,1)S(1)} %all-to-all-done.near_ref), channel_id=1, source_target_pairs={{0,1},{1,0},{2,3},{3,2},{4,5},{5,4},{6,7},{7,6},{8,9},{9,8},{10,11... | collective-permute-start | bytes 3538952 | tf_op jit(solution)/shard_map/ppermute | solution.py:364
  85.7 1.2 copy-start.1
  86.9 31.5 %all-to-all-start.1 = ((bf16[16,80,576]{2,1,0:T(8,128)(2,1)}), bf16[16,80,576]{2,1,0:T(8,128)(2,1)S(1)}, u32[]{:S(2)}, u32[]{:S(2)}) async-start(bf16[16,80,576]{2,1,0:T(8,128)(2,1)} %copy-done.1), calls=%async_computation.1 | async-start | bytes 3276800 | tf_op jit(solution)/shard_map/all_to_all | solution.py:385
  121.3 13.7 %all-to-all-start.2 = ((bf16[16,32,512]{2,1,0:T(8,128)(2,1)}), bf16[16,32,512]{2,1,0:T(8,128)(2,1)S(1)}, u32[]{:S(2)}, u32[]{:S(2)}) async-start(bf16[16,32,512]{2,1,0:T(8,128)(2,1)} %bitcast.22), calls=%async_computation.2 | async-start | bytes 1048576 | tf_op jit(solution)/shard_map/all_to_all | solution.py:410
  125.4 9.6 %copy-start.4 = (bf16[8,512,128]{2,1,0:T(8,128)(2,1)S(1)}, bf16[8,512,128]{2,1,0:T(8,128)(2,1)}, u32[]{:S(2)}) copy-start(bf16[8,512,128]{2,1,0:T(8,128)(2,1)} %param.14) | copy-start | bytes 3145732

commit v9 on v8

--- a/solution.py
+++ b/solution.py
@@ -32,11 +32,18 @@
 
 def project_kernel(
     len_ref, hid_ref, down_w_ref, up_ref, down_ref, wait_ref, own_ref,
-    span_ref, shift_ref, turned_ref, hold_ref, wait_hold_ref, own_hold_ref, in_sem, out_sem,
+    span_ref, shift_ref, turned_ref, hold_ref, wait_hold_ref, own_hold_ref, up_hold_ref,
+    down_hold_ref, in_sem, out_sem, up_sem, down_sem,
 ):
     def load(part):
         where = pl.ds(part * PAIR * TOK, PAIR * TOK)
         return pltpu.make_async_copy(hid_ref.at[:, where], span_ref.at[:, where], in_sem.at[part])
+
+    def go(step, lane, up):
+        hold, out, sem = (
+            (up_hold_ref, up_ref, up_sem) if up else (down_hold_ref, down_ref, down_sem)
+        )
+        return pltpu.make_async_copy(hold.at[step, lane], out.at[step, lane], sem.at[step, lane])
 
     keep_own = pltpu.make_async_copy(own_hold_ref, own_ref, out_sem.at[0])
     keep_wait = pltpu.make_async_copy(wait_hold_ref, wait_ref, out_sem.at[1])
@@ -93,23 +100,31 @@
             if away == 0:
                 own_hold_ref[item] = part
             elif away == 1 and late:
-                up_ref[1, lane] = part.astype(BF)
+                up_hold_ref[1, lane] = part.astype(BF)
+                go(1, lane, True).start()
             elif away == 1:
                 wait_hold_ref[0, lane] = part
             elif away == 3 and late:
                 wait_hold_ref[1, lane] = part
             elif away == 3:
-                down_ref[1, lane] = part.astype(BF)
+                down_hold_ref[1, lane] = part.astype(BF)
+                go(1, lane, False).start()
             elif late:
-                down_ref[0, lane] = part.astype(BF)
+                down_hold_ref[0, lane] = part.astype(BF)
+                go(0, lane, False).start()
             else:
-                up_ref[0, lane] = part.astype(BF)
+                up_hold_ref[0, lane] = part.astype(BF)
+                go(0, lane, True).start()
         if away == 0:
             keep_own.start()
         elif away == 3:
             keep_wait.start()
     keep_own.wait()
     keep_wait.wait()
+    for step in range(2):
+        for lane in range(HALF):
+            go(step, lane, True).wait()
+            go(step, lane, False).wait()
 
 
 def project(lengths, hidden_t, kv_down):
@@ -129,7 +144,7 @@
             pl.BlockSpec(memory_space=pl.ANY),
             vmem,
         ],
-        out_specs=(vmem, vmem, pl.BlockSpec(memory_space=pl.ANY), pl.BlockSpec(memory_space=pl.ANY)),
+        out_specs=(pl.BlockSpec(memory_space=pl.ANY),) * 4,
         scratch_shapes=[
             pltpu.VMEM((depth, REQS * TOK), BF),
             pltpu.VMEM((REQS, 24, 256), jnp.int32),
@@ -137,8 +152,12 @@
             pltpu.VMEM((REQS, HOLD, depth), F32),
             pltpu.VMEM(pair, F32),
             pltpu.VMEM((SIDE, WIDTH, PACK), F32),
+            pltpu.VMEM(pair, BF),
+            pltpu.VMEM(pair, BF),
             pltpu.SemaphoreType.DMA((REQS // PAIR,)),
             pltpu.SemaphoreType.DMA((2,)),
+            pltpu.SemaphoreType.DMA((2, HALF)),
+            pltpu.SemaphoreType.DMA((2, HALF)),
         ],
         compiler_params=pltpu.CompilerParams(vmem_limit_bytes=58 << 20),
         cost_estimate=pl.CostEstimate(

time: 137 us -> 137 us (level)
  no operation moved by 1% of the time
where the time goes in v9:
time: 137 us; the launch traced here: 136 us
  waiting for transfers between devices  67.4 us (49%)
  starting transfers between devices  27.5 us (20%)
  Pallas kernels  24.1 us (18%)
  local copies, waits for them, and re-layouts  10.8 us (8%)
  matrix products  2.46 us (2%)
  other arithmetic  2.28 us (2%)
  between operations  1.66 us (1%)
    all_to_all x1, waiting for transfers between devices, shards(): arrived = lax.all_to_all(outgoing, 'pre', 0, 0, tiled=True)  21.3 us
    ppermute x1, waiting for transfers between devices, shards(): below = lax.ppermute(up, both, neighbours(1))  11.9 us
    all_to_all x1, waiting for transfers between devices, shards(): lax.all_to_all(rows, 'dec', 0, 0, tiled=True, axis_index_groups=along_x)  11.4 us
    pallas_call x1, Pallas kernels, project(): pl.pallas_call(project_kernel, out_shape=(jax.ShapeDtypeStruct(pair, BF),...  11.4 us
    all_to_all x1, waiting for transfers between devices, shards(): lax.all_to_all(mixed.reshape(REQS, -1, LAT), 'pre', 0, 0, tiled=True)  8.13 us
    ppermute x3, waiting for transfers between devices, shards(): lax.ppermute(part, both, neighbours(k + 1, 1))  6.64 us
    ppermute x3, starting transfers between devices, shards(): lax.ppermute(part, both, neighbours(k + 1, 1))  6.58 us
    all_to_all x1, starting transfers between devices, shards(): arrived = lax.all_to_all(outgoing, 'pre', 0, 0, tiled=True)  6.31 us
  transfers between devices with their start and end apart: 11, of which 10 were waited for; matrix products, arithmetic and copies ran while one was open for 7% of the time, Pallas kernels for 0%

profile of v9, /device:TPU:0, one launch (start us, length us, event | category | flops | bytes accessed | tf_op | source)
XLA Modules:
  0.0 136.1 jit_solution(574240461480893786)
XLA Ops:
  0.7 11.4 %shard_map.113 = (bf16[2,2,576,256]{3,2,1,0:T(8,128)(2,1)}, bf16[2,2,576,256]{3,2,1,0:T(8,128)(2,1)}, f32[2,2,576,256]{3,2,1,0:T(8,128)}, f32[4,576,256]{2,1,0:T(8,128)}) custom-call(s32[8,16]{1,0:T(8,128)} %len_ref.1, bf16[448,6144]{1,0:T(8,128)(2,1)} %bitcast.67, bf16[448,576]{1,0:T(8,128)(2,1)} %down_w_ref.1), custom_call_target="tpu_custom_call" | custom-call | flops 3170893824 | bytes 11534336 | tf_op jit(solution)/shard_map/pallas_call | solution.py:134
  12.1 1.7 %collective-permute-start = (bf16[2,2,576,256]{3,2,1,0:T(8,128)(2,1)}, bf16[2,2,576,256]{3,2,1,0:T(8,128)(2,1)}, u32[]{:S(2)}, u32[]{:S(2)}) collective-permute-start(bf16[2,2,576,256]{3,2,1,0:T(8,128)(2,1)} %get-tuple-element.17), channel_id=1, source_target_pairs={{0,32},{1,9},{2,34},{3,11},{4,36},{5,13},{6,38},{7,15},{8,40},{9,1... | collective-permute-start | bytes 3538952 | tf_op jit(solution)/shard_map/ppermute | solution.py:354
  13.8 1.6 %collective-permute-start.1 = (bf16[2,2,576,256]{3,2,1,0:T(8,128)(2,1)}, bf16[2,2,576,256]{3,2,1,0:T(8,128)(2,1)}, u32[]{:S(2)}, u32[]{:S(2)}) collective-permute-start(bf16[2,2,576,256]{3,2,1,0:T(8,128)(2,1)} %get-tuple-element.18), channel_id=1, source_target_pairs={{0,96},{1,25},{2,98},{3,27},{4,100},{5,29},{6,102},{7,31},{8,104},... | collective-permute-start | bytes 3538952 | tf_op jit(solution)/shard_map/ppermute | solution.py:355
  15.6 1.7 %copy-done.3 = f32[2,2,576,256]{3,2,1,0:T(8,128)S(1)} copy-done((f32[2,2,576,256]{3,2,1,0:T(8,128)S(1)}, f32[2,2,576,256]{3,2,1,0:T(8,128)}, u32[]{:S(2)}) %copy-start.3) | copy-done | bytes 2359320
  18.0 11.9 %collective-permute-done.from_below_ref.below_ref = bf16[2,2,576,256]{3,2,1,0:T(8,128)(2,1)} collective-permute-done((bf16[2,2,576,256]{3,2,1,0:T(8,128)(2,1)}, bf16[2,2,576,256]{3,2,1,0:T(8,128)(2,1)}, u32[]{:S(2)}, u32[]{:S(2)}) %collective-permute-start) | collective-permute-done | bytes 1179680 | tf_op jit(solution)/shard_map/ppermute | solution.py:354
  30.3 2.8 %shard_map.115 = (bf16[2,576,256]{2,1,0:T(8,128)(2,1)}, bf16[2,576,256]{2,1,0:T(8,128)(2,1)}) custom-call(f32[2,2,576,256]{3,2,1,0:T(8,128)S(1)} %shard_map.114.wait_ref, bf16[2,2,576,256]{3,2,1,0:T(8,128)(2,1)} %collective-permute-done.from_below_ref.below_ref, bf16[2,2,576,256]{3,2,1,0:T(8,128)(2,1)} %collective-permute-done.1.from_above_ref.above_ref), custom_call_target="tpu_custom_call" | custom-call | tf_op jit(solution)/shard_map/pallas_call | solution.py:194
  33.1 1.6 %collective-permute-start.2 = (bf16[2,576,256]{2,1,0:T(8,128)(2,1)}, bf16[2,576,256]{2,1,0:T(8,128)(2,1)S(1)}, u32[]{:S(2)}, u32[]{:S(2)}) collective-permute-start(bf16[2,576,256]{2,1,0:T(8,128)(2,1)} %get-tuple-element.22), channel_id=1, source_target_pairs={{0,32},{1,9},{2,34},{3,11},{4,36},{5,13},{6,38},{7,15},{8,40},{9,1... | collective-permute-start | bytes 1769480 | tf_op jit(solution)/shard_map/ppermute | solution.py:358
  34.7 1.7 %collective-permute-start.3 = (bf16[2,576,256]{2,1,0:T(8,128)(2,1)}, bf16[2,576,256]{2,1,0:T(8,128)(2,1)S(1)}, u32[]{:S(2)}, u32[]{:S(2)}) collective-permute-start(bf16[2,576,256]{2,1,0:T(8,128)(2,1)} %get-tuple-element.23), channel_id=1, source_target_pairs={{0,96},{1,25},{2,98},{3,27},{4,100},{5,29},{6,102},{7,31},{8,104},... | collective-permute-start | bytes 1769480 | tf_op jit(solution)/shard_map/ppermute | solution.py:359
  36.9 1.7 %copy-done.2 = f32[4,576,256]{2,1,0:T(8,128)S(1)} copy-done((f32[4,576,256]{2,1,0:T(8,128)S(1)}, f32[4,576,256]{2,1,0:T(8,128)}, u32[]{:S(2)}) %copy-start.2) | copy-done | bytes 2359320
  38.8 5.7 %collective-permute-done.2.late_below_ref = bf16[2,576,256]{2,1,0:T(8,128)(2,1)S(1)} collective-permute-done((bf16[2,576,256]{2,1,0:T(8,128)(2,1)}, bf16[2,576,256]{2,1,0:T(8,128)(2,1)S(1)}, u32[]{:S(2)}, u32[]{:S(2)}) %collective-permute-start.2) | collective-permute-done | bytes 589856 | tf_op jit(solution)/shard_map/ppermute | solution.py:358
  44.8 2.0 %shard_map.117 = (f32[576,256]{1,0:T(8,128)S(1)}, bf16[576,256]{1,0:T(8,128)(2,1)S(1)}, bf16[576,256]{1,0:T(8,128)(2,1)S(1)}, bf16[576,256]{1,0:T(8,128)(2,1)S(1)}) custom-call(f32[4,576,256]{2,1,0:T(8,128)S(1)} %shard_map.116.own_ref, bf16[2,2,576,256]{3,2,1,0:T(8,128)(2,1)} %collective-permute-done.from_below_ref.below_ref, ...), custom_call_target="tpu_custom_call" | custom-call | tf_op jit(solution)/shard_map/pallas_call | solution.py:219
  46.8 2.0 %collective-permute-start.4 = (bf16[576,256]{1,0:T(8,128)(2,1)S(1)}, bf16[576,256]{1,0:T(8,128)(2,1)S(1)}, u32[]{:S(2)}, u32[]{:S(2)}) collective-permute-start(bf16[576,256]{1,0:T(8,128)(2,1)S(1)} %get-tuple-element.25), channel_id=1, source_target_pairs={{0,8},{1,33},{2,10},{3,35},{4,12},{5,37},{6,14},{7,39},{8,16},{9,4... | collective-permute-start | bytes 884744 | tf_op jit(solution)/shard_map/ppermute | solution.py:361
  48.8 3.6 %collective-permute-start.5 = (bf16[576,256]{1,0:T(8,128)(2,1)S(1)}, bf16[576,256]{1,0:T(8,128)(2,1)S(1)}, u32[]{:S(2)}, u32[]{:S(2)}) collective-permute-start(bf16[576,256]{1,0:T(8,128)(2,1)S(1)} %get-tuple-element.26), channel_id=1, source_target_pairs={{0,16},{1,65},{2,18},{3,67},{4,20},{5,69},{6,22},{7,71},{8,24},{9,... | collective-permute-start | bytes 884744 | tf_op jit(solution)/shard_map/ppermute | solution.py:361
  52.4 1.0 collective-permute-start.6
  53.6 2.0 %collective-permute-done.4.one_ref = bf16[576,256]{1,0:T(8,128)(2,1)S(1)} collective-permute-done((bf16[576,256]{1,0:T(8,128)(2,1)S(1)}, bf16[576,256]{1,0:T(8,128)(2,1)S(1)}, u32[]{:S(2)}, u32[]{:S(2)}) %collective-permute-start.4) | collective-permute-done | bytes 294944 | tf_op jit(solution)/shard_map/ppermute | solution.py:361
  55.6 4.6 %collective-permute-done.5.two_ref = bf16[576,256]{1,0:T(8,128)(2,1)S(1)} collective-permute-done((bf16[576,256]{1,0:T(8,128)(2,1)S(1)}, bf16[576,256]{1,0:T(8,128)(2,1)S(1)}, u32[]{:S(2)}, u32[]{:S(2)}) %collective-permute-start.5) | collective-permute-done | bytes 294944 | tf_op jit(solution)/shard_map/ppermute | solution.py:361
  60.2 1.4 %shard_map.118 = bf16[4,576,256]{2,1,0:T(8,128)(2,1)} custom-call(f32[576,256]{1,0:T(8,128)S(1)} %get-tuple-element.24.kept_ref, bf16[576,256]{1,0:T(8,128)(2,1)S(1)} %collective-permute-done.4.one_ref, bf16[576,256]{1,0:T(8,128)(2,1)S(1)} %collective-permute-done.5.two_ref, bf16[576,256]{1,0:T(8,128)(2,1)S(1)} %collective-permute-done.6.three_ref, ...), custom_call_target="tpu_custom_call" | custom-call | tf_op jit(solution)/shard_map/pallas_call | solution.py:249
  61.6 4.4 %all-to-all-start = ((bf16[4,576,256]{2,1,0:T(8,128)(2,1)}), bf16[4,576,256]{2,1,0:T(8,128)(2,1)S(1)}, u32[]{:S(2)}, u32[]{:S(2)}) async-start(bf16[4,576,256]{2,1,0:T(8,128)(2,1)} %shard_map.118), calls=%async_computation | async-start | bytes 2359296 | tf_op jit(solution)/shard_map/all_to_all | solution.py:382
  67.7 11.4 %all-to-all-done.near_ref = bf16[4,576,256]{2,1,0:T(8,128)(2,1)S(1)} async-done(((bf16[4,576,256]{2,1,0:T(8,128)(2,1)}), bf16[4,576,256]{2,1,0:T(8,128)(2,1)S(1)}, u32[]{:S(2)}, u32[]{:S(2)}) %all-to-all-start) | async-done | bytes 1179680 | tf_op jit(solution)/shard_map/all_to_all | solution.py:382
  80.5 1.6 %collective-permute-done.7.far_ref = bf16[4,576,256]{2,1,0:T(8,128)(2,1)} collective-permute-done((bf16[4,576,256]{2,1,0:T(8,128)(2,1)S(1)}, bf16[4,576,256]{2,1,0:T(8,128)(2,1)}, u32[]{:S(2)}, u32[]{:S(2)}) %collective-permute-start.7) | collective-permute-done | bytes 1179680 | tf_op jit(solution)/shard_map/ppermute | solution.py:383
  82.1 3.3 %shard_map.119 = bf16[16,80,576]{2,1,0:T(8,128)(2,1)S(1)} custom-call(s32[2,384]{1,0:T(2,128)S(1)} %pad_add_fusion.1.source_ref, s32[768,1]{1,0:T(8,128)S(1)} %reshape.446.order_ref, bf16[4,576,256]{2,1,0:T(8,128)(2,1)S(1)} %all-to-all-done.near_ref, bf16[4,576,256]{2,1,0:T(8,128)(2,1)} %collective-permute-done.7.far_ref, bf16[16,32,576]{2,1,0:T(8,128)(2,1)S(1)} %bitcast.57), custom_call_target="tpu_custom_call" | custom-call | tf_op jit(solution)/shard_map/pallas_call | solution.py:274
  85.4 1.2 copy-done.1
  86.6 6.3 %all-to-all-start.1 = ((bf16[16,80,576]{2,1,0:T(8,128)(2,1)}), bf16[16,80,576]{2,1,0:T(8,128)(2,1)S(1)}, u32[]{:S(2)}, u32[]{:S(2)}) async-start(bf16[16,80,576]{2,1,0:T(8,128)(2,1)} %copy-done.1), calls=%async_computation.1 | async-start | bytes 3276800 | tf_op jit(solution)/shard_map/all_to_all | solution.py:404
  95.2 0.8 fusion.9
  96.0 0.7 dynamic-slice_bitcast_fusion
  96.8 21.3 %all-to-all-done.1.arrived_ref = bf16[16,80,576]{2,1,0:T(8,128)(2,1)S(1)} async-done(((bf16[16,80,576]{2,1,0:T(8,128)(2,1)}), bf16[16,80,576]{2,1,0:T(8,128)(2,1)S(1)}, u32[]{:S(2)}, u32[]{:S(2)}) %all-to-all-start.1) | async-done | bytes 1474592 | tf_op jit(solution)/shard_map/all_to_all | solution.py:404
  118.1 2.9 %shard_map.120 = bf16[512,512]{1,0:T(8,128)(2,1)} custom-call(bf16[16,80,576]{2,1,0:T(8,128)(2,1)S(1)} %all-to-all-done.1.arrived_ref, bf16[16,576]{1,0:T(8,128)(2,1)S(1)} %pad.5.fresh_ref, s32[1,384]{1,0:T(1,128)S(1)} %reshape.443.live_ref), custom_call_target="tpu_custom_call" | custom-call | tf_op jit(solution)/shard_map/pallas_call | solution.py:312
  120.9 3.6 %all-to-all-start.2 = ((bf16[16,32,512]{2,1,0:T(8,128)(2,1)}), bf16[16,32,512]{2,1,0:T(8,128)(2,1)S(1)}, u32[]{:S(2)}, u32[]{:S(2)}) async-start(bf16[16,32,512]{2,1,0:T(8,128)(2,1)} %bitcast.22), calls=%async_computation.2 | async-start | bytes 1048576 | tf_op jit(solution)/shard_map/all_to_all | solution.py:429
  125.1 1.4 %fusion.1 = bf16[1,384,576]{1,2,0:T(8,128)(2,1)} fusion(bf16[768,576]{1,0:T(8,128)(2,1)S(1)} %bitcast.60, s32[768]{0:T(1024)S(1)} %eq.106), kind=kOutput, calls=%fused_computation.3 | convolution fusion | flops 340254720 | bytes 1330176 | tf_op jit(solution)/shard_map/dot_general | solution.py:419
  126.5 8.1 %all-to-all-done.2 = bf16[16,32,512]{2,1,0:T(8,128)(2,1)S(1)} async-done(((bf16[16,32,512]{2,1,0:T(8,128)(2,1)}), bf16[16,32,512]{2,1,0:T(8,128)(2,1)S(1)}, u32[]{:S(2)}, u32[]{:S(2)}) %all-to-all-start.2) | async-done | bytes 524320 | tf_op jit(solution)/shard_map/all_to_all | solution.py:429
  134.6 0.7 fusion.2
  135.4 0.8 copy.68
  (97 shorter events, 7.8 us)
Async XLA Ops:
  0.6 79.1 %copy-start = (bf16[8,128,512]{2,1,0:T(8,128)(2,1)S(1)}, bf16[8,128,512]{2,1,0:T(8,128)(2,1)}, u32[]{:S(2)}) copy-start(bf16[8,128,512]{2,1,0:T(8,128)(2,1)} %param.13) | copy-start | bytes 3145732
  0.6 14.7 %copy-start.6 = (s32[8,16]{1,0:T(8,128)S(1)}, s32[8,16]{1,0:T(8,128)}, u32[]{:S(2)}) copy-start(s32[8,16]{1,0:T(8,128)} %len_ref.1) | copy-start | bytes 1540
  12.1 17.8 %collective-permute-start = (bf16[2,2,576,256]{3,2,1,0:T(8,128)(2,1)}, bf16[2,2,576,256]{3,2,1,0:T(8,128)(2,1)}, u32[]{:S(2)}, u32[]{:S(2)}) collective-permute-start(bf16[2,2,576,256]{3,2,1,0:T(8,128)(2,1)} %get-tuple-element.17), channel_id=1, source_target_pairs={{0,32},{1,9},{2,34},{3,11},{4,36},{5,13},{6,38},{7,15},{8,40},{9,1... | collective-permute-start | bytes 3538952 | tf_op jit(solution)/shard_map/ppermute | solution.py:354
  13.8 16.5 %collective-permute-start.1 = (bf16[2,2,576,256]{3,2,1,0:T(8,128)(2,1)}, bf16[2,2,576,256]{3,2,1,0:T(8,128)(2,1)}, u32[]{:S(2)}, u32[]{:S(2)}) collective-permute-start(bf16[2,2,576,256]{3,2,1,0:T(8,128)(2,1)} %get-tuple-element.18), channel_id=1, source_target_pairs={{0,96},{1,25},{2,98},{3,27},{4,100},{5,29},{6,102},{7,31},{8,104},... | collective-permute-start | bytes 3538952 | tf_op jit(solution)/shard_map/ppermute | solution.py:355
  15.6 1.7 %copy-start.3 = (f32[2,2,576,256]{3,2,1,0:T(8,128)S(1)}, f32[2,2,576,256]{3,2,1,0:T(8,128)}, u32[]{:S(2)}) copy-start(f32[2,2,576,256]{3,2,1,0:T(8,128)} %get-tuple-element.16.share_ref) | copy-start | bytes 7077892
  17.2 0.7 copy-start.8
  18.0 18.6 %copy-start.7 = (f32[512]{0:T(512)S(1)}, f32[512]{0:T(512)}, u32[]{:S(2)}) copy-start(f32[512]{0:T(512)} %param.12) | copy-start | bytes 6148
  33.1 11.3 %collective-permute-start.2 = (bf16[2,576,256]{2,1,0:T(8,128)(2,1)}, bf16[2,576,256]{2,1,0:T(8,128)(2,1)S(1)}, u32[]{:S(2)}, u32[]{:S(2)}) collective-permute-start(bf16[2,576,256]{2,1,0:T(8,128)(2,1)} %get-tuple-element.22), channel_id=1, source_target_pairs={{0,32},{1,9},{2,34},{3,11},{4,36},{5,13},{6,38},{7,15},{8,40},{9,1... | collective-permute-start | bytes 1769480 | tf_op jit(solution)/shard_map/ppermute | solution.py:358
  34.7 10.1 %collective-permute-start.3 = (bf16[2,576,256]{2,1,0:T(8,128)(2,1)}, bf16[2,576,256]{2,1,0:T(8,128)(2,1)S(1)}, u32[]{:S(2)}, u32[]{:S(2)}) collective-permute-start(bf16[2,576,256]{2,1,0:T(8,128)(2,1)} %get-tuple-element.23), channel_id=1, source_target_pairs={{0,96},{1,25},{2,98},{3,27},{4,100},{5,29},{6,102},{7,31},{8,104},... | collective-permute-start | bytes 1769480 | tf_op jit(solution)/shard_map/ppermute | solution.py:359
  36.9 1.7 %copy-start.2 = (f32[4,576,256]{2,1,0:T(8,128)S(1)}, f32[4,576,256]{2,1,0:T(8,128)}, u32[]{:S(2)}) copy-start(f32[4,576,256]{2,1,0:T(8,128)} %get-tuple-element.21.share_ref) | copy-start | bytes 7077892
  46.8 8.8 %collective-permute-start.4 = (bf16[576,256]{1,0:T(8,128)(2,1)S(1)}, bf16[576,256]{1,0:T(8,128)(2,1)S(1)}, u32[]{:S(2)}, u32[]{:S(2)}) collective-permute-start(bf16[576,256]{1,0:T(8,128)(2,1)S(1)} %get-tuple-element.25), channel_id=1, source_target_pairs={{0,8},{1,33},{2,10},{3,35},{4,12},{5,37},{6,14},{7,39},{8,16},{9,4... | collective-permute-start | bytes 884744 | tf_op jit(solution)/shard_map/ppermute | solution.py:361
  48.8 11.4 %collective-permute-start.5 = (bf16[576,256]{1,0:T(8,128)(2,1)S(1)}, bf16[576,256]{1,0:T(8,128)(2,1)S(1)}, u32[]{:S(2)}, u32[]{:S(2)}) collective-permute-start(bf16[576,256]{1,0:T(8,128)(2,1)S(1)} %get-tuple-element.26), channel_id=1, source_target_pairs={{0,16},{1,65},{2,18},{3,67},{4,20},{5,69},{6,22},{7,71},{8,24},{9,... | collective-permute-start | bytes 884744 | tf_op jit(solution)/shard_map/ppermute | solution.py:361
  52.4 7.9 %collective-permute-start.6 = (bf16[576,256]{1,0:T(8,128)(2,1)S(1)}, bf16[576,256]{1,0:T(8,128)(2,1)S(1)}, u32[]{:S(2)}, u32[]{:S(2)}) collective-permute-start(bf16[576,256]{1,0:T(8,128)(2,1)S(1)} %get-tuple-element.27), channel_id=1, source_target_pairs={{0,24},{1,97},{2,26},{3,99},{4,28},{5,101},{6,30},{7,103},{8,0},{9... | collective-permute-start | bytes 884744 | tf_op jit(solution)/shard_map/ppermute | solution.py:361
  61.6 5.3 %copy-start.9 = (s32[1,96]{1,0:T(1,128)S(1)}, s32[1,96]{1,0:T(1,128)}, u32[]{:S(2)}) copy-start(s32[1,96]{1,0:T(1,128)} %param.19) | copy-start | bytes 1156
  61.6 17.9 %copy-start.5 = (bf16[1,16,4,8,192]{4,3,2,1,0:T(8,128)(2,1)S(1)}, bf16[1,16,4,8,192]{4,3,2,1,0:T(8,128)(2,1)}, u32[]{:S(2)}) copy-start(bf16[1,16,4,8,192]{4,3,2,1,0:T(8,128)(2,1)} %param.15) | copy-start | bytes 589828
  61.6 17.5 %all-to-all-start = ((bf16[4,576,256]{2,1,0:T(8,128)(2,1)}), bf16[4,576,256]{2,1,0:T(8,128)(2,1)S(1)}, u32[]{:S(2)}, u32[]{:S(2)}) async-start(bf16[4,576,256]{2,1,0:T(8,128)(2,1)} %shard_map.118), calls=%async_computation | async-start | bytes 2359296 | tf_op jit(solution)/shard_map/all_to_all | solution.py:382
  79.1 3.0 %collective-permute-start.7 = (bf16[4,576,256]{2,1,0:T(8,128)(2,1)S(1)}, bf16[4,576,256]{2,1,0:T(8,128)(2,1)}, u32[]{:S(2)}, u32[]{:S(2)}) collective-permute-start(bf16[4,576,256]{2,1,0:T(8,128)(2,1)S(1)} %all-to-all-done.near_ref), channel_id=1, source_target_pairs={{0,1},{1,0},{2,3},{3,2},{4,5},{5,4},{6,7},{7,6},{8,9},{9,8},{10,11... | collective-permute-start | bytes 3538952 | tf_op jit(solution)/shard_map/ppermute | solution.py:383
  85.4 1.2 copy-start.1
  86.6 31.5 %all-to-all-start.1 = ((bf16[16,80,576]{2,1,0:T(8,128)(2,1)}), bf16[16,80,576]{2,1,0:T(8,128)(2,1)S(1)}, u32[]{:S(2)}, u32[]{:S(2)}) async-start(bf16[16,80,576]{2,1,0:T(8,128)(2,1)} %copy-done.1), calls=%async_computation.1 | async-start | bytes 3276800 | tf_op jit(solution)/shard_map/all_to_all | solution.py:404
  120.9 13.7 %all-to-all-start.2 = ((bf16[16,32,512]{2,1,0:T(8,128)(2,1)}), bf16[16,32,512]{2,1,0:T(8,128)(2,1)S(1)}, u32[]{:S(2)}, u32[]{:S(2)}) async-start(bf16[16,32,512]{2,1,0:T(8,128)(2,1)} %bitcast.22), calls=%async_computation.2 | async-start | bytes 1048576 | tf_op jit(solution)/shard_map/all_to_all | solution.py:429
  125.1 9.6 %copy-start.4 = (bf16[8,512,128]{2,1,0:T(8,128)(2,1)S(1)}, bf16[8,512,128]{2,1,0:T(8,128)(2,1)}, u32[]{:S(2)}) copy-start(bf16[8,512,128]{2,1,0:T(8,128)(2,1)} %param.14) | copy-start | bytes 3145732
